TPU v7x, 32 devices: a whole 2x2x4 slice. The times are simulated.
32 devices in a mesh: mem: 16 (over z, x, core), lat: 2 (over y).
Axes of the slice: x: 2, y: 2, z: 4, core: 2. Of those that a mesh axis runs over, the one named last changes fastest.
Arguments:
- perturb: bfloat16 [3, 3, 48, 32, 8, 256], P(None, None, 'mem', None, 'lat'), may hold values from -0.875 to 0.875
- alpha_init: float32 [48, 32, 8, 256], P('mem', None, 'lat'), may hold values from -6 to 6
- innovation: float32 [288, 8, 256], P('mem', 'lat'), may hold values from -6 to 6
- obs_weight: float32 [288, 8, 256], P('mem', 'lat'), may hold values from 0.5 to 2
- coef: float32 [2, 8, 256], P(None, 'lat'), may hold values from 0.12 to 0.24
- obs_mask: int32 [3, 2, 64], P(None, 'lat'), may hold values 0 or 1
Outputs:
- alpha_out: float32 [48, 32, 8, 256], P('mem', None, 'lat')
- misfit: float32 [288, 8, 256], P('mem', 'lat')
All inputs are finite; a program needn't handle non-finite values. No bound on the sum of `obs_mask` on one device may be relied on, other than what follows from the above.
Results may differ from a plain program's by a relative error of at most 0.0003.
Values sent between devices are 32-bit elements; how exact they have to be, the bound alone decides.
No kernel may reach another device: no remote copies, remote signals or barrier semaphores. Data moves between devices by JAX's collectives and lax.ppermute only.
A program may use at most 64 MiB of HBM per device.

v0:
```python
import functools
import math

import jax
import jax.numpy as jnp
from jax import lax
from jax.experimental import pallas as pl
from jax.experimental.pallas import tpu as pltpu
from jax.sharding import PartitionSpec as P

ITERS = 2
DIFF_STEPS = 4
TILE = 4


def with_halo(cells, sides, width):
    for axis, dim in sides:
        count = lax.axis_size(axis)
        ends = count - 1
        head = lax.slice_in_dim(cells, 0, width, axis=dim)
        tail = lax.slice_in_dim(cells, cells.shape[dim] - width, cells.shape[dim], axis=dim)
        cells = jnp.concatenate(
            [
                lax.ppermute(tail, axis, [(i, (i + 1) % count) for i in range(ends)]),
                cells,
                lax.ppermute(head, axis, [((i + 1) % count, i) for i in range(ends)]),
            ],
            axis=dim,
        )
    return cells


def face_weights(coef):
    klat = coef[0]
    klon = coef[1]
    zero_row = jnp.zeros_like(klat[:1])
    north_face = 0.5 * (klat + jnp.concatenate([zero_row, klat[:-1]], axis=0))
    south_face = 0.5 * (klat + jnp.concatenate([klat[1:], zero_row], axis=0))
    east_face = 0.5 * (klon + jnp.roll(klon, -1, axis=1))
    west_face = 0.5 * (klon + jnp.roll(klon, 1, axis=1))
    return (north_face, south_face, east_face, west_face)


def diffuse_once(layer_field, face_list, valid_rows):
    north_face, south_face, east_face, west_face = face_list
    zero_row = jnp.zeros_like(layer_field[..., :1, :])
    above = jnp.concatenate([zero_row, layer_field[..., :-1, :]], axis=-2)
    below = jnp.concatenate([layer_field[..., 1:, :], zero_row], axis=-2)
    east_val = jnp.roll(layer_field, -1, axis=-1)
    west_val = jnp.roll(layer_field, 1, axis=-1)
    updated = layer_field + north_face * (above - layer_field) + south_face * (below - layer_field)
    updated = updated + east_face * (east_val - layer_field) + west_face * (west_val - layer_field)
    return updated * valid_rows


def rim_rows(all_faces):
    return tuple((face for face in all_faces))


def valid_mask(margin, band_rows):
    global_row = (
        lax.axis_index("lat") * band_rows
        + jnp.arange(band_rows + 2 * margin, dtype=jnp.int32)
        - margin
    )
    total_rows = band_rows * lax.axis_size("lat")
    inside = jnp.logical_and(global_row >= 0, global_row < total_rows)
    return inside.astype(jnp.float32)[:, None]


def diffuse_field(layer_field, all_faces, band_rows):
    face_list = rim_rows(all_faces)
    valid_rows = valid_mask(DIFF_STEPS, band_rows)
    extended = with_halo(layer_field, (("lat", 2),), DIFF_STEPS)
    for sweep in range(DIFF_STEPS):
        extended = diffuse_once(extended, face_list, valid_rows)
    return extended[..., DIFF_STEPS : DIFF_STEPS + band_rows, :]


def shards(perturb, alpha_init, innovation, obs_weight, coef, obs_mask):
    slot_count, var_count, members, levels, band_rows, lon_cells = perturb.shape
    owned_rows = innovation.shape[0]
    coef_ext = with_halo(coef, (("lat", 1),), DIFF_STEPS)
    all_faces = face_weights(coef_ext)
    tile_mask = jnp.repeat(jnp.repeat(obs_mask, TILE, axis=1), TILE, axis=2).astype(jnp.float32)
    first_row = lax.axis_index("mem") * owned_rows
    slot_of_row = (first_row + jnp.arange(owned_rows, dtype=jnp.int32)) // (var_count * levels)
    one_hot = (slot_of_row[:, None] == jnp.arange(slot_count, dtype=jnp.int32)[None, :]).astype(
        jnp.float32
    )
    row_mask = jnp.sum(one_hot[:, :, None, None] * tile_mask[None], axis=1)
    row_gain = obs_weight * row_mask
    alpha = alpha_init
    misfit = jnp.zeros_like(innovation)
    for sweep in range(ITERS):
        spread = diffuse_field(alpha, all_faces, band_rows)
        partial_sum = jnp.sum(perturb.astype(jnp.float32) * spread[None, None], axis=2)
        partial_sum = partial_sum.reshape(slot_count * var_count * levels, band_rows, lon_cells)
        increment = lax.psum_scatter(partial_sum, "mem", scatter_dimension=0, tiled=True)
        misfit = row_gain * (increment - innovation)
        gathered = lax.all_gather(misfit, "mem", axis=0, tiled=True)
        misfit_rows = gathered.reshape(slot_count, var_count, levels, band_rows, lon_cells)
        adjoint = jnp.sum(perturb.astype(jnp.float32) * misfit_rows[:, :, None], axis=(0, 1))
        alpha = alpha - 0.3 * (alpha + diffuse_field(adjoint, all_faces, band_rows))
    return (alpha, misfit)


LANES = 128
SUBLANES = 8
CHIPS = 8
CORES = 2
GROUP = CHIPS * CORES
EARLY = (1, 6, 2, 5)
LATE = (4, 3, 7)


def fold(cells):
    lead, (rows, cols) = cells.shape[:-2], cells.shape[-2:]
    parts = cells.reshape(*lead, rows, cols // LANES, LANES).swapaxes(-3, -2)
    return parts.reshape(*lead, rows * cols // LANES, LANES)


def fits(mesh, perturb, innovation):
    slot_count, var_count, members, levels, rows, lon_cells = perturb.shape
    mem, lat = mesh.shape["mem"], mesh.shape["lat"]
    if lat != 2 or mem != 2 * GROUP // lat:
        return False
    if rows != lat * TILE or DIFF_STEPS > TILE or TILE * lon_cells != SUBLANES * LANES:
        return False
    total = slot_count * var_count * levels
    if members % mem or levels % GROUP or total % mem or total // mem > levels:
        return False
    return held_fields(slot_count * var_count, levels) is not None


def held_fields(fields, levels):
    chunks = []
    for chunk in range(levels // GROUP):
        halves = ([], [])
        for field in range(fields):
            rows = [field * levels + chunk * GROUP + place for place in range(GROUP)]
            sides = {2 * row // (fields * levels) for row in rows}
            if len(sides) != 1:
                return None
            halves[sides.pop()].append(field)
        if not halves[0] or not halves[1]:
            return None
        longest = max(len(half) for half in halves)
        chunks.append([half + half[-1:] * (longest - len(half)) for half in halves])
    return chunks


def flat_offset(chip, core):
    return ((chip >> 1) << 2) | (core << 1) | (chip & 1)


def shift_by(mask, cells):
    axes = ("mem", "lat")
    count = lax.axis_size("mem") * lax.axis_size("lat")
    return lax.ppermute(cells, axes, [(i, i ^ mask) for i in range(count)])


class Sizes:
    def __init__(self, perturb, owned_rows):
        slots, variables, members, levels = perturb.shape[:4]
        self.slots = slots
        self.vars = variables
        self.fields = slots * variables
        self.members = members
        self.levels = levels
        self.owned = owned_rows
        self.chunks = levels // GROUP
        self.planes = self.fields * members
        self.rows = self.planes + members + 2
        self.all_rows = self.chunks * self.rows
        self.held = held_fields(self.fields, levels)
        self.sums = self.fields * 2


def row_in_block(size, level, mem_index):
    row = lax.rem(level + size.levels * size.owned - lax.rem(size.owned * mem_index, size.levels), size.levels)
    return row, row < size.owned, lax.div(size.owned * mem_index + row, size.levels)


def pack_target(size, outs, chip, core):
    if chip == 0:
        return outs[core]
    if chip in EARLY:
        return outs[2 + EARLY.index(chip)].at[core]
    place = LATE.index(chip)
    return outs[2 + len(EARLY) + place] if core == 0 else outs[-1].at[place]


def pack_kernel(size, flat_ref, perturb_hbm, alpha_hbm, innov_hbm, weight_hbm, mask_ref, near_ref, *refs):
    outs, scratch = refs[:-7], refs[-7:]
    perturb_ref, alpha_ref, innov_ref, weight_ref, tiles_ref, plane_sems, sems = scratch
    flat = flat_ref[0]
    own = lax.rem(flat, GROUP)
    mem_index = lax.div(flat, 2)
    step = size.fields
    plane_copies = [
        pltpu.make_async_copy(
            perturb_hbm.at[pl.ds(part * step, step)], perturb_ref.at[pl.ds(part * step, step)], plane_sems.at[part]
        )
        for part in range(size.members)
    ]
    copies = [
        pltpu.make_async_copy(source, target, sems.at[place])
        for place, (source, target) in enumerate(
            ((alpha_hbm, alpha_ref), (innov_hbm, innov_ref), (weight_hbm, weight_ref))
        )
    ]
    for copy in plane_copies + copies:
        copy.start()
    tiles = mask_ref.shape[-1]
    shape = (tiles, tiles * TILE)
    spread_out = lax.broadcasted_iota(jnp.int32, shape, 0) == lax.div(lax.broadcasted_iota(jnp.int32, shape, 1), TILE)
    line = lax.broadcasted_iota(jnp.int32, (SUBLANES, LANES), 0)
    for slot in range(size.slots):
        cells = jnp.dot(
            mask_ref[slot].astype(jnp.float32), spread_out.astype(jnp.float32), preferred_element_type=jnp.float32
        )
        tiles_ref[slot] = jnp.where(line < TILE, cells[:, :LANES], cells[:, LANES:])
    coef_out = outs[2 + EARLY.index(1)]
    coef_out[0, size.all_rows] = near_ref[0]
    coef_out[1, size.all_rows] = near_ref[1]
    places = [(chip, core, chunk) for chip in range(CHIPS) for core in range(CORES) for chunk in range(size.chunks)]

    def level_of(chip, core, chunk):
        return lax.bitwise_xor(own, flat_offset(chip, core)) + chunk * GROUP

    for part in range(size.members):
        plane_copies[part].wait()
        for chip, core, chunk in places:
            planes = perturb_ref[part * step : (part + 1) * step, level_of(chip, core, chunk)]
            base = chunk * size.rows + part * step
            pack_target(size, outs, chip, core)[base : base + step] = planes.astype(jnp.float32)
    for copy in copies:
        copy.wait()
    for chip, core, chunk in places:
        out = pack_target(size, outs, chip, core)
        level = level_of(chip, core, chunk)
        base = chunk * size.rows + size.planes
        out[base : base + size.members] = alpha_ref[:, level]
        row, inside, field = row_in_block(size, level, mem_index)
        row = jnp.minimum(row, size.owned - 1)
        slot = jnp.minimum(lax.div(field, size.vars), size.slots - 1)
        kept = jnp.where(inside, 1.0, 0.0).astype(jnp.float32)
        out[base + size.members] = innov_ref[row] * kept
        out[base + size.members + 1] = weight_ref[row] * tiles_ref[slot] * kept


class Pieces:
    def __init__(self, size, refs):
        self.size = size
        self.refs = refs
        self.far_ref = refs[2 + EARLY.index(1)]

    def at(self, chip, core):
        if chip == 0:
            return self.refs[core], ()
        if chip in EARLY:
            place = EARLY.index(chip)
            return (self.refs[2 + place], (0,)) if core == 0 else (self.refs[2 + len(EARLY)], (place,))
        return self.refs[3 + len(EARLY) + LATE.index(chip)], (core,)

    def block(self, chip, core, chunk, row):
        ref, lead = self.at(chip, core)
        return ref[lead + (chunk * self.size.rows + row,)]

    def alpha(self, chip, core, chunk):
        ref, lead = self.at(chip, core)
        base = chunk * self.size.rows + self.size.planes
        return ref[lead + (slice(base, base + self.size.members),)]

    def far(self):
        return [self.far_ref[part, self.size.all_rows] for part in range(2)]


def roll(cells, shift, axis):
    return pltpu.roll(cells, shift, axis=cells.ndim + axis)


def neighbours(own, other, edges):
    row0, row3, lane0, lane_last = edges
    turned = roll(own, SUBLANES // 2, -2)
    across = roll(other, SUBLANES // 2, -2)
    above = roll(jnp.where(row3, across, own), 1, -2)
    below = roll(jnp.where(row0, across, own), SUBLANES - 1, -2)
    east = roll(jnp.where(lane0, turned, own), LANES - 1, -1)
    west = roll(jnp.where(lane_last, turned, own), 1, -1)
    return above, below, east, west


def stencils(flat, near, far):
    shape = (SUBLANES, LANES)
    line = lax.rem(lax.broadcasted_iota(jnp.int32, shape, 0), TILE)
    lane = lax.broadcasted_iota(jnp.int32, shape, 1)
    edges = (line == 0, line == TILE - 1, lane == 0, lane == LANES - 1)
    band = lax.rem(flat, 2)
    weights = []
    for half, (own, other) in enumerate(((near, far), (far, near))):
        here = lax.bitwise_xor(band, half)
        open_top = jnp.where(jnp.logical_and(edges[0], here == 0), 0.0, 1.0).astype(jnp.float32)
        open_end = jnp.where(jnp.logical_and(edges[1], here == 1), 0.0, 1.0).astype(jnp.float32)
        above, below, _, _ = neighbours(own[0], other[0], edges)
        _, _, east, west = neighbours(own[1], other[1], edges)
        north = 0.5 * (own[0] + above * open_top)
        south = 0.5 * (own[0] + below * open_end)
        east = 0.5 * (own[1] + east)
        west = 0.5 * (own[1] + west)
        centre = 1.0 - north - south - east - west
        weights.append((centre, north * open_top, south * open_end, east, west))
    return edges, weights


def diffuse_pair(near, far, stencil):
    edges, weights = stencil
    for _ in range(DIFF_STEPS):
        pair = []
        for (own, other), (centre, north, south, east, west) in zip(((near, far), (far, near)), weights):
            above, below, right, left = neighbours(own, other, edges)
            pair.append(centre * own + north * above + south * below + east * right + west * left)
        near, far = pair
    return near, far


def add_products(size, pieces, chunk, pair, spread, sums):
    for half in range(2):
        for core in range(CORES):
            for field in range(size.fields):
                for member in range(size.members):
                    plane = pieces.block(2 * pair + half, core, chunk, field * size.members + member)
                    term = plane * spread[half][core * size.members + member]
                    known = sums[half][field]
                    sums[half][field] = term if known is None else known + term


def adjoint_of(size, pieces, chunk, pair, misfit):
    halves = []
    for half in range(2):
        found = []
        for core in range(CORES):
            for member in range(size.members):
                total = None
                for field in range(size.fields):
                    plane = pieces.block(2 * pair + half, core, chunk, field * size.members + member)
                    term = plane * misfit[half][field]
                    total = term if total is None else total + term
                found.append(total)
        halves.append(jnp.stack(found))
    return halves


def first_alpha(pieces, chunk, pair):
    return [
        jnp.concatenate([pieces.alpha(2 * pair + half, core, chunk) for core in range(CORES)]) for half in range(2)
    ]


def first_kernel(chunk, size, flat_ref, near_ref, *refs):
    pieces, (sum_ref, gain_ref, innov_ref) = Pieces(size, refs[:-3]), refs[-3:]
    flat = flat_ref[0]
    stencil = stencils(flat, [near_ref[0], near_ref[1]], pieces.far())
    mem_index = lax.div(flat, 2)
    side = lax.div(flat, GROUP)
    gain_ref[...] = jnp.zeros_like(gain_ref)
    innov_ref[...] = jnp.zeros_like(innov_ref)
    level = lax.rem(flat, GROUP) + chunk * GROUP
    for chip in range(0, CHIPS, 2):
        for core in range(CORES):
            source = lax.bitwise_xor(mem_index, (chip & 6) | core)
            _, inside, field = row_in_block(size, level, source)

            @pl.when(inside)
            def _(chip=chip, core=core, field=field):
                for half in range(2):
                    innov_ref[field, half] = pieces.block(chip + half, core, chunk, size.rows - 2)
                    gain_ref[field, half] = pieces.block(chip + half, core, chunk, size.rows - 1)

    for place, (first, second) in enumerate(zip(*size.held[chunk])):
        field = jnp.where(side == 0, first, second)
        sum_ref[pl.ds(size.sums + 2 * place, 2)] = gain_ref[field]
    sums = [[None] * size.fields for _ in range(2)]
    for pair in range(CHIPS // 2):
        spread = diffuse_pair(*first_alpha(pieces, chunk, pair), stencil)
        add_products(size, pieces, chunk, pair, spread, sums)
    for field in range(size.fields):
        for half in range(2):
            sum_ref[field * 2 + half] = sums[half][field] - innov_ref[field, half]


def misfit_of(size, gain_ref, mine_ref, theirs_ref):
    return [
        [
            gain_ref[field, half] * (mine_ref[field * 2 + half] + theirs_ref[field * 2 + half])
            for field in range(size.fields)
        ]
        for half in range(2)
    ]


def middle_kernel(chunk, size, flat_ref, near_ref, mine_ref, theirs_ref, held_ref, innov_ref, *refs):
    pieces, (sum_ref, gain_ref, alpha_ref) = Pieces(size, refs[:-3]), refs[-3:]
    flat = flat_ref[0]
    side = lax.div(flat, GROUP)
    stencil = stencils(flat, [near_ref[0], near_ref[1]], pieces.far())
    gain_ref[...] = held_ref[...]
    for place, (first, second) in enumerate(zip(*size.held[chunk])):
        field = jnp.where(side == 0, second, first)
        gain_ref[field] = theirs_ref[pl.ds(size.sums + 2 * place, 2)]
    misfit = misfit_of(size, gain_ref, mine_ref, theirs_ref)
    sums = [[None] * size.fields for _ in range(2)]
    for pair in range(CHIPS // 2):
        change = diffuse_pair(*adjoint_of(size, pieces, chunk, pair, misfit), stencil)
        before = first_alpha(pieces, chunk, pair)
        alpha = [old - 0.3 * (old + new) for old, new in zip(before, change)]
        for half in range(2):
            alpha_ref[pair, half] = alpha[half]
        add_products(size, pieces, chunk, pair, diffuse_pair(*alpha, stencil), sums)
    for field in range(size.fields):
        for half in range(2):
            sum_ref[field * 2 + half] = sums[half][field] - innov_ref[field, half]


def last_kernel(chunk, size, flat_ref, near_ref, mine_ref, theirs_ref, gain_ref, alpha_ref, *refs):
    refs, (out_ref, misfit_ref) = refs[:-2], refs[-2:]
    flat = flat_ref[0]
    own = lax.rem(flat, GROUP)
    mem_index = lax.div(flat, 2)
    base = chunk * (size.members + 1)
    if chunk:
        out_ref[:, :base] = refs[0][...]
        refs = refs[1:]
    pieces = Pieces(size, refs)
    stencil = stencils(flat, [near_ref[0], near_ref[1]], pieces.far())
    misfit = misfit_of(size, gain_ref, mine_ref, theirs_ref)
    for half in range(2):
        for field in range(size.fields):
            misfit_ref[half, field] = misfit[half][field]
    level = own + chunk * GROUP
    for pair in range(CHIPS // 2):
        change = diffuse_pair(*adjoint_of(size, pieces, chunk, pair, misfit), stencil)
        for half in range(2):
            old = alpha_ref[pair, half]
            alpha = old - 0.3 * (old + change[half])
            chip = 2 * pair + half
            for core in range(CORES):
                target = lax.bitwise_xor(own, flat_offset(chip, core))
                out_ref[target, base : base + size.members] = alpha[core * size.members : (core + 1) * size.members]
                _, _, field = row_in_block(size, level, lax.bitwise_xor(mem_index, (chip & 6) | core))
                out_ref[target, base + size.members] = misfit_ref[half, jnp.minimum(field, size.fields - 1)]


def unfold_into(out, at, block):
    rows = block.shape[-2] // 2
    out[at + (slice(None), slice(0, LANES))] = block[..., :rows, :]
    out[at + (slice(None), slice(LANES, 2 * LANES))] = block[..., rows:, :]


def place_kernel(size, flat_ref, back_ref, alpha_ref, misfit_ref):
    mem_index = lax.div(flat_ref[0], 2)
    for source in range(GROUP):
        for chunk in range(size.chunks):
            base = chunk * (size.members + 1)
            level = source + chunk * GROUP
            for member in range(size.members):
                unfold_into(alpha_ref, (member, level), back_ref[source, base + member])
            row, inside, _ = row_in_block(size, level, mem_index)

            @pl.when(inside)
            def _(source=source, base=base, row=row):
                unfold_into(misfit_ref, (row,), back_ref[source, base + size.members])


def call(kernel, outs, operands, scratch=(), spaces=None, limit=24):
    spaces = spaces or [pltpu.VMEM] * len(operands)
    moved = 4 * sum(math.prod(shape) for shape in outs) + sum(x.size * x.dtype.itemsize for x in operands)
    return pl.pallas_call(
        kernel,
        out_shape=[jax.ShapeDtypeStruct(shape, jnp.float32) for shape in outs],
        in_specs=[pl.BlockSpec(memory_space=space) for space in [pltpu.SMEM] + spaces[1:]],
        out_specs=[pl.BlockSpec(memory_space=pltpu.VMEM)] * len(outs),
        scratch_shapes=scratch,
        cost_estimate=pl.CostEstimate(flops=moved, bytes_accessed=moved, transcendentals=0),
        compiler_params=pltpu.CompilerParams(vmem_limit_bytes=limit * 1024 * 1024),
    )(*operands)


def spread_levels(size, flat, near, perturb, alpha_init, innovation, obs_weight, obs_mask):
    levels = size.levels
    block = (SUBLANES, LANES)
    one = (size.all_rows, *block)
    early_shapes = [(CORES, size.all_rows + (chip == 1), *block) for chip in EARLY]
    packed = call(
        functools.partial(pack_kernel, size),
        [one, one] + early_shapes + [one] * len(LATE) + [(len(LATE), *one)],
        (
            flat,
            fold(perturb).reshape(size.planes, levels, *block),
            fold(alpha_init),
            fold(innovation),
            fold(obs_weight),
            obs_mask,
            near,
        ),
        [
            pltpu.VMEM((size.planes, levels, *block), jnp.bfloat16),
            pltpu.VMEM((size.members, levels, *block), jnp.float32),
            pltpu.VMEM((size.owned, *block), jnp.float32),
            pltpu.VMEM((size.owned, *block), jnp.float32),
            pltpu.VMEM((size.slots, *block), jnp.float32),
            pltpu.SemaphoreType.DMA((size.members,)),
            pltpu.SemaphoreType.DMA((3,)),
        ],
        [pltpu.SMEM] + [pltpu.HBM] * 4 + [pltpu.VMEM] * 2,
    )
    kept, early, late, late_out = packed[:2], packed[2:6], packed[6:9], packed[9]
    crossed = shift_by(CORES, late_out)
    late = [jnp.stack([cells, crossed[place]]) for place, cells in enumerate(late)]
    own_crossed = shift_by(CORES, kept[1])
    got = [shift_by(flat_offset(chip, 0), cells) for chip, cells in zip(EARLY, early)]
    got[0], got[1], late[0], late[1] = lax.optimization_barrier((got[0], got[1], late[0], late[1]))
    got_late = [shift_by(flat_offset(chip, 0), cells) for chip, cells in zip(LATE[:2], late[:2])]
    got[2], got[3], late[2] = lax.optimization_barrier((got[2], got[3], late[2]))
    got_late.append(shift_by(flat_offset(LATE[2], 0), late[2]))
    early_crossed = shift_by(CORES, jnp.stack([cells[1, : size.all_rows] for cells in got]))
    return (kept[0], own_crossed, *got, early_crossed, *got_late)


def level_shards(perturb, alpha_init, innovation, obs_weight, coef, obs_mask):
    size = Sizes(perturb, innovation.shape[0])
    levels, rows, lon_cells = perturb.shape[3:]
    block = (SUBLANES, LANES)
    flat = (lax.axis_index("mem") * lax.axis_size("lat") + lax.axis_index("lat")).astype(jnp.int32).reshape(1)
    near = fold(coef)
    pieces = spread_levels(size, flat, near, perturb, alpha_init, innovation, obs_weight, obs_mask)
    common = (flat, near)
    per_field = (size.fields, 2, *block)
    alpha_shape = (CHIPS // 2, 2, CORES * size.members, *block)
    chunks = range(size.chunks)
    first, second, back = [], [], None
    for chunk in chunks:
        sent = size.sums + 2 * len(size.held[chunk][0])
        mine, held, innov = call(
            functools.partial(first_kernel, chunk, size),
            [(sent, *block), per_field, per_field],
            common + pieces,
        )
        first.append((mine, shift_by(GROUP, mine), held, innov))
    for chunk in chunks:
        mine, gain, alpha = call(
            functools.partial(middle_kernel, chunk, size),
            [(size.sums, *block), per_field, alpha_shape],
            common + first[chunk] + pieces,
        )
        second.append((mine, shift_by(GROUP, mine), gain, alpha))
    for chunk in chunks:
        (back,) = call(
            functools.partial(last_kernel, chunk, size),
            [(GROUP, (chunk + 1) * (size.members + 1), *block)],
            common + second[chunk] + (() if back is None else (back,)) + pieces,
            [pltpu.VMEM((2, size.fields, *block), jnp.float32)],
        )
    groups = [[half * GROUP + place for place in range(GROUP)] for half in range(2)]
    back = lax.all_to_all(back, ("mem", "lat"), 0, 0, axis_index_groups=groups, tiled=True)
    return tuple(
        call(
            functools.partial(place_kernel, size),
            [(size.members, levels, rows, lon_cells), (size.owned, rows, lon_cells)],
            (flat, back),
        )
    )


def solution(mesh):
    in_specs = (
        P(None, None, "mem", None, "lat", None),
        P("mem", None, "lat", None),
        P("mem", "lat", None),
        P("mem", "lat", None),
        P(None, "lat", None),
        P(None, "lat", None),
    )
    out_specs = (P("mem", None, "lat", None), P("mem", "lat", None))

    def run(*args):
        body = level_shards if fits(mesh, args[0], args[2]) else shards
        return jax.shard_map(body, mesh=mesh, in_specs=in_specs, out_specs=out_specs, check_vma=False)(*args)

    return run
```

profile of v0, /device:TPU:0, one launch (start us, length us, event | category | flops | bytes accessed | tf_op | source)
XLA Modules:
  0.0 103.4 jit_solution(1278833278229940697)
XLA Ops:
  0.6 0.0 copy-start
  0.6 1.5 %copy-done = bf16[3,3,3,32,4,256]{5,4,3,2,1,0:T(4,128)(2,1)S(1)} copy-done((bf16[3,3,3,32,4,256]{5,4,3,2,1,0:T(4,128)(2,1)S(1)}, bf16[3,3,3,32,4,256]{5,4,3,2,1,0:T(4,128)(2,1)}, u32[]{:S(2)}) %copy-start) | copy-done | bytes 1769496
  2.1 0.7 copy-done.1
  2.8 1.0 copy-done.3
  3.8 0.9 copy-done.4
  4.7 0.9 copy-done.5
  5.6 0.7 copy-done.6
  6.3 1.7 %shard_map.77 = (f32[64,8,128]{2,1,0:T(8,128)S(1)}, f32[64,8,128]{2,1,0:T(8,128)S(1)}, f32[2,65,8,128]{3,2,1,0:T(8,128)S(1)}, f32[2,64,8,128]{3,2,1,0:T(8,128)S(...) custom-call(s32[1]{0:T(128)} %bitcast.flat_ref, ...), custom_call_target="tpu_custom_call" | custom-call | flops 6521604 | bytes 6521604 | tf_op jit(solution)/shard_map/pallas_call | solution.py:479
  8.0 0.5 collective-permute-start.3
  8.5 2.6 %collective-permute-start.4 = (f32[2,64,8,128]{3,2,1,0:T(8,128)S(1)}, f32[2,64,8,128]{3,2,1,0:T(8,128)S(1)}, u32[]{:S(2)}, u32[]{:S(2)}) collective-permute-start(f32[2,64,8,128]{3,2,1,0:T(8,128)S(1)} %get-tuple-element.40), channel_id=1, source_target_pairs={{0,4},{1,5},{2,6},{3,7},{4,0},{5,1},{6,2},{7,3},{8,12},{9,13},{10,... | collective-permute-start | bytes 1572872 | tf_op jit(solution)/shard_map/ppermute | solution.py:160
  11.0 2.5 %collective-permute-start.5 = (f32[2,64,8,128]{3,2,1,0:T(8,128)S(1)}, f32[2,64,8,128]{3,2,1,0:T(8,128)S(1)}, u32[]{:S(2)}, u32[]{:S(2)}) collective-permute-start(f32[2,64,8,128]{3,2,1,0:T(8,128)S(1)} %get-tuple-element.41), channel_id=1, source_target_pairs={{0,9},{1,8},{2,11},{3,10},{4,13},{5,12},{6,15},{7,14},{8,1},{9,0},... | collective-permute-start | bytes 1572872 | tf_op jit(solution)/shard_map/ppermute | solution.py:160
  13.6 0.5 collective-permute-start.1
  14.1 0.0 collective-permute-start.2
  14.1 0.0 collective-permute-done.3
  14.1 0.1 fusion
  14.2 9.3 %collective-permute-done.4.refs_4_.refs_5_ = f32[2,64,8,128]{3,2,1,0:T(8,128)S(1)} collective-permute-done((f32[2,64,8,128]{3,2,1,0:T(8,128)S(1)}, f32[2,64,8,128]{3,2,1,0:T(8,128)S(1)}, u32[]{:S(2)}, u32[]{:S(2)}) %collective-permute-start.4) | collective-permute-done | bytes 524320 | tf_op jit(solution)/shard_map/ppermute | solution.py:160
  23.6 3.2 %collective-permute-done.5.refs_5_.refs_6_ = f32[2,64,8,128]{3,2,1,0:T(8,128)S(1)} collective-permute-done((f32[2,64,8,128]{3,2,1,0:T(8,128)S(1)}, f32[2,64,8,128]{3,2,1,0:T(8,128)S(1)}, u32[]{:S(2)}, u32[]{:S(2)}) %collective-permute-start.5) | collective-permute-done | bytes 524320 | tf_op jit(solution)/shard_map/ppermute | solution.py:160
  26.8 0.1 pad_maximum_fusion.1
  26.9 0.0 copy-start.2
  26.9 10.3 %collective-permute-done.2.refs_3_.refs_4_ = f32[2,64,8,128]{3,2,1,0:T(8,128)S(1)} collective-permute-done((f32[2,64,8,128]{3,2,1,0:T(8,128)S(1)}, f32[2,64,8,128]{3,2,1,0:T(8,128)S(1)}, u32[]{:S(2)}, u32[]{:S(2)}) %collective-permute-start.2) | collective-permute-done | bytes 524320 | tf_op jit(solution)/shard_map/ppermute | solution.py:160
  37.2 0.1 collective-permute-done.1.refs_2_.refs_3_
  37.4 0.1 pad_maximum_fusion
  37.5 0.1 collective-permute-start.6
  37.6 1.6 %collective-permute-start.7 = (f32[2,64,8,128]{3,2,1,0:T(8,128)S(1)}, f32[2,64,8,128]{3,2,1,0:T(8,128)S(1)}, u32[]{:S(2)}, u32[]{:S(2)}) collective-permute-start(f32[2,64,8,128]{3,2,1,0:T(8,128)S(1)} %get-tuple-element.45), channel_id=1, source_target_pairs={{0,8},{1,9},{2,10},{3,11},{4,12},{5,13},{6,14},{7,15},{8,0},{9,1},... | collective-permute-start | bytes 1572872 | tf_op jit(solution)/shard_map/ppermute | solution.py:160
  39.2 1.3 %collective-permute-start.8 = (f32[2,64,8,128]{3,2,1,0:T(8,128)S(1)}, f32[2,64,8,128]{3,2,1,0:T(8,128)S(1)}, u32[]{:S(2)}, u32[]{:S(2)}) collective-permute-start(f32[2,64,8,128]{3,2,1,0:T(8,128)S(1)} %get-tuple-element.46), channel_id=1, source_target_pairs={{0,5},{1,4},{2,7},{3,6},{4,1},{5,0},{6,3},{7,2},{8,13},{9,12},{10,... | collective-permute-start | bytes 1572872 | tf_op jit(solution)/shard_map/ppermute | solution.py:160
  40.5 1.5 %collective-permute-start.9 = (f32[2,64,8,128]{3,2,1,0:T(8,128)S(1)}, f32[2,64,8,128]{3,2,1,0:T(8,128)S(1)}, u32[]{:S(2)}, u32[]{:S(2)}) collective-permute-start(f32[2,64,8,128]{3,2,1,0:T(8,128)S(1)} %pad_maximum_fusion.3), channel_id=1, source_target_pairs={{0,13},{1,12},{2,15},{3,14},{4,9},{5,8},{6,11},{7,10},{8,5},{9,4},... | collective-permute-start | bytes 1572872 | tf_op jit(solution)/shard_map/ppermute | solution.py:160
  42.0 0.0 collective-permute-start
  42.0 1.5 %collective-permute-done.refs_1_.refs_2_ = f32[64,8,128]{2,1,0:T(8,128)S(1)} collective-permute-done((f32[64,8,128]{2,1,0:T(8,128)S(1)}, f32[64,8,128]{2,1,0:T(8,128)S(1)}, u32[]{:S(2)}, u32[]{:S(2)}) %collective-permute-start) | collective-permute-done | bytes 262176 | tf_op jit(solution)/shard_map/ppermute | solution.py:160
  43.6 8.8 %collective-permute-done.7.refs_7_.refs_8_ = f32[2,64,8,128]{3,2,1,0:T(8,128)S(1)} collective-permute-done((f32[2,64,8,128]{3,2,1,0:T(8,128)S(1)}, f32[2,64,8,128]{3,2,1,0:T(8,128)S(1)}, u32[]{:S(2)}, u32[]{:S(2)}) %collective-permute-start.7) | collective-permute-done | bytes 524320 | tf_op jit(solution)/shard_map/ppermute | solution.py:160
  52.4 13.0 %collective-permute-done.8.refs_8_.refs_9_ = f32[2,64,8,128]{3,2,1,0:T(8,128)S(1)} collective-permute-done((f32[2,64,8,128]{3,2,1,0:T(8,128)S(1)}, f32[2,64,8,128]{3,2,1,0:T(8,128)S(1)}, u32[]{:S(2)}, u32[]{:S(2)}) %collective-permute-start.8) | collective-permute-done | bytes 524320 | tf_op jit(solution)/shard_map/ppermute | solution.py:160
  65.3 0.0 collective-permute-done.9.refs_9_.refs_10_
  65.3 0.0 collective-permute-done.6.refs_6_.refs_7_
  65.3 0.9 shard_map.80
  66.2 2.6 %collective-permute-start.12 = (f32[28,8,128]{2,1,0:T(8,128)S(1)}, f32[28,8,128]{2,1,0:T(8,128)S(1)}, u32[]{:S(2)}, u32[]{:S(2)}) collective-permute-start(f32[28,8,128]{2,1,0:T(8,128)S(1)} %get-tuple-element.54.mine_ref), channel_id=1, source_target_pairs={{0,16},{1,17},{2,18},{3,19},{4,20},{5,21},{6,22},{7,23},{8,24},{9,... | collective-permute-start | bytes 344072 | tf_op jit(solution)/shard_map/ppermute | solution.py:160
  68.9 0.8 shard_map.78
  69.7 0.4 collective-permute-start.10
  70.1 6.6 %collective-permute-done.12.theirs_ref = f32[28,8,128]{2,1,0:T(8,128)S(1)} collective-permute-done((f32[28,8,128]{2,1,0:T(8,128)S(1)}, f32[28,8,128]{2,1,0:T(8,128)S(1)}, u32[]{:S(2)}, u32[]{:S(2)}) %collective-permute-start.12) | collective-permute-done | bytes 114720 | tf_op jit(solution)/shard_map/ppermute | solution.py:160
  76.8 1.4 %shard_map.81 = (f32[18,8,128]{2,1,0:T(8,128)S(1)}, f32[9,2,8,128]{3,2,1,0:T(8,128)S(1)}, f32[4,2,6,8,128]{4,3,2,1,0:T(8,128)S(1)}) custom-call(s32[1]{0:T(128)} %bitcast.flat_ref, f32[2,8,128]{2,1,0:T(8,128)S(1)} %bitcast.33, f32[28,8,128]{2,1,0:T(8,128)S(1)} %get-tuple-element.54.mine_ref, f32[28,8,128]{2,1,0:T(8,128)S(1)} %collective-permute-done.12.theirs_ref, ...), custom_call_target="tpu_custom_call" | custom-call | flops 5980164 | bytes 5980164 | tf_op jit(solution)/shard_map/pallas_call | solution.py:479
  78.2 0.1 collective-permute-start.13
  78.3 0.6 collective-permute-done.10.theirs_ref
  78.9 1.4 %shard_map.79 = (f32[18,8,128]{2,1,0:T(8,128)S(1)}, f32[9,2,8,128]{3,2,1,0:T(8,128)S(1)}, f32[4,2,6,8,128]{4,3,2,1,0:T(8,128)S(1)}) custom-call(s32[1]{0:T(128)} %bitcast.flat_ref, f32[2,8,128]{2,1,0:T(8,128)S(1)} %bitcast.34, f32[28,8,128]{2,1,0:T(8,128)S(1)} %get-tuple-element.48.mine_ref, f32[28,8,128]{2,1,0:T(8,128)S(1)} %collective-permute-done.10.theirs_ref, ...), custom_call_target="tpu_custom_call" | custom-call | flops 5980164 | bytes 5980164 | tf_op jit(solution)/shard_map/pallas_call | solution.py:479
  80.3 2.4 %collective-permute-start.11 = (f32[18,8,128]{2,1,0:T(8,128)S(1)}, f32[18,8,128]{2,1,0:T(8,128)S(1)}, u32[]{:S(2)}, u32[]{:S(2)}) collective-permute-start(f32[18,8,128]{2,1,0:T(8,128)S(1)} %get-tuple-element.51.mine_ref), channel_id=1, source_target_pairs={{0,16},{1,17},{2,18},{3,19},{4,20},{5,21},{6,22},{7,23},{8,24},{9,... | collective-permute-start | bytes 221192 | tf_op jit(solution)/shard_map/ppermute | solution.py:160
  82.7 2.7 %collective-permute-done.13.theirs_ref = f32[18,8,128]{2,1,0:T(8,128)S(1)} collective-permute-done((f32[18,8,128]{2,1,0:T(8,128)S(1)}, f32[18,8,128]{2,1,0:T(8,128)S(1)}, u32[]{:S(2)}, u32[]{:S(2)}) %collective-permute-start.13) | collective-permute-done | bytes 73760 | tf_op jit(solution)/shard_map/ppermute | solution.py:160
  85.4 0.7 shard_map.82.refs_0_
  86.1 0.6 collective-permute-done.11.theirs_ref
  86.7 0.8 shard_map.83
  87.4 15.0 %all_to_all.5.back_ref = f32[16,8,8,128]{3,2,1,0:T(8,128)S(1)} all-to-all(f32[16,8,8,128]{3,2,1,0:T(8,128)S(1)} %shard_map.83), channel_id=1, replica_groups={{0,1,2,3,4,5,6,7,8,9,10,11,12,13,14,15},{16,17,18,19,20,21,22,23,24,25,..., dimensions={0} | all-to-all | bytes 1048576 | tf_op jit(solution)/shard_map/all_to_all | solution.py:566
  102.5 1.0 shard_map.84
  (11 shorter events, 0.1 us)
Async XLA Ops:
  0.6 1.5 %copy-start = (bf16[3,3,3,32,4,256]{5,4,3,2,1,0:T(4,128)(2,1)S(1)}, bf16[3,3,3,32,4,256]{5,4,3,2,1,0:T(4,128)(2,1)}, u32[]{:S(2)}) copy-start(bf16[3,3,3,32,4,256]{5,4,3,2,1,0:T(4,128)(2,1)} %param.6) | copy-start | bytes 5308420
  2.1 0.7 copy-start.1
  2.8 1.0 copy-start.3
  3.8 0.9 copy-start.4
  4.7 0.9 copy-start.5
  5.6 0.7 copy-start.6
  8.0 6.2 %collective-permute-start.3 = (f32[3,64,8,128]{3,2,1,0:T(8,128)S(1)}, f32[3,64,8,128]{3,2,1,0:T(8,128)S(1)}, u32[]{:S(2)}, u32[]{:S(2)}) collective-permute-start(f32[3,64,8,128]{3,2,1,0:T(8,128)S(1)} %get-tuple-element.36), channel_id=1, source_target_pairs={{0,2},{1,3},{2,0},{3,1},{4,6},{5,7},{6,4},{7,5},{8,10},{9,11},{10,... | collective-permute-start | bytes 2359304 | tf_op jit(solution)/shard_map/ppermute | solution.py:160
  8.5 15.1 %collective-permute-start.4 = (f32[2,64,8,128]{3,2,1,0:T(8,128)S(1)}, f32[2,64,8,128]{3,2,1,0:T(8,128)S(1)}, u32[]{:S(2)}, u32[]{:S(2)}) collective-permute-start(f32[2,64,8,128]{3,2,1,0:T(8,128)S(1)} %get-tuple-element.40), channel_id=1, source_target_pairs={{0,4},{1,5},{2,6},{3,7},{4,0},{5,1},{6,2},{7,3},{8,12},{9,13},{10,... | collective-permute-start | bytes 1572872 | tf_op jit(solution)/shard_map/ppermute | solution.py:160
  11.0 15.7 %collective-permute-start.5 = (f32[2,64,8,128]{3,2,1,0:T(8,128)S(1)}, f32[2,64,8,128]{3,2,1,0:T(8,128)S(1)}, u32[]{:S(2)}, u32[]{:S(2)}) collective-permute-start(f32[2,64,8,128]{3,2,1,0:T(8,128)S(1)} %get-tuple-element.41), channel_id=1, source_target_pairs={{0,9},{1,8},{2,11},{3,10},{4,13},{5,12},{6,15},{7,14},{8,1},{9,0},... | collective-permute-start | bytes 1572872 | tf_op jit(solution)/shard_map/ppermute | solution.py:160
  13.6 23.8 %collective-permute-start.1 = (f32[2,65,8,128]{3,2,1,0:T(8,128)S(1)}, f32[2,65,8,128]{3,2,1,0:T(8,128)S(1)}, u32[]{:S(2)}, u32[]{:S(2)}) collective-permute-start(f32[2,65,8,128]{3,2,1,0:T(8,128)S(1)} %get-tuple-element.33), channel_id=1, source_target_pairs={{0,1},{1,0},{2,3},{3,2},{4,5},{5,4},{6,7},{7,6},{8,9},{9,8},{10,11... | collective-permute-start | bytes 1597448 | tf_op jit(solution)/shard_map/ppermute | solution.py:160
  14.1 23.2 %collective-permute-start.2 = (f32[2,64,8,128]{3,2,1,0:T(8,128)S(1)}, f32[2,64,8,128]{3,2,1,0:T(8,128)S(1)}, u32[]{:S(2)}, u32[]{:S(2)}) collective-permute-start(f32[2,64,8,128]{3,2,1,0:T(8,128)S(1)} %get-tuple-element.34), channel_id=1, source_target_pairs={{0,12},{1,13},{2,14},{3,15},{4,8},{5,9},{6,10},{7,11},{8,4},{9,5},... | collective-permute-start | bytes 1572872 | tf_op jit(solution)/shard_map/ppermute | solution.py:160
  26.9 38.4 %copy-start.2 = (f32[2,4,256]{2,1,0:T(4,128)S(1)}, f32[2,4,256]{2,1,0:T(4,128)}, u32[]{:S(2)}) copy-start(f32[2,4,256]{2,1,0:T(4,128)} %param.10) | copy-start | bytes 24580
  37.5 27.9 %collective-permute-start.6 = (f32[4,64,8,128]{3,2,1,0:T(8,128)S(1)}, f32[4,64,8,128]{3,2,1,0:T(8,128)S(1)}, u32[]{:S(2)}, u32[]{:S(2)}) collective-permute-start(f32[4,64,8,128]{3,2,1,0:T(8,128)S(1)} %pad_maximum_fusion), channel_id=1, source_target_pairs={{0,2},{1,3},{2,0},{3,1},{4,6},{5,7},{6,4},{7,5},{8,10},{9,11},{10,... | collective-permute-start | bytes 3145736 | tf_op jit(solution)/shard_map/ppermute | solution.py:160
  37.6 14.8 %collective-permute-start.7 = (f32[2,64,8,128]{3,2,1,0:T(8,128)S(1)}, f32[2,64,8,128]{3,2,1,0:T(8,128)S(1)}, u32[]{:S(2)}, u32[]{:S(2)}) collective-permute-start(f32[2,64,8,128]{3,2,1,0:T(8,128)S(1)} %get-tuple-element.45), channel_id=1, source_target_pairs={{0,8},{1,9},{2,10},{3,11},{4,12},{5,13},{6,14},{7,15},{8,0},{9,1},... | collective-permute-start | bytes 1572872 | tf_op jit(solution)/shard_map/ppermute | solution.py:160
  39.2 26.1 %collective-permute-start.8 = (f32[2,64,8,128]{3,2,1,0:T(8,128)S(1)}, f32[2,64,8,128]{3,2,1,0:T(8,128)S(1)}, u32[]{:S(2)}, u32[]{:S(2)}) collective-permute-start(f32[2,64,8,128]{3,2,1,0:T(8,128)S(1)} %get-tuple-element.46), channel_id=1, source_target_pairs={{0,5},{1,4},{2,7},{3,6},{4,1},{5,0},{6,3},{7,2},{8,13},{9,12},{10,... | collective-permute-start | bytes 1572872 | tf_op jit(solution)/shard_map/ppermute | solution.py:160
  40.5 24.8 %collective-permute-start.9 = (f32[2,64,8,128]{3,2,1,0:T(8,128)S(1)}, f32[2,64,8,128]{3,2,1,0:T(8,128)S(1)}, u32[]{:S(2)}, u32[]{:S(2)}) collective-permute-start(f32[2,64,8,128]{3,2,1,0:T(8,128)S(1)} %pad_maximum_fusion.3), channel_id=1, source_target_pairs={{0,13},{1,12},{2,15},{3,14},{4,9},{5,8},{6,11},{7,10},{8,5},{9,4},... | collective-permute-start | bytes 1572872 | tf_op jit(solution)/shard_map/ppermute | solution.py:160
  42.0 1.5 %collective-permute-start = (f32[64,8,128]{2,1,0:T(8,128)S(1)}, f32[64,8,128]{2,1,0:T(8,128)S(1)}, u32[]{:S(2)}, u32[]{:S(2)}) collective-permute-start(f32[64,8,128]{2,1,0:T(8,128)S(1)} %get-tuple-element.32), channel_id=1, source_target_pairs={{0,2},{1,3},{2,0},{3,1},{4,6},{5,7},{6,4},{7,5},{8,10},{9,11},{10,... | collective-permute-start | bytes 786440 | tf_op jit(solution)/shard_map/ppermute | solution.py:160
  66.2 10.6 %collective-permute-start.12 = (f32[28,8,128]{2,1,0:T(8,128)S(1)}, f32[28,8,128]{2,1,0:T(8,128)S(1)}, u32[]{:S(2)}, u32[]{:S(2)}) collective-permute-start(f32[28,8,128]{2,1,0:T(8,128)S(1)} %get-tuple-element.54.mine_ref), channel_id=1, source_target_pairs={{0,16},{1,17},{2,18},{3,19},{4,20},{5,21},{6,22},{7,23},{8,24},{9,... | collective-permute-start | bytes 344072 | tf_op jit(solution)/shard_map/ppermute | solution.py:160
  69.7 9.2 %collective-permute-start.10 = (f32[28,8,128]{2,1,0:T(8,128)S(1)}, f32[28,8,128]{2,1,0:T(8,128)S(1)}, u32[]{:S(2)}, u32[]{:S(2)}) collective-permute-start(f32[28,8,128]{2,1,0:T(8,128)S(1)} %get-tuple-element.48.mine_ref), channel_id=1, source_target_pairs={{0,16},{1,17},{2,18},{3,19},{4,20},{5,21},{6,22},{7,23},{8,24},{9,... | collective-permute-start | bytes 344072 | tf_op jit(solution)/shard_map/ppermute | solution.py:160
  78.2 7.2 %collective-permute-start.13 = (f32[18,8,128]{2,1,0:T(8,128)S(1)}, f32[18,8,128]{2,1,0:T(8,128)S(1)}, u32[]{:S(2)}, u32[]{:S(2)}) collective-permute-start(f32[18,8,128]{2,1,0:T(8,128)S(1)} %get-tuple-element.57.mine_ref), channel_id=1, source_target_pairs={{0,16},{1,17},{2,18},{3,19},{4,20},{5,21},{6,22},{7,23},{8,24},{9,... | collective-permute-start | bytes 221192 | tf_op jit(solution)/shard_map/ppermute | solution.py:160
  80.3 6.4 %collective-permute-start.11 = (f32[18,8,128]{2,1,0:T(8,128)S(1)}, f32[18,8,128]{2,1,0:T(8,128)S(1)}, u32[]{:S(2)}, u32[]{:S(2)}) collective-permute-start(f32[18,8,128]{2,1,0:T(8,128)S(1)} %get-tuple-element.51.mine_ref), channel_id=1, source_target_pairs={{0,16},{1,17},{2,18},{3,19},{4,20},{5,21},{6,22},{7,23},{8,24},{9,... | collective-permute-start | bytes 221192 | tf_op jit(solution)/shard_map/ppermute | solution.py:160
where the time goes:
time: 104 us; the launch traced here: 103 us
  waiting for transfers between devices  56.8 us (55%)
  starting transfers between devices  16.2 us (16%)
  blocking collectives  15 us (14%)
  Pallas kernels  8.68 us (8%)
  local copies, waits for them, and re-layouts  5.74 us (6%)
    ppermute x14, waiting for transfers between devices, shift_by(): return lax.ppermute(cells, axes, [(i, i ^ mask) for i in range(count)])  56.8 us
    ppermute x14, starting transfers between devices, shift_by(): return lax.ppermute(cells, axes, [(i, i ^ mask) for i in range(count)])  16.2 us
    all_to_all x1, blocking collectives, level_shards(): lax.all_to_all(back, ('mem', 'lat'), 0, 0, axis_index_groups=groups, tile...  15 us
    pallas_call x8, Pallas kernels, call(): pl.pallas_call(kernel, out_shape=[jax.ShapeDtypeStruct(shape, jnp.float32...  8.68 us
    unnamed x14, local copies, waits for them, and re-layouts  5.61 us
  transfers between devices with their start and end apart: 14, of which 11 were waited for; matrix products, arithmetic and copies ran while one was open for 0% of the time, Pallas kernels for 4%

commit v1 on v0

--- a/solution.py
+++ b/solution.py
@@ -171,10 +171,18 @@
         self.owned = owned_rows
         self.chunks = levels // GROUP
         self.planes = self.fields * members
-        self.rows = self.planes + members + 2
-        self.all_rows = self.chunks * self.rows
+        self.extras = members + 2
+        self.lead_rows = self.planes + self.chunks * self.extras
+        self.all_rows = self.lead_rows + (self.chunks - 1) * self.planes
         self.held = held_fields(self.fields, levels)
         self.sums = self.fields * 2
+        self.sent_gains = 2 * sum(len(half[0]) for half in self.held)
+
+    def planes_at(self, chunk):
+        return self.lead_rows + (chunk - 1) * self.planes if chunk else 0
+
+    def extras_at(self, chunk):
+        return self.planes + chunk * self.extras
 
 
 def row_in_block(size, level, mem_index):
@@ -191,9 +199,9 @@
     return outs[2 + len(EARLY) + place] if core == 0 else outs[-1].at[place]
 
 
-def pack_kernel(size, flat_ref, perturb_hbm, alpha_hbm, innov_hbm, weight_hbm, mask_ref, near_ref, *refs):
-    outs, scratch = refs[:-7], refs[-7:]
-    perturb_ref, alpha_ref, innov_ref, weight_ref, tiles_ref, plane_sems, sems = scratch
+def pack_kernel(size, flat_ref, perturb_hbm, alpha_hbm, innov_hbm, weight_hbm, mask_hbm, near_hbm, *refs):
+    outs, scratch = refs[:-9], refs[-9:]
+    perturb_ref, alpha_ref, innov_ref, weight_ref, mask_ref, near_ref, tiles_ref, plane_sems, sems = scratch
     flat = flat_ref[0]
     own = lax.rem(flat, GROUP)
     mem_index = lax.div(flat, 2)
@@ -207,11 +215,19 @@
     copies = [
         pltpu.make_async_copy(source, target, sems.at[place])
         for place, (source, target) in enumerate(
-            ((alpha_hbm, alpha_ref), (innov_hbm, innov_ref), (weight_hbm, weight_ref))
+            (
+                (mask_hbm, mask_ref),
+                (near_hbm, near_ref),
+                (alpha_hbm, alpha_ref),
+                (innov_hbm, innov_ref),
+                (weight_hbm, weight_ref),
+            )
         )
     ]
     for copy in plane_copies + copies:
         copy.start()
+    copies[0].wait()
+    copies[1].wait()
     tiles = mask_ref.shape[-1]
     shape = (tiles, tiles * TILE)
     spread_out = lax.broadcasted_iota(jnp.int32, shape, 0) == lax.div(lax.broadcasted_iota(jnp.int32, shape, 1), TILE)
@@ -233,14 +249,14 @@
         plane_copies[part].wait()
         for chip, core, chunk in places:
             planes = perturb_ref[part * step : (part + 1) * step, level_of(chip, core, chunk)]
-            base = chunk * size.rows + part * step
+            base = size.planes_at(chunk) + part * step
             pack_target(size, outs, chip, core)[base : base + step] = planes.astype(jnp.float32)
-    for copy in copies:
+    for copy in copies[2:]:
         copy.wait()
     for chip, core, chunk in places:
         out = pack_target(size, outs, chip, core)
         level = level_of(chip, core, chunk)
-        base = chunk * size.rows + size.planes
+        base = size.extras_at(chunk)
         out[base : base + size.members] = alpha_ref[:, level]
         row, inside, field = row_in_block(size, level, mem_index)
         row = jnp.minimum(row, size.owned - 1)
@@ -251,26 +267,36 @@
 
 
 class Pieces:
-    def __init__(self, size, refs):
+    def __init__(self, size, chunk, refs):
         self.size = size
+        self.chunk = chunk
         self.refs = refs
         self.far_ref = refs[2 + EARLY.index(1)]
 
-    def at(self, chip, core):
+    def place(self, chip, core):
         if chip == 0:
-            return self.refs[core], ()
+            return self.refs[core], (), True
         if chip in EARLY:
             place = EARLY.index(chip)
-            return (self.refs[2 + place], (0,)) if core == 0 else (self.refs[2 + len(EARLY)], (place,))
-        return self.refs[3 + len(EARLY) + LATE.index(chip)], (core,)
-
-    def block(self, chip, core, chunk, row):
-        ref, lead = self.at(chip, core)
-        return ref[lead + (chunk * self.size.rows + row,)]
-
-    def alpha(self, chip, core, chunk):
-        ref, lead = self.at(chip, core)
-        base = chunk * self.size.rows + self.size.planes
+            if core == 0:
+                return self.refs[2 + place], (0,), True
+            return self.refs[2 + len(EARLY)], (place,), True
+        return self.refs[3 + len(EARLY) + LATE.index(chip)], (core,), False
+
+    def plane(self, chip, core, row):
+        ref, lead, whole = self.place(chip, core)
+        if not whole and self.chunk:
+            ref = self.refs[3 + len(EARLY) + len(LATE) + LATE.index(chip)]
+        base = self.size.planes_at(self.chunk) if whole else 0
+        return ref[lead + (base + row,)]
+
+    def extra(self, chip, core, chunk, row):
+        ref, lead, _ = self.place(chip, core)
+        return ref[lead + (self.size.extras_at(chunk) + row,)]
+
+    def alpha(self, chip, core):
+        ref, lead, _ = self.place(chip, core)
+        base = self.size.extras_at(self.chunk)
         return ref[lead + (slice(base, base + self.size.members),)]
 
     def far(self):
@@ -325,18 +351,18 @@
     return near, far
 
 
-def add_products(size, pieces, chunk, pair, spread, sums):
+def add_products(size, pieces, pair, spread, sums):
     for half in range(2):
         for core in range(CORES):
             for field in range(size.fields):
                 for member in range(size.members):
-                    plane = pieces.block(2 * pair + half, core, chunk, field * size.members + member)
+                    plane = pieces.plane(2 * pair + half, core, field * size.members + member)
                     term = plane * spread[half][core * size.members + member]
                     known = sums[half][field]
                     sums[half][field] = term if known is None else known + term
 
 
-def adjoint_of(size, pieces, chunk, pair, misfit):
+def adjoint_of(size, pieces, pair, misfit):
     halves = []
     for half in range(2):
         found = []
@@ -344,7 +370,7 @@
             for member in range(size.members):
                 total = None
                 for field in range(size.fields):
-                    plane = pieces.block(2 * pair + half, core, chunk, field * size.members + member)
+                    plane = pieces.plane(2 * pair + half, core, field * size.members + member)
                     term = plane * misfit[half][field]
                     total = term if total is None else total + term
                 found.append(total)
@@ -352,75 +378,96 @@
     return halves
 
 
-def first_alpha(pieces, chunk, pair):
+def first_alpha(pieces, pair):
     return [
-        jnp.concatenate([pieces.alpha(2 * pair + half, core, chunk) for core in range(CORES)]) for half in range(2)
+        jnp.concatenate([pieces.alpha(2 * pair + half, core) for core in range(CORES)]) for half in range(2)
     ]
 
 
+def gather_slots(size, pieces, mem_index, own, gain_ref, innov_ref):
+    gain_ref[...] = jnp.zeros_like(gain_ref)
+    innov_ref[...] = jnp.zeros_like(innov_ref)
+    for chunk in range(size.chunks):
+        for chip in range(0, CHIPS, 2):
+            for core in range(CORES):
+                source = lax.bitwise_xor(mem_index, (chip & 6) | core)
+                _, inside, field = row_in_block(size, own + chunk * GROUP, source)
+
+                @pl.when(inside)
+                def _(chip=chip, core=core, chunk=chunk, field=field):
+                    for half in range(2):
+                        innov_ref[chunk, field, half] = pieces.extra(chip + half, core, chunk, size.members)
+                        gain_ref[chunk, field, half] = pieces.extra(chip + half, core, chunk, size.members + 1)
+
+
+def gain_places(size):
+    row, found = size.sums, []
+    for chunk, halves in enumerate(size.held):
+        for first, second in zip(*halves):
+            found.append((row, chunk, first, second))
+            row += 2
+    return found
+
+
 def first_kernel(chunk, size, flat_ref, near_ref, *refs):
-    pieces, (sum_ref, gain_ref, innov_ref) = Pieces(size, refs[:-3]), refs[-3:]
+    if chunk:
+        innov_ref, sum_ref = refs[0], refs[-1]
+        pieces = Pieces(size, chunk, refs[1:-1])
+    else:
+        sum_ref, gain_ref, innov_ref = refs[-3:]
+        pieces = Pieces(size, chunk, refs[:-3])
     flat = flat_ref[0]
     stencil = stencils(flat, [near_ref[0], near_ref[1]], pieces.far())
-    mem_index = lax.div(flat, 2)
-    side = lax.div(flat, GROUP)
-    gain_ref[...] = jnp.zeros_like(gain_ref)
-    innov_ref[...] = jnp.zeros_like(innov_ref)
-    level = lax.rem(flat, GROUP) + chunk * GROUP
-    for chip in range(0, CHIPS, 2):
-        for core in range(CORES):
-            source = lax.bitwise_xor(mem_index, (chip & 6) | core)
-            _, inside, field = row_in_block(size, level, source)
-
-            @pl.when(inside)
-            def _(chip=chip, core=core, field=field):
-                for half in range(2):
-                    innov_ref[field, half] = pieces.block(chip + half, core, chunk, size.rows - 2)
-                    gain_ref[field, half] = pieces.block(chip + half, core, chunk, size.rows - 1)
-
-    for place, (first, second) in enumerate(zip(*size.held[chunk])):
-        field = jnp.where(side == 0, first, second)
-        sum_ref[pl.ds(size.sums + 2 * place, 2)] = gain_ref[field]
+    if not chunk:
+        side = lax.div(flat, GROUP)
+        gather_slots(size, pieces, lax.div(flat, 2), lax.rem(flat, GROUP), gain_ref, innov_ref)
+        for row, part, first, second in gain_places(size):
+            sum_ref[pl.ds(row, 2)] = gain_ref[part, jnp.where(side == 0, first, second)]
     sums = [[None] * size.fields for _ in range(2)]
     for pair in range(CHIPS // 2):
-        spread = diffuse_pair(*first_alpha(pieces, chunk, pair), stencil)
-        add_products(size, pieces, chunk, pair, spread, sums)
+        spread = diffuse_pair(*first_alpha(pieces, pair), stencil)
+        add_products(size, pieces, pair, spread, sums)
     for field in range(size.fields):
         for half in range(2):
-            sum_ref[field * 2 + half] = sums[half][field] - innov_ref[field, half]
-
-
-def misfit_of(size, gain_ref, mine_ref, theirs_ref):
+            sum_ref[field * 2 + half] = sums[half][field] - innov_ref[chunk, field, half]
+
+
+def misfit_of(size, chunk, gain_ref, mine_ref, theirs_ref):
     return [
         [
-            gain_ref[field, half] * (mine_ref[field * 2 + half] + theirs_ref[field * 2 + half])
+            gain_ref[chunk, field, half] * (mine_ref[field * 2 + half] + theirs_ref[field * 2 + half])
             for field in range(size.fields)
         ]
         for half in range(2)
     ]
 
 
-def middle_kernel(chunk, size, flat_ref, near_ref, mine_ref, theirs_ref, held_ref, innov_ref, *refs):
-    pieces, (sum_ref, gain_ref, alpha_ref) = Pieces(size, refs[:-3]), refs[-3:]
+def middle_kernel(chunk, size, flat_ref, near_ref, mine_ref, theirs_ref, gain_in_ref, innov_ref, *refs):
+    if chunk:
+        gain_ref, (sum_ref, alpha_ref) = gain_in_ref, refs[-2:]
+        pieces = Pieces(size, chunk, refs[:-2])
+    else:
+        sum_ref, alpha_ref, gain_ref = refs[-3:]
+        pieces = Pieces(size, chunk, refs[:-3])
     flat = flat_ref[0]
-    side = lax.div(flat, GROUP)
     stencil = stencils(flat, [near_ref[0], near_ref[1]], pieces.far())
-    gain_ref[...] = held_ref[...]
-    for place, (first, second) in enumerate(zip(*size.held[chunk])):
-        field = jnp.where(side == 0, second, first)
-        gain_ref[field] = theirs_ref[pl.ds(size.sums + 2 * place, 2)]
-    misfit = misfit_of(size, gain_ref, mine_ref, theirs_ref)
+    if not chunk:
+        side = lax.div(flat, GROUP)
+        gain_ref[...] = gain_in_ref[...]
+        for row, part, first, second in gain_places(size):
+            gain_ref[part, jnp.where(side == 0, second, first)] = theirs_ref[pl.ds(row, 2)]
+    misfit = misfit_of(size, chunk, gain_ref, mine_ref, theirs_ref)
     sums = [[None] * size.fields for _ in range(2)]
     for pair in range(CHIPS // 2):
-        change = diffuse_pair(*adjoint_of(size, pieces, chunk, pair, misfit), stencil)
-        before = first_alpha(pieces, chunk, pair)
+        change = diffuse_pair(*adjoint_of(size, pieces, pair, misfit), stencil)
+        before = first_alpha(pieces, pair)
         alpha = [old - 0.3 * (old + new) for old, new in zip(before, change)]
         for half in range(2):
             alpha_ref[pair, half] = alpha[half]
-        add_products(size, pieces, chunk, pair, diffuse_pair(*alpha, stencil), sums)
+        add_products(size, pieces, pair, diffuse_pair(*alpha, stencil), sums)
     for field in range(size.fields):
         for half in range(2):
-            sum_ref[field * 2 + half] = sums[half][field] - innov_ref[field, half]
+            sum_ref[field * 2 + half] = sums[half][field] - innov_ref[chunk, field, half]
 
 
 def last_kernel(chunk, size, flat_ref, near_ref, mine_ref, theirs_ref, gain_ref, alpha_ref, *refs):
@@ -432,15 +479,15 @@
     if chunk:
         out_ref[:, :base] = refs[0][...]
         refs = refs[1:]
-    pieces = Pieces(size, refs)
+    pieces = Pieces(size, chunk, refs)
     stencil = stencils(flat, [near_ref[0], near_ref[1]], pieces.far())
-    misfit = misfit_of(size, gain_ref, mine_ref, theirs_ref)
+    misfit = misfit_of(size, chunk, gain_ref, mine_ref, theirs_ref)
     for half in range(2):
         for field in range(size.fields):
             misfit_ref[half, field] = misfit[half][field]
     level = own + chunk * GROUP
     for pair in range(CHIPS // 2):
-        change = diffuse_pair(*adjoint_of(size, pieces, chunk, pair, misfit), stencil)
+        change = diffuse_pair(*adjoint_of(size, pieces, pair, misfit), stencil)
         for half in range(2):
             old = alpha_ref[pair, half]
             alpha = old - 0.3 * (old + change[half])
@@ -484,7 +531,11 @@
         scratch_shapes=scratch,
         cost_estimate=pl.CostEstimate(flops=moved, bytes_accessed=moved, transcendentals=0),
         compiler_params=pltpu.CompilerParams(vmem_limit_bytes=limit * 1024 * 1024),
-    )(*operands)
+    )(*[in_hbm(x) if space is pltpu.HBM else x for x, space in zip(operands, spaces)])
+
+
+def in_hbm(cells):
+    return pltpu.with_memory_space_constraint(cells, pltpu.HBM)
 
 
 def spread_levels(size, flat, near, perturb, alpha_init, innovation, obs_weight, obs_mask):
@@ -509,23 +560,32 @@
             pltpu.VMEM((size.members, levels, *block), jnp.float32),
             pltpu.VMEM((size.owned, *block), jnp.float32),
             pltpu.VMEM((size.owned, *block), jnp.float32),
+            pltpu.VMEM(obs_mask.shape, jnp.int32),
+            pltpu.VMEM(near.shape, jnp.float32),
             pltpu.VMEM((size.slots, *block), jnp.float32),
             pltpu.SemaphoreType.DMA((size.members,)),
-            pltpu.SemaphoreType.DMA((3,)),
+            pltpu.SemaphoreType.DMA((5,)),
         ],
-        [pltpu.SMEM] + [pltpu.HBM] * 4 + [pltpu.VMEM] * 2,
+        [pltpu.SMEM] + [pltpu.HBM] * 6,
     )
     kept, early, late, late_out = packed[:2], packed[2:6], packed[6:9], packed[9]
     crossed = shift_by(CORES, late_out)
-    late = [jnp.stack([cells, crossed[place]]) for place, cells in enumerate(late)]
     own_crossed = shift_by(CORES, kept[1])
     got = [shift_by(flat_offset(chip, 0), cells) for chip, cells in zip(EARLY, early)]
-    got[0], got[1], late[0], late[1] = lax.optimization_barrier((got[0], got[1], late[0], late[1]))
-    got_late = [shift_by(flat_offset(chip, 0), cells) for chip, cells in zip(LATE[:2], late[:2])]
-    got[2], got[3], late[2] = lax.optimization_barrier((got[2], got[3], late[2]))
-    got_late.append(shift_by(flat_offset(LATE[2], 0), late[2]))
+    got_late = []
+    for chunk in range(size.chunks):
+        base = size.planes_at(chunk)
+        rows = slice(base, base + (size.planes if chunk else size.lead_rows))
+        parts = [jnp.stack([cells[rows], crossed[place, rows]]) for place, cells in enumerate(late)]
+        if chunk == 0:
+            got[0], got[1], parts[0], parts[1] = lax.optimization_barrier((got[0], got[1], parts[0], parts[1]))
+            got[2], got[3], parts[2] = lax.optimization_barrier((got[2], got[3], parts[2]))
+        else:
+            got[0], got[1], got[2], got[3], *parts = lax.optimization_barrier((*got, *parts))
+        got_late.append(tuple(shift_by(flat_offset(chip, 0), cells) for chip, cells in zip(LATE, parts)))
     early_crossed = shift_by(CORES, jnp.stack([cells[1, : size.all_rows] for cells in got]))
-    return (kept[0], own_crossed, *got, early_crossed, *got_late)
+    shared = (kept[0], own_crossed, *got, early_crossed)
+    return [shared + got_late[0] + (got_late[chunk] if chunk else ()) for chunk in range(size.chunks)]
 
 
 def level_shards(perturb, alpha_init, innovation, obs_weight, coef, obs_mask):
@@ -536,30 +596,30 @@
     near = fold(coef)
     pieces = spread_levels(size, flat, near, perturb, alpha_init, innovation, obs_weight, obs_mask)
     common = (flat, near)
-    per_field = (size.fields, 2, *block)
+    all_fields = (size.chunks, size.fields, 2, *block)
     alpha_shape = (CHIPS // 2, 2, CORES * size.members, *block)
     chunks = range(size.chunks)
-    first, second, back = [], [], None
+    first, second, back, held, innov, gain = [], [], None, None, None, None
     for chunk in chunks:
-        sent = size.sums + 2 * len(size.held[chunk][0])
-        mine, held, innov = call(
-            functools.partial(first_kernel, chunk, size),
-            [(sent, *block), per_field, per_field],
-            common + pieces,
-        )
-        first.append((mine, shift_by(GROUP, mine), held, innov))
+        kernel = functools.partial(first_kernel, chunk, size)
+        if chunk:
+            (mine,) = call(kernel, [(size.sums, *block)], common + (innov,) + pieces[chunk])
+        else:
+            shapes = [(size.sums + size.sent_gains, *block), all_fields, all_fields]
+            mine, held, innov = call(kernel, shapes, common + pieces[chunk])
+        first.append((mine, shift_by(GROUP, mine)))
     for chunk in chunks:
-        mine, gain, alpha = call(
-            functools.partial(middle_kernel, chunk, size),
-            [(size.sums, *block), per_field, alpha_shape],
-            common + first[chunk] + pieces,
-        )
+        kernel = functools.partial(middle_kernel, chunk, size)
+        shapes = [(size.sums, *block), alpha_shape] + ([] if chunk else [all_fields])
+        operands = common + first[chunk] + (gain if chunk else held, innov) + pieces[chunk]
+        mine, alpha, *rest = call(kernel, shapes, operands)
+        gain = gain if chunk else rest[0]
         second.append((mine, shift_by(GROUP, mine), gain, alpha))
     for chunk in chunks:
         (back,) = call(
             functools.partial(last_kernel, chunk, size),
             [(GROUP, (chunk + 1) * (size.members + 1), *block)],
-            common + second[chunk] + (() if back is None else (back,)) + pieces,
+            common + second[chunk] + (() if back is None else (back,)) + pieces[chunk],
             [pltpu.VMEM((2, size.fields, *block), jnp.float32)],
         )
     groups = [[half * GROUP + place for place in range(GROUP)] for half in range(2)]

time: 104 us -> 93.9 us (0.903)
  waiting for transfers between devices: 56.8 us -> 49.7 us
  local copies, waits for them, and re-layouts: 5.74 us -> 0.19 us
  starting transfers between devices: 16.2 us -> 19.6 us
    ppermute x14 -> x17, waiting for transfers between devices: 56.8 us -> 49.7 us  [shift_by(): return lax.ppermute(cells, axes, [(i, i ^ mask) for i in range(count)])]
    unnamed x14 -> x2, local copies, waits for them, and re-layouts: 5.61 us -> 0.01 us
    ppermute x14 -> x17, starting transfers between devices: 16.2 us -> 19.6 us  [shift_by(): return lax.ppermute(cells, axes, [(i, i ^ mask) for i in range(count)])]
  transfers between devices with their start and end apart: 14 -> 17, of which waited for: 11 -> 11; matrix products, arithmetic and copies ran while one was open for 0% -> 0% of each run, Pallas kernels for 4% -> 6%
where the time goes in v1:
time: 93.9 us; the launch traced here: 93.7 us
  waiting for transfers between devices  49.7 us (53%)
  starting transfers between devices  19.6 us (21%)
  blocking collectives  14.1 us (15%)
  Pallas kernels  9.02 us (10%)
    ppermute x17, waiting for transfers between devices, shift_by(): return lax.ppermute(cells, axes, [(i, i ^ mask) for i in range(count)])  49.7 us
    ppermute x17, starting transfers between devices, shift_by(): return lax.ppermute(cells, axes, [(i, i ^ mask) for i in range(count)])  19.6 us
    all_to_all x1, blocking collectives, level_shards(): lax.all_to_all(back, ('mem', 'lat'), 0, 0, axis_index_groups=groups, tile...  14.1 us
    pallas_call x8, Pallas kernels, call(): pl.pallas_call(kernel, out_shape=[jax.ShapeDtypeStruct(shape, jnp.float32...  9.02 us
  transfers between devices with their start and end apart: 17, of which 11 were waited for; matrix products, arithmetic and copies ran while one was open for 0% of the time, Pallas kernels for 6%

profile of v1, /device:TPU:0, one launch (start us, length us, event | category | flops | bytes accessed | tf_op | source)
XLA Modules:
  0.0 93.7 jit_solution(16530710574463260266)
XLA Ops:
  0.6 2.1 %shard_map.77 = (f32[64,8,128]{2,1,0:T(8,128)S(1)}, f32[64,8,128]{2,1,0:T(8,128)S(1)}, f32[2,65,8,128]{3,2,1,0:T(8,128)S(1)}, f32[2,64,8,128]{3,2,1,0:T(8,128)S(...) custom-call(s32[1]{0:T(128)} %bitcast.flat_ref, ...), custom_call_target="tpu_custom_call" | custom-call | flops 6521604 | bytes 6521604 | tf_op jit(solution)/shard_map/pallas_call | solution.py:526
  2.8 4.0 %collective-permute-start.2 = (f32[2,64,8,128]{3,2,1,0:T(8,128)S(1)}, f32[2,64,8,128]{3,2,1,0:T(8,128)S(1)}, u32[]{:S(2)}, u32[]{:S(2)}) collective-permute-start(f32[2,64,8,128]{3,2,1,0:T(8,128)S(1)} %get-tuple-element.37), channel_id=1, source_target_pairs={{0,12},{1,13},{2,14},{3,15},{4,8},{5,9},{6,10},{7,11},{8,4},{9,5},... | collective-permute-start | bytes 1572872 | tf_op jit(solution)/shard_map/ppermute | solution.py:160
  6.8 0.5 collective-permute-start.4
  7.3 1.4 %collective-permute-start.5 = (f32[2,64,8,128]{3,2,1,0:T(8,128)S(1)}, f32[2,64,8,128]{3,2,1,0:T(8,128)S(1)}, u32[]{:S(2)}, u32[]{:S(2)}) collective-permute-start(f32[2,64,8,128]{3,2,1,0:T(8,128)S(1)} %get-tuple-element.44), channel_id=1, source_target_pairs={{0,9},{1,8},{2,11},{3,10},{4,13},{5,12},{6,15},{7,14},{8,1},{9,0},... | collective-permute-start | bytes 1572872 | tf_op jit(solution)/shard_map/ppermute | solution.py:160
  8.7 0.2 collective-permute-start.1
  8.9 0.0 collective-permute-start.3
  9.0 2.2 %collective-permute-done.3 = f32[3,64,8,128]{3,2,1,0:T(8,128)S(1)} collective-permute-done((f32[3,64,8,128]{3,2,1,0:T(8,128)S(1)}, f32[3,64,8,128]{3,2,1,0:T(8,128)S(1)}, u32[]{:S(2)}, u32[]{:S(2)}) %collective-permute-start.3) | collective-permute-done | bytes 786464 | tf_op jit(solution)/shard_map/ppermute | solution.py:160
  11.3 18.7 %collective-permute-done.4.refs_4_.refs_5_ = f32[2,64,8,128]{3,2,1,0:T(8,128)S(1)} collective-permute-done((f32[2,64,8,128]{3,2,1,0:T(8,128)S(1)}, f32[2,64,8,128]{3,2,1,0:T(8,128)S(1)}, u32[]{:S(2)}, u32[]{:S(2)}) %collective-permute-start.4) | collective-permute-done | bytes 524320 | tf_op jit(solution)/shard_map/ppermute | solution.py:160
  30.0 1.3 %collective-permute-done.5.refs_5_.refs_6_ = f32[2,64,8,128]{3,2,1,0:T(8,128)S(1)} collective-permute-done((f32[2,64,8,128]{3,2,1,0:T(8,128)S(1)}, f32[2,64,8,128]{3,2,1,0:T(8,128)S(1)}, u32[]{:S(2)}, u32[]{:S(2)}) %collective-permute-start.5) | collective-permute-done | bytes 524320 | tf_op jit(solution)/shard_map/ppermute | solution.py:160
  31.3 0.0 collective-permute-done.2.refs_3_.refs_4_
  31.3 1.7 %collective-permute-done.1.refs_2_.refs_3_ = f32[2,65,8,128]{3,2,1,0:T(8,128)S(1)} collective-permute-done((f32[2,65,8,128]{3,2,1,0:T(8,128)S(1)}, f32[2,65,8,128]{3,2,1,0:T(8,128)S(1)}, u32[]{:S(2)}, u32[]{:S(2)}) %collective-permute-start.1) | collective-permute-done | bytes 532512 | tf_op jit(solution)/shard_map/ppermute | solution.py:160
  33.1 0.0 copy-start
  33.2 0.1 pad_maximum_fusion
  33.3 0.1 collective-permute-start.6
  33.4 1.6 %collective-permute-start.7 = (f32[2,37,8,128]{3,2,1,0:T(8,128)S(1)}, f32[2,37,8,128]{3,2,1,0:T(8,128)S(1)}, u32[]{:S(2)}, u32[]{:S(2)}) collective-permute-start(f32[2,37,8,128]{3,2,1,0:T(8,128)S(1)} %pad_maximum_fusion.1), channel_id=1, source_target_pairs={{0,8},{1,9},{2,10},{3,11},{4,12},{5,13},{6,14},{7,15},{8,0},{9,1},... | collective-permute-start | bytes 909320 | tf_op jit(solution)/shard_map/ppermute | solution.py:160
  35.0 1.4 %collective-permute-start.8 = (f32[2,37,8,128]{3,2,1,0:T(8,128)S(1)}, f32[2,37,8,128]{3,2,1,0:T(8,128)S(1)}, u32[]{:S(2)}, u32[]{:S(2)}) collective-permute-start(f32[2,37,8,128]{3,2,1,0:T(8,128)S(1)} %pad_maximum_fusion.2), channel_id=1, source_target_pairs={{0,5},{1,4},{2,7},{3,6},{4,1},{5,0},{6,3},{7,2},{8,13},{9,12},{10,... | collective-permute-start | bytes 909320 | tf_op jit(solution)/shard_map/ppermute | solution.py:160
  36.4 0.0 collective-permute-start
  36.4 1.4 %collective-permute-start.9 = (f32[2,37,8,128]{3,2,1,0:T(8,128)S(1)}, f32[2,37,8,128]{3,2,1,0:T(8,128)S(1)}, u32[]{:S(2)}, u32[]{:S(2)}) collective-permute-start(f32[2,37,8,128]{3,2,1,0:T(8,128)S(1)} %pad_maximum_fusion.3), channel_id=1, source_target_pairs={{0,13},{1,12},{2,15},{3,14},{4,9},{5,8},{6,11},{7,10},{8,5},{9,4},... | collective-permute-start | bytes 909320 | tf_op jit(solution)/shard_map/ppermute | solution.py:160
  37.8 0.2 collective-permute-done.refs_1_.refs_2_
  38.0 1.4 %collective-permute-start.10 = (f32[2,27,8,128]{3,2,1,0:T(8,128)S(1)}, f32[2,27,8,128]{3,2,1,0:T(8,128)S(1)}, u32[]{:S(2)}, u32[]{:S(2)}) collective-permute-start(f32[2,27,8,128]{3,2,1,0:T(8,128)S(1)} %pad_maximum_fusion.4), channel_id=1, source_target_pairs={{0,8},{1,9},{2,10},{3,11},{4,12},{5,13},{6,14},{7,15},{8,0},{9,1},... | collective-permute-start | bytes 663560 | tf_op jit(solution)/shard_map/ppermute | solution.py:160
  39.4 4.0 %collective-permute-done.7.refs_7_.refs_8_ = f32[2,37,8,128]{3,2,1,0:T(8,128)S(1)} collective-permute-done((f32[2,37,8,128]{3,2,1,0:T(8,128)S(1)}, f32[2,37,8,128]{3,2,1,0:T(8,128)S(1)}, u32[]{:S(2)}, u32[]{:S(2)}) %collective-permute-start.7) | collective-permute-done | bytes 303136 | tf_op jit(solution)/shard_map/ppermute | solution.py:160
  43.4 1.4 %collective-permute-start.11 = (f32[2,27,8,128]{3,2,1,0:T(8,128)S(1)}, f32[2,27,8,128]{3,2,1,0:T(8,128)S(1)}, u32[]{:S(2)}, u32[]{:S(2)}) collective-permute-start(f32[2,27,8,128]{3,2,1,0:T(8,128)S(1)} %pad_maximum_fusion.5), channel_id=1, source_target_pairs={{0,5},{1,4},{2,7},{3,6},{4,1},{5,0},{6,3},{7,2},{8,13},{9,12},{10,... | collective-permute-start | bytes 663560 | tf_op jit(solution)/shard_map/ppermute | solution.py:160
  44.8 7.6 %collective-permute-done.8.refs_8_.refs_9_ = f32[2,37,8,128]{3,2,1,0:T(8,128)S(1)} collective-permute-done((f32[2,37,8,128]{3,2,1,0:T(8,128)S(1)}, f32[2,37,8,128]{3,2,1,0:T(8,128)S(1)}, u32[]{:S(2)}, u32[]{:S(2)}) %collective-permute-start.8) | collective-permute-done | bytes 303136 | tf_op jit(solution)/shard_map/ppermute | solution.py:160
  52.4 0.2 collective-permute-start.12
  52.6 0.0 collective-permute-done.9.refs_9_.refs_10_
  52.6 0.0 collective-permute-done.6.refs_6_.refs_7_
  52.6 0.0 copy-done
  52.6 0.9 %shard_map.78 = (f32[38,8,128]{2,1,0:T(8,128)S(1)}, f32[2,9,2,8,128]{4,3,2,1,0:T(8,128)S(1)}, f32[2,9,2,8,128]{4,3,2,1,0:T(8,128)S(1)}) custom-call(s32[1]{0:T(128)} %bitcast.flat_ref, f32[2,8,128]{2,1,0:T(8,128)S(1)} %bitcast.39, f32[64,8,128]{2,1,0:T(8,128)S(1)} %get-tuple-element.34.refs_0_.refs_1_, ...), custom_call_target="tpu_custom_call" | custom-call | flops 5046276 | bytes 5046276 | tf_op jit(solution)/shard_map/pallas_call | solution.py:526
  53.6 2.6 %collective-permute-start.14 = (f32[38,8,128]{2,1,0:T(8,128)S(1)}, f32[38,8,128]{2,1,0:T(8,128)S(1)}, u32[]{:S(2)}, u32[]{:S(2)}) collective-permute-start(f32[38,8,128]{2,1,0:T(8,128)S(1)} %get-tuple-element.59.mine_ref), channel_id=1, source_target_pairs={{0,16},{1,17},{2,18},{3,19},{4,20},{5,21},{6,22},{7,23},{8,24},{9,... | collective-permute-start | bytes 466952 | tf_op jit(solution)/shard_map/ppermute | solution.py:160
  56.2 0.0 collective-permute-done.10.refs_11_.refs_10_
  56.2 1.2 %collective-permute-done.11.refs_12_.refs_11_ = f32[2,27,8,128]{3,2,1,0:T(8,128)S(1)} collective-permute-done((f32[2,27,8,128]{3,2,1,0:T(8,128)S(1)}, f32[2,27,8,128]{3,2,1,0:T(8,128)S(1)}, u32[]{:S(2)}, u32[]{:S(2)}) %collective-permute-start.11) | collective-permute-done | bytes 221216 | tf_op jit(solution)/shard_map/ppermute | solution.py:160
  57.4 6.0 %collective-permute-done.12.refs_13_.refs_12_ = f32[2,27,8,128]{3,2,1,0:T(8,128)S(1)} collective-permute-done((f32[2,27,8,128]{3,2,1,0:T(8,128)S(1)}, f32[2,27,8,128]{3,2,1,0:T(8,128)S(1)}, u32[]{:S(2)}, u32[]{:S(2)}) %collective-permute-start.12) | collective-permute-done | bytes 221216 | tf_op jit(solution)/shard_map/ppermute | solution.py:160
  63.5 0.7 shard_map.79.mine_ref
  64.2 1.0 %collective-permute-start.13 = (f32[18,8,128]{2,1,0:T(8,128)S(1)}, f32[18,8,128]{2,1,0:T(8,128)S(1)}, u32[]{:S(2)}, u32[]{:S(2)}) collective-permute-start(f32[18,8,128]{2,1,0:T(8,128)S(1)} %shard_map.79.mine_ref), channel_id=1, source_target_pairs={{0,16},{1,17},{2,18},{3,19},{4,20},{5,21},{6,22},{7,23},{8,24},{9,... | collective-permute-start | bytes 221192 | tf_op jit(solution)/shard_map/ppermute | solution.py:160
  65.2 0.0 collective-permute-done.14.theirs_ref
  65.2 1.4 %shard_map.80 = (f32[18,8,128]{2,1,0:T(8,128)S(1)}, f32[4,2,6,8,128]{4,3,2,1,0:T(8,128)S(1)}, f32[2,9,2,8,128]{4,3,2,1,0:T(8,128)S(1)}) custom-call(s32[1]{0:T(128)} %bitcast.flat_ref, f32[2,8,128]{2,1,0:T(8,128)S(1)} %bitcast.41, f32[38,8,128]{2,1,0:T(8,128)S(1)} %get-tuple-element.59.mine_ref, f32[38,8,128]{2,1,0:T(8,128)S(1)} %collective-permute-done.14.theirs_ref, ...), custom_call_target="tpu_custom_call" | custom-call | flops 5619716 | bytes 5619716 | tf_op jit(solution)/shard_map/pallas_call | solution.py:526
  66.6 2.0 %collective-permute-start.16 = (f32[18,8,128]{2,1,0:T(8,128)S(1)}, f32[18,8,128]{2,1,0:T(8,128)S(1)}, u32[]{:S(2)}, u32[]{:S(2)}) collective-permute-start(f32[18,8,128]{2,1,0:T(8,128)S(1)} %get-tuple-element.64.mine_ref), channel_id=1, source_target_pairs={{0,16},{1,17},{2,18},{3,19},{4,20},{5,21},{6,22},{7,23},{8,24},{9,... | collective-permute-start | bytes 221192 | tf_op jit(solution)/shard_map/ppermute | solution.py:160
  68.7 1.7 %collective-permute-done.13.theirs_ref = f32[18,8,128]{2,1,0:T(8,128)S(1)} collective-permute-done((f32[18,8,128]{2,1,0:T(8,128)S(1)}, f32[18,8,128]{2,1,0:T(8,128)S(1)}, u32[]{:S(2)}, u32[]{:S(2)}) %collective-permute-start.13) | collective-permute-done | bytes 73760 | tf_op jit(solution)/shard_map/ppermute | solution.py:160
  70.4 1.3 %shard_map.81 = (f32[18,8,128]{2,1,0:T(8,128)S(1)}, f32[4,2,6,8,128]{4,3,2,1,0:T(8,128)S(1)}) custom-call(s32[1]{0:T(128)} %bitcast.flat_ref, f32[2,8,128]{2,1,0:T(8,128)S(1)} %bitcast.42, f32[18,8,128]{2,1,0:T(8,128)S(1)} %shard_map.79.mine_ref, f32[18,8,128]{2,1,0:T(8,128)S(1)} %collective-permute-done.13.theirs_ref, ...), custom_call_target="tpu_custom_call" | custom-call | flops 5971972 | bytes 5971972 | tf_op jit(solution)/shard_map/pallas_call | solution.py:526
  71.7 0.2 collective-permute-start.15
  72.0 0.0 collective-permute-done.16.theirs_ref
  72.0 0.7 shard_map.82.refs_0_
  72.7 5.1 %collective-permute-done.15.theirs_ref = f32[18,8,128]{2,1,0:T(8,128)S(1)} collective-permute-done((f32[18,8,128]{2,1,0:T(8,128)S(1)}, f32[18,8,128]{2,1,0:T(8,128)S(1)}, u32[]{:S(2)}, u32[]{:S(2)}) %collective-permute-start.15) | collective-permute-done | bytes 73760 | tf_op jit(solution)/shard_map/ppermute | solution.py:160
  77.8 0.8 shard_map.83
  78.6 14.1 %all_to_all.5.back_ref = f32[16,8,8,128]{3,2,1,0:T(8,128)S(1)} all-to-all(f32[16,8,8,128]{3,2,1,0:T(8,128)S(1)} %shard_map.83), channel_id=1, replica_groups={{0,1,2,3,4,5,6,7,8,9,10,11,12,13,14,15},{16,17,18,19,20,21,22,23,24,25,..., dimensions={0} | all-to-all | bytes 1048576 | tf_op jit(solution)/shard_map/all_to_all | solution.py:626
  92.7 1.0 %shard_map.84 = (f32[3,32,4,256]{3,2,1,0:T(4,128)}, f32[18,4,256]{2,1,0:T(4,128)}) custom-call(s32[1]{0:T(128)} %bitcast.flat_ref, f32[16,8,8,128]{3,2,1,0:T(8,128)S(1)} %all_to_all.5.back_ref), custom_call_target="tpu_custom_call" | custom-call | flops 991236 | bytes 991236 | tf_op jit(solution)/shard_map/pallas_call | solution.py:526
  (16 shorter events, 0.3 us)
Async XLA Ops:
  2.8 28.5 %collective-permute-start.2 = (f32[2,64,8,128]{3,2,1,0:T(8,128)S(1)}, f32[2,64,8,128]{3,2,1,0:T(8,128)S(1)}, u32[]{:S(2)}, u32[]{:S(2)}) collective-permute-start(f32[2,64,8,128]{3,2,1,0:T(8,128)S(1)} %get-tuple-element.37), channel_id=1, source_target_pairs={{0,12},{1,13},{2,14},{3,15},{4,8},{5,9},{6,10},{7,11},{8,4},{9,5},... | collective-permute-start | bytes 1572872 | tf_op jit(solution)/shard_map/ppermute | solution.py:160
  6.8 23.2 %collective-permute-start.4 = (f32[2,64,8,128]{3,2,1,0:T(8,128)S(1)}, f32[2,64,8,128]{3,2,1,0:T(8,128)S(1)}, u32[]{:S(2)}, u32[]{:S(2)}) collective-permute-start(f32[2,64,8,128]{3,2,1,0:T(8,128)S(1)} %get-tuple-element.43), channel_id=1, source_target_pairs={{0,4},{1,5},{2,6},{3,7},{4,0},{5,1},{6,2},{7,3},{8,12},{9,13},{10,... | collective-permute-start | bytes 1572872 | tf_op jit(solution)/shard_map/ppermute | solution.py:160
  7.3 23.9 %collective-permute-start.5 = (f32[2,64,8,128]{3,2,1,0:T(8,128)S(1)}, f32[2,64,8,128]{3,2,1,0:T(8,128)S(1)}, u32[]{:S(2)}, u32[]{:S(2)}) collective-permute-start(f32[2,64,8,128]{3,2,1,0:T(8,128)S(1)} %get-tuple-element.44), channel_id=1, source_target_pairs={{0,9},{1,8},{2,11},{3,10},{4,13},{5,12},{6,15},{7,14},{8,1},{9,0},... | collective-permute-start | bytes 1572872 | tf_op jit(solution)/shard_map/ppermute | solution.py:160
  8.7 24.2 %collective-permute-start.1 = (f32[2,65,8,128]{3,2,1,0:T(8,128)S(1)}, f32[2,65,8,128]{3,2,1,0:T(8,128)S(1)}, u32[]{:S(2)}, u32[]{:S(2)}) collective-permute-start(f32[2,65,8,128]{3,2,1,0:T(8,128)S(1)} %get-tuple-element.36), channel_id=1, source_target_pairs={{0,1},{1,0},{2,3},{3,2},{4,5},{5,4},{6,7},{7,6},{8,9},{9,8},{10,11... | collective-permute-start | bytes 1597448 | tf_op jit(solution)/shard_map/ppermute | solution.py:160
  8.9 2.3 %collective-permute-start.3 = (f32[3,64,8,128]{3,2,1,0:T(8,128)S(1)}, f32[3,64,8,128]{3,2,1,0:T(8,128)S(1)}, u32[]{:S(2)}, u32[]{:S(2)}) collective-permute-start(f32[3,64,8,128]{3,2,1,0:T(8,128)S(1)} %get-tuple-element.39), channel_id=1, source_target_pairs={{0,2},{1,3},{2,0},{3,1},{4,6},{5,7},{6,4},{7,5},{8,10},{9,11},{10,... | collective-permute-start | bytes 2359304 | tf_op jit(solution)/shard_map/ppermute | solution.py:160
  33.1 19.5 %copy-start = (f32[2,4,256]{2,1,0:T(4,128)S(1)}, f32[2,4,256]{2,1,0:T(4,128)}, u32[]{:S(2)}) copy-start(f32[2,4,256]{2,1,0:T(4,128)} %param.10) | copy-start | bytes 24580
  33.3 19.3 %collective-permute-start.6 = (f32[4,64,8,128]{3,2,1,0:T(8,128)S(1)}, f32[4,64,8,128]{3,2,1,0:T(8,128)S(1)}, u32[]{:S(2)}, u32[]{:S(2)}) collective-permute-start(f32[4,64,8,128]{3,2,1,0:T(8,128)S(1)} %pad_maximum_fusion), channel_id=1, source_target_pairs={{0,2},{1,3},{2,0},{3,1},{4,6},{5,7},{6,4},{7,5},{8,10},{9,11},{10,... | collective-permute-start | bytes 3145736 | tf_op jit(solution)/shard_map/ppermute | solution.py:160
  33.4 10.1 %collective-permute-start.7 = (f32[2,37,8,128]{3,2,1,0:T(8,128)S(1)}, f32[2,37,8,128]{3,2,1,0:T(8,128)S(1)}, u32[]{:S(2)}, u32[]{:S(2)}) collective-permute-start(f32[2,37,8,128]{3,2,1,0:T(8,128)S(1)} %pad_maximum_fusion.1), channel_id=1, source_target_pairs={{0,8},{1,9},{2,10},{3,11},{4,12},{5,13},{6,14},{7,15},{8,0},{9,1},... | collective-permute-start | bytes 909320 | tf_op jit(solution)/shard_map/ppermute | solution.py:160
  35.0 17.4 %collective-permute-start.8 = (f32[2,37,8,128]{3,2,1,0:T(8,128)S(1)}, f32[2,37,8,128]{3,2,1,0:T(8,128)S(1)}, u32[]{:S(2)}, u32[]{:S(2)}) collective-permute-start(f32[2,37,8,128]{3,2,1,0:T(8,128)S(1)} %pad_maximum_fusion.2), channel_id=1, source_target_pairs={{0,5},{1,4},{2,7},{3,6},{4,1},{5,0},{6,3},{7,2},{8,13},{9,12},{10,... | collective-permute-start | bytes 909320 | tf_op jit(solution)/shard_map/ppermute | solution.py:160
  36.4 1.5 %collective-permute-start = (f32[64,8,128]{2,1,0:T(8,128)S(1)}, f32[64,8,128]{2,1,0:T(8,128)S(1)}, u32[]{:S(2)}, u32[]{:S(2)}) collective-permute-start(f32[64,8,128]{2,1,0:T(8,128)S(1)} %get-tuple-element.35), channel_id=1, source_target_pairs={{0,2},{1,3},{2,0},{3,1},{4,6},{5,7},{6,4},{7,5},{8,10},{9,11},{10,... | collective-permute-start | bytes 786440 | tf_op jit(solution)/shard_map/ppermute | solution.py:160
  36.4 16.2 %collective-permute-start.9 = (f32[2,37,8,128]{3,2,1,0:T(8,128)S(1)}, f32[2,37,8,128]{3,2,1,0:T(8,128)S(1)}, u32[]{:S(2)}, u32[]{:S(2)}) collective-permute-start(f32[2,37,8,128]{3,2,1,0:T(8,128)S(1)} %pad_maximum_fusion.3), channel_id=1, source_target_pairs={{0,13},{1,12},{2,15},{3,14},{4,9},{5,8},{6,11},{7,10},{8,5},{9,4},... | collective-permute-start | bytes 909320 | tf_op jit(solution)/shard_map/ppermute | solution.py:160
  38.0 18.2 %collective-permute-start.10 = (f32[2,27,8,128]{3,2,1,0:T(8,128)S(1)}, f32[2,27,8,128]{3,2,1,0:T(8,128)S(1)}, u32[]{:S(2)}, u32[]{:S(2)}) collective-permute-start(f32[2,27,8,128]{3,2,1,0:T(8,128)S(1)} %pad_maximum_fusion.4), channel_id=1, source_target_pairs={{0,8},{1,9},{2,10},{3,11},{4,12},{5,13},{6,14},{7,15},{8,0},{9,1},... | collective-permute-start | bytes 663560 | tf_op jit(solution)/shard_map/ppermute | solution.py:160
  43.4 14.0 %collective-permute-start.11 = (f32[2,27,8,128]{3,2,1,0:T(8,128)S(1)}, f32[2,27,8,128]{3,2,1,0:T(8,128)S(1)}, u32[]{:S(2)}, u32[]{:S(2)}) collective-permute-start(f32[2,27,8,128]{3,2,1,0:T(8,128)S(1)} %pad_maximum_fusion.5), channel_id=1, source_target_pairs={{0,5},{1,4},{2,7},{3,6},{4,1},{5,0},{6,3},{7,2},{8,13},{9,12},{10,... | collective-permute-start | bytes 663560 | tf_op jit(solution)/shard_map/ppermute | solution.py:160
  52.4 11.1 %collective-permute-start.12 = (f32[2,27,8,128]{3,2,1,0:T(8,128)S(1)}, f32[2,27,8,128]{3,2,1,0:T(8,128)S(1)}, u32[]{:S(2)}, u32[]{:S(2)}) collective-permute-start(f32[2,27,8,128]{3,2,1,0:T(8,128)S(1)} %pad_maximum_fusion.6), channel_id=1, source_target_pairs={{0,13},{1,12},{2,15},{3,14},{4,9},{5,8},{6,11},{7,10},{8,5},{9,4},... | collective-permute-start | bytes 663560 | tf_op jit(solution)/shard_map/ppermute | solution.py:160
  53.6 11.7 %collective-permute-start.14 = (f32[38,8,128]{2,1,0:T(8,128)S(1)}, f32[38,8,128]{2,1,0:T(8,128)S(1)}, u32[]{:S(2)}, u32[]{:S(2)}) collective-permute-start(f32[38,8,128]{2,1,0:T(8,128)S(1)} %get-tuple-element.59.mine_ref), channel_id=1, source_target_pairs={{0,16},{1,17},{2,18},{3,19},{4,20},{5,21},{6,22},{7,23},{8,24},{9,... | collective-permute-start | bytes 466952 | tf_op jit(solution)/shard_map/ppermute | solution.py:160
  64.2 6.2 %collective-permute-start.13 = (f32[18,8,128]{2,1,0:T(8,128)S(1)}, f32[18,8,128]{2,1,0:T(8,128)S(1)}, u32[]{:S(2)}, u32[]{:S(2)}) collective-permute-start(f32[18,8,128]{2,1,0:T(8,128)S(1)} %shard_map.79.mine_ref), channel_id=1, source_target_pairs={{0,16},{1,17},{2,18},{3,19},{4,20},{5,21},{6,22},{7,23},{8,24},{9,... | collective-permute-start | bytes 221192 | tf_op jit(solution)/shard_map/ppermute | solution.py:160
  66.6 5.4 %collective-permute-start.16 = (f32[18,8,128]{2,1,0:T(8,128)S(1)}, f32[18,8,128]{2,1,0:T(8,128)S(1)}, u32[]{:S(2)}, u32[]{:S(2)}) collective-permute-start(f32[18,8,128]{2,1,0:T(8,128)S(1)} %get-tuple-element.64.mine_ref), channel_id=1, source_target_pairs={{0,16},{1,17},{2,18},{3,19},{4,20},{5,21},{6,22},{7,23},{8,24},{9,... | collective-permute-start | bytes 221192 | tf_op jit(solution)/shard_map/ppermute | solution.py:160
  71.7 6.1 %collective-permute-start.15 = (f32[18,8,128]{2,1,0:T(8,128)S(1)}, f32[18,8,128]{2,1,0:T(8,128)S(1)}, u32[]{:S(2)}, u32[]{:S(2)}) collective-permute-start(f32[18,8,128]{2,1,0:T(8,128)S(1)} %get-tuple-element.62.mine_ref), channel_id=1, source_target_pairs={{0,16},{1,17},{2,18},{3,19},{4,20},{5,21},{6,22},{7,23},{8,24},{9,... | collective-permute-start | bytes 221192 | tf_op jit(solution)/shard_map/ppermute | solution.py:160

commit v2 on v1

--- a/solution.py
+++ b/solution.py
@@ -190,44 +190,49 @@
     return row, row < size.owned, lax.div(size.owned * mem_index + row, size.levels)
 
 
-def pack_target(size, outs, chip, core):
+def pack_shapes(size, chips):
+    one = (size.all_rows, SUBLANES, LANES)
+    shapes = []
+    for chip in chips:
+        if chip == 0:
+            shapes += [one, one]
+        elif chip in EARLY:
+            shapes.append((CORES, size.all_rows + (chip == 1), SUBLANES, LANES))
+        else:
+            shapes.append(one)
+    return shapes + [(len(LATE), *one)] * (LATE[0] in chips)
+
+
+def pack_target(outs, chips, chip, core):
+    place = chips.index(chip) + (0 in chips[: chips.index(chip)])
     if chip == 0:
-        return outs[core]
+        return outs[place + core]
     if chip in EARLY:
-        return outs[2 + EARLY.index(chip)].at[core]
-    place = LATE.index(chip)
-    return outs[2 + len(EARLY) + place] if core == 0 else outs[-1].at[place]
-
-
-def pack_kernel(size, flat_ref, perturb_hbm, alpha_hbm, innov_hbm, weight_hbm, mask_hbm, near_hbm, *refs):
-    outs, scratch = refs[:-9], refs[-9:]
-    perturb_ref, alpha_ref, innov_ref, weight_ref, mask_ref, near_ref, tiles_ref, plane_sems, sems = scratch
+        return outs[place].at[core]
+    return outs[place] if core == 0 else outs[-1].at[LATE.index(chip)]
+
+
+def pack_kernel(size, chips, flat_ref, perturb_hbm, alpha_hbm, innov_hbm, weight_hbm, mask_hbm, near_hbm, *refs):
+    outs, scratch = refs[:-10], refs[-10:]
+    perturb_ref, alpha_ref, innov_ref, weight_ref, mask_ref, near_ref, tiles_ref, plane_sems, alpha_sems, sems = scratch
     flat = flat_ref[0]
     own = lax.rem(flat, GROUP)
     mem_index = lax.div(flat, 2)
-    step = size.fields
+    places = [(chip, core, chunk) for chip in chips for core in range(CORES) for chunk in range(size.chunks)]
+    levels = [lax.bitwise_xor(own, flat_offset(chip, core)) + chunk * GROUP for chip, core, chunk in places]
     plane_copies = [
-        pltpu.make_async_copy(
-            perturb_hbm.at[pl.ds(part * step, step)], perturb_ref.at[pl.ds(part * step, step)], plane_sems.at[part]
-        )
-        for part in range(size.members)
+        pltpu.make_async_copy(perturb_hbm.at[:, level], perturb_ref.at[place], plane_sems.at[place])
+        for place, level in enumerate(levels)
     ]
-    copies = [
-        pltpu.make_async_copy(source, target, sems.at[place])
-        for place, (source, target) in enumerate(
-            (
-                (mask_hbm, mask_ref),
-                (near_hbm, near_ref),
-                (alpha_hbm, alpha_ref),
-                (innov_hbm, innov_ref),
-                (weight_hbm, weight_ref),
-            )
-        )
+    alpha_copies = [
+        pltpu.make_async_copy(alpha_hbm.at[:, level], alpha_ref.at[place], alpha_sems.at[place])
+        for place, level in enumerate(levels)
     ]
-    for copy in plane_copies + copies:
+    pairs = ((mask_hbm, mask_ref), (near_hbm, near_ref), (innov_hbm, innov_ref), (weight_hbm, weight_ref))
+    copies = [pltpu.make_async_copy(source, target, sems.at[place]) for place, (source, target) in enumerate(pairs)]
+    for copy in plane_copies + copies + alpha_copies:
         copy.start()
     copies[0].wait()
-    copies[1].wait()
     tiles = mask_ref.shape[-1]
     shape = (tiles, tiles * TILE)
     spread_out = lax.broadcasted_iota(jnp.int32, shape, 0) == lax.div(lax.broadcasted_iota(jnp.int32, shape, 1), TILE)
@@ -237,28 +242,23 @@
             mask_ref[slot].astype(jnp.float32), spread_out.astype(jnp.float32), preferred_element_type=jnp.float32
         )
         tiles_ref[slot] = jnp.where(line < TILE, cells[:, :LANES], cells[:, LANES:])
-    coef_out = outs[2 + EARLY.index(1)]
-    coef_out[0, size.all_rows] = near_ref[0]
-    coef_out[1, size.all_rows] = near_ref[1]
-    places = [(chip, core, chunk) for chip in range(CHIPS) for core in range(CORES) for chunk in range(size.chunks)]
-
-    def level_of(chip, core, chunk):
-        return lax.bitwise_xor(own, flat_offset(chip, core)) + chunk * GROUP
-
-    for part in range(size.members):
-        plane_copies[part].wait()
-        for chip, core, chunk in places:
-            planes = perturb_ref[part * step : (part + 1) * step, level_of(chip, core, chunk)]
-            base = size.planes_at(chunk) + part * step
-            pack_target(size, outs, chip, core)[base : base + step] = planes.astype(jnp.float32)
-    for copy in copies[2:]:
-        copy.wait()
-    for chip, core, chunk in places:
-        out = pack_target(size, outs, chip, core)
-        level = level_of(chip, core, chunk)
+    copies[1].wait()
+    if 1 in chips:
+        coef_out = outs[chips.index(1)]
+        coef_out[0, size.all_rows] = near_ref[0]
+        coef_out[1, size.all_rows] = near_ref[1]
+    for place, (chip, core, chunk) in enumerate(places):
+        plane_copies[place].wait()
+        base = size.planes_at(chunk)
+        pack_target(outs, chips, chip, core)[base : base + size.planes] = perturb_ref[place].astype(jnp.float32)
+    copies[2].wait()
+    copies[3].wait()
+    for place, (chip, core, chunk) in enumerate(places):
+        out = pack_target(outs, chips, chip, core)
         base = size.extras_at(chunk)
-        out[base : base + size.members] = alpha_ref[:, level]
-        row, inside, field = row_in_block(size, level, mem_index)
+        alpha_copies[place].wait()
+        out[base : base + size.members] = alpha_ref[place]
+        row, inside, field = row_in_block(size, levels[place], mem_index)
         row = jnp.minimum(row, size.owned - 1)
         slot = jnp.minimum(lax.div(field, size.vars), size.slots - 1)
         kept = jnp.where(inside, 1.0, 0.0).astype(jnp.float32)
@@ -539,36 +539,42 @@
 
 
 def spread_levels(size, flat, near, perturb, alpha_init, innovation, obs_weight, obs_mask):
-    levels = size.levels
     block = (SUBLANES, LANES)
-    one = (size.all_rows, *block)
-    early_shapes = [(CORES, size.all_rows + (chip == 1), *block) for chip in EARLY]
-    packed = call(
-        functools.partial(pack_kernel, size),
-        [one, one] + early_shapes + [one] * len(LATE) + [(len(LATE), *one)],
-        (
-            flat,
-            fold(perturb).reshape(size.planes, levels, *block),
-            fold(alpha_init),
-            fold(innovation),
-            fold(obs_weight),
-            obs_mask,
-            near,
-        ),
-        [
-            pltpu.VMEM((size.planes, levels, *block), jnp.bfloat16),
-            pltpu.VMEM((size.members, levels, *block), jnp.float32),
-            pltpu.VMEM((size.owned, *block), jnp.float32),
-            pltpu.VMEM((size.owned, *block), jnp.float32),
-            pltpu.VMEM(obs_mask.shape, jnp.int32),
-            pltpu.VMEM(near.shape, jnp.float32),
-            pltpu.VMEM((size.slots, *block), jnp.float32),
-            pltpu.SemaphoreType.DMA((size.members,)),
-            pltpu.SemaphoreType.DMA((5,)),
-        ],
-        [pltpu.SMEM] + [pltpu.HBM] * 6,
+    operands = (
+        fold(perturb).reshape(size.planes, size.levels, *block),
+        fold(alpha_init),
+        fold(innovation),
+        fold(obs_weight),
+        obs_mask,
+        near,
     )
-    kept, early, late, late_out = packed[:2], packed[2:6], packed[6:9], packed[9]
+
+    def pack(chips, flat):
+        count = len(chips) * CORES * size.chunks
+        return call(
+            functools.partial(pack_kernel, size, chips),
+            pack_shapes(size, chips),
+            (flat,) + operands,
+            [
+                pltpu.VMEM((count, size.planes, *block), jnp.bfloat16),
+                pltpu.VMEM((count, size.members, *block), jnp.float32),
+                pltpu.VMEM((size.owned, *block), jnp.float32),
+                pltpu.VMEM((size.owned, *block), jnp.float32),
+                pltpu.VMEM(obs_mask.shape, jnp.int32),
+                pltpu.VMEM(near.shape, jnp.float32),
+                pltpu.VMEM((size.slots, *block), jnp.float32),
+                pltpu.SemaphoreType.DMA((count,)),
+                pltpu.SemaphoreType.DMA((count,)),
+                pltpu.SemaphoreType.DMA((4,)),
+            ],
+            [pltpu.SMEM] + [pltpu.HBM] * 6,
+        )
+
+    early = list(pack(EARLY[:2], flat))
+    flat, early[0], early[1] = lax.optimization_barrier((flat, early[0], early[1]))
+    packed = pack(EARLY[2:] + (0,) + LATE, flat)
+    early += packed[:2]
+    kept, late, late_out = packed[2:4], packed[4:7], packed[7]
     crossed = shift_by(CORES, late_out)
     own_crossed = shift_by(CORES, kept[1])
     got = [shift_by(flat_offset(chip, 0), cells) for chip, cells in zip(EARLY, early)]
@@ -578,10 +584,15 @@
         rows = slice(base, base + (size.planes if chunk else size.lead_rows))
         parts = [jnp.stack([cells[rows], crossed[place, rows]]) for place, cells in enumerate(late)]
         if chunk == 0:
-            got[0], got[1], parts[0], parts[1] = lax.optimization_barrier((got[0], got[1], parts[0], parts[1]))
-            got[2], got[3], parts[2] = lax.optimization_barrier((got[2], got[3], parts[2]))
+            got[1], parts[0] = lax.optimization_barrier((got[1], parts[0]))
+            got[2], parts[1] = lax.optimization_barrier((got[2], parts[1]))
+            got[0], got[3], parts[2] = lax.optimization_barrier((got[0], got[3], parts[2]))
         else:
-            got[0], got[1], got[2], got[3], *parts = lax.optimization_barrier((*got, *parts))
+            prev = list(got_late[chunk - 1])
+            prev[0], parts[0] = lax.optimization_barrier((prev[0], parts[0]))
+            prev[1], parts[1] = lax.optimization_barrier((prev[1], parts[1]))
+            prev[2], parts[2] = lax.optimization_barrier((prev[2], parts[2]))
+            got_late[chunk - 1] = tuple(prev)
         got_late.append(tuple(shift_by(flat_offset(chip, 0), cells) for chip, cells in zip(LATE, parts)))
     early_crossed = shift_by(CORES, jnp.stack([cells[1, : size.all_rows] for cells in got]))
     shared = (kept[0], own_crossed, *got, early_crossed)

time: 93.9 us -> 89.9 us (0.957)
  waiting for transfers between devices: 49.7 us -> 43.1 us
  Pallas kernels: 9.02 us -> 11 us
  starting transfers between devices: 19.6 us -> 21.5 us
  blocking collectives: 14.1 us -> 12.7 us
    ppermute x17, waiting for transfers between devices: 49.7 us -> 43.1 us  [shift_by(): return lax.ppermute(cells, axes, [(i, i ^ mask) for i in range(count)])]
    pallas_call x8 -> x9, Pallas kernels: 9.02 us -> 11 us  [call(): pl.pallas_call(kernel, out_shape=[jax.ShapeDtypeStruct(shape, jnp.float32...]
    ppermute x17, starting transfers between devices: 19.6 us -> 21.5 us  [shift_by(): return lax.ppermute(cells, axes, [(i, i ^ mask) for i in range(count)])]
    all_to_all x1, blocking collectives: 14.1 us -> 12.7 us  [level_shards(): lax.all_to_all(back, ('mem', 'lat'), 0, 0, axis_index_groups=groups, tile...]
  transfers between devices with their start and end apart: 17 -> 17, of which waited for: 11 -> 10; matrix products, arithmetic and copies ran while one was open for 0% -> 0% of each run, Pallas kernels for 6% -> 9%
where the time goes in v2:
time: 89.9 us; the launch traced here: 89.6 us
  waiting for transfers between devices  43.1 us (48%)
  starting transfers between devices  21.5 us (24%)
  blocking collectives  12.7 us (14%)
  Pallas kernels  11 us (12%)
    ppermute x17, waiting for transfers between devices, shift_by(): return lax.ppermute(cells, axes, [(i, i ^ mask) for i in range(count)])  43.1 us
    ppermute x17, starting transfers between devices, shift_by(): return lax.ppermute(cells, axes, [(i, i ^ mask) for i in range(count)])  21.5 us
    all_to_all x1, blocking collectives, level_shards(): lax.all_to_all(back, ('mem', 'lat'), 0, 0, axis_index_groups=groups, tile...  12.7 us
    pallas_call x9, Pallas kernels, call(): pl.pallas_call(kernel, out_shape=[jax.ShapeDtypeStruct(shape, jnp.float32...  11 us
  transfers between devices with their start and end apart: 17, of which 10 were waited for; matrix products, arithmetic and copies ran while one was open for 0% of the time, Pallas kernels for 9%

profile of v2, /device:TPU:0, one launch (start us, length us, event | category | flops | bytes accessed | tf_op | source)
XLA Modules:
  0.0 89.6 jit_solution(1487907449671093475)
XLA Ops:
  0.6 1.5 %shard_map.77 = (f32[2,65,8,128]{3,2,1,0:T(8,128)S(1)}, f32[2,64,8,128]{3,2,1,0:T(8,128)S(1)}) custom-call(s32[1]{0:T(128)} %bitcast.flat_ref, bf16[27,32,8,128]{3,2,1,0:T(8,128)(2,1)} %bitcast.46, f32[3,32,8,128]{3,2,1,0:T(8,128)} %bitcast.48, f32[18,8,128]{2,1,0:T(8,128)} %bitcast.50, f32[18,8,128]{2,1,0:T(8,128)} %bitcast.52, s32[3,1,64]{2,1,0:T(1,128)} %mask_hbm.3, ...), custom_call_target="tpu_custom_call" | custom-call | flops 3375876 | bytes 3375876 | tf_op jit(solution)/shard_map/pallas_call | solution.py:526
  2.2 4.0 %collective-permute-start.4 = (f32[2,64,8,128]{3,2,1,0:T(8,128)S(1)}, f32[2,64,8,128]{3,2,1,0:T(8,128)S(1)}, u32[]{:S(2)}, u32[]{:S(2)}) collective-permute-start(f32[2,64,8,128]{3,2,1,0:T(8,128)S(1)} %get-tuple-element.46), channel_id=1, source_target_pairs={{0,12},{1,13},{2,14},{3,15},{4,8},{5,9},{6,10},{7,11},{8,4},{9,5},... | collective-permute-start | bytes 1572872 | tf_op jit(solution)/shard_map/ppermute | solution.py:160
  6.2 1.5 %collective-permute-start.1 = (f32[2,65,8,128]{3,2,1,0:T(8,128)S(1)}, f32[2,65,8,128]{3,2,1,0:T(8,128)S(1)}, u32[]{:S(2)}, u32[]{:S(2)}) collective-permute-start(f32[2,65,8,128]{3,2,1,0:T(8,128)S(1)} %get-tuple-element.41), channel_id=1, source_target_pairs={{0,1},{1,0},{2,3},{3,2},{4,5},{5,4},{6,7},{7,6},{8,9},{9,8},{10,11... | collective-permute-start | bytes 1597448 | tf_op jit(solution)/shard_map/ppermute | solution.py:160
  7.7 2.6 %shard_map.78 = (f32[2,64,8,128]{3,2,1,0:T(8,128)S(1)}, f32[2,64,8,128]{3,2,1,0:T(8,128)S(1)}, f32[64,8,128]{2,1,0:T(8,128)S(1)}, f32[64,8,128]{2,1,0:T(8,128)S(...) custom-call(s32[1]{0:T(128)} %bitcast.flat_ref, ...), custom_call_target="tpu_custom_call" | custom-call | flops 5464836 | bytes 5464836 | tf_op jit(solution)/shard_map/pallas_call | solution.py:526
  10.3 0.1 collective-permute-start
  10.4 0.6 collective-permute-start.5
  11.0 0.2 collective-permute-start.3
  11.2 2.0 %collective-permute-done.3 = f32[3,64,8,128]{3,2,1,0:T(8,128)S(1)} collective-permute-done((f32[3,64,8,128]{3,2,1,0:T(8,128)S(1)}, f32[3,64,8,128]{3,2,1,0:T(8,128)S(1)}, u32[]{:S(2)}, u32[]{:S(2)}) %collective-permute-start.3) | collective-permute-done | bytes 786464 | tf_op jit(solution)/shard_map/ppermute | solution.py:160
  13.3 0.2 collective-permute-start.2
  13.5 15.9 %collective-permute-done.5.refs_4_.refs_5_ = f32[2,64,8,128]{3,2,1,0:T(8,128)S(1)} collective-permute-done((f32[2,64,8,128]{3,2,1,0:T(8,128)S(1)}, f32[2,64,8,128]{3,2,1,0:T(8,128)S(1)}, u32[]{:S(2)}, u32[]{:S(2)}) %collective-permute-start.5) | collective-permute-done | bytes 524320 | tf_op jit(solution)/shard_map/ppermute | solution.py:160
  29.4 0.0 collective-permute-done.4.refs_3_.refs_4_
  29.4 1.2 %collective-permute-done.2.refs_5_.refs_6_ = f32[2,64,8,128]{3,2,1,0:T(8,128)S(1)} collective-permute-done((f32[2,64,8,128]{3,2,1,0:T(8,128)S(1)}, f32[2,64,8,128]{3,2,1,0:T(8,128)S(1)}, u32[]{:S(2)}, u32[]{:S(2)}) %collective-permute-start.2) | collective-permute-done | bytes 524320 | tf_op jit(solution)/shard_map/ppermute | solution.py:160
  30.6 0.4 collective-permute-done.1.refs_2_.refs_3_
  31.1 0.0 copy-start
  31.1 0.1 pad_maximum_fusion
  31.2 0.1 collective-permute-start.6
  31.3 2.2 %collective-permute-start.9 = (f32[2,37,8,128]{3,2,1,0:T(8,128)S(1)}, f32[2,37,8,128]{3,2,1,0:T(8,128)S(1)}, u32[]{:S(2)}, u32[]{:S(2)}) collective-permute-start(f32[2,37,8,128]{3,2,1,0:T(8,128)S(1)} %pad_maximum_fusion.1), channel_id=1, source_target_pairs={{0,13},{1,12},{2,15},{3,14},{4,9},{5,8},{6,11},{7,10},{8,5},{9,4},... | collective-permute-start | bytes 909320 | tf_op jit(solution)/shard_map/ppermute | solution.py:160
  33.5 0.9 collective-permute-start.7
  34.3 1.4 %collective-permute-start.8 = (f32[2,37,8,128]{3,2,1,0:T(8,128)S(1)}, f32[2,37,8,128]{3,2,1,0:T(8,128)S(1)}, u32[]{:S(2)}, u32[]{:S(2)}) collective-permute-start(f32[2,37,8,128]{3,2,1,0:T(8,128)S(1)} %pad_maximum_fusion.3), channel_id=1, source_target_pairs={{0,5},{1,4},{2,7},{3,6},{4,1},{5,0},{6,3},{7,2},{8,13},{9,12},{10,... | collective-permute-start | bytes 909320 | tf_op jit(solution)/shard_map/ppermute | solution.py:160
  35.9 7.3 %collective-permute-done.9.refs_9_.refs_10_ = f32[2,37,8,128]{3,2,1,0:T(8,128)S(1)} collective-permute-done((f32[2,37,8,128]{3,2,1,0:T(8,128)S(1)}, f32[2,37,8,128]{3,2,1,0:T(8,128)S(1)}, u32[]{:S(2)}, u32[]{:S(2)}) %collective-permute-start.9) | collective-permute-done | bytes 303136 | tf_op jit(solution)/shard_map/ppermute | solution.py:160
  43.2 2.1 %collective-permute-start.12 = (f32[2,27,8,128]{3,2,1,0:T(8,128)S(1)}, f32[2,27,8,128]{3,2,1,0:T(8,128)S(1)}, u32[]{:S(2)}, u32[]{:S(2)}) collective-permute-start(f32[2,27,8,128]{3,2,1,0:T(8,128)S(1)} %pad_maximum_fusion.6), channel_id=1, source_target_pairs={{0,13},{1,12},{2,15},{3,14},{4,9},{5,8},{6,11},{7,10},{8,5},{9,4},... | collective-permute-start | bytes 663560 | tf_op jit(solution)/shard_map/ppermute | solution.py:160
  45.3 3.5 %collective-permute-done.7.refs_7_.refs_8_ = f32[2,37,8,128]{3,2,1,0:T(8,128)S(1)} collective-permute-done((f32[2,37,8,128]{3,2,1,0:T(8,128)S(1)}, f32[2,37,8,128]{3,2,1,0:T(8,128)S(1)}, u32[]{:S(2)}, u32[]{:S(2)}) %collective-permute-start.7) | collective-permute-done | bytes 303136 | tf_op jit(solution)/shard_map/ppermute | solution.py:160
  48.8 1.2 %collective-permute-start.10 = (f32[2,27,8,128]{3,2,1,0:T(8,128)S(1)}, f32[2,27,8,128]{3,2,1,0:T(8,128)S(1)}, u32[]{:S(2)}, u32[]{:S(2)}) collective-permute-start(f32[2,27,8,128]{3,2,1,0:T(8,128)S(1)} %pad_maximum_fusion.4), channel_id=1, source_target_pairs={{0,8},{1,9},{2,10},{3,11},{4,12},{5,13},{6,14},{7,15},{8,0},{9,1},... | collective-permute-start | bytes 663560 | tf_op jit(solution)/shard_map/ppermute | solution.py:160
  50.0 0.0 collective-permute-done.8.refs_8_.refs_9_
  50.0 1.4 %collective-permute-start.11 = (f32[2,27,8,128]{3,2,1,0:T(8,128)S(1)}, f32[2,27,8,128]{3,2,1,0:T(8,128)S(1)}, u32[]{:S(2)}, u32[]{:S(2)}) collective-permute-start(f32[2,27,8,128]{3,2,1,0:T(8,128)S(1)} %pad_maximum_fusion.5), channel_id=1, source_target_pairs={{0,5},{1,4},{2,7},{3,6},{4,1},{5,0},{6,3},{7,2},{8,13},{9,12},{10,... | collective-permute-start | bytes 663560 | tf_op jit(solution)/shard_map/ppermute | solution.py:160
  51.4 0.0 collective-permute-done.refs_1_.refs_2_
  51.4 0.0 collective-permute-done.6.refs_6_.refs_7_
  51.4 0.0 copy-done
  51.4 0.9 %shard_map.79 = (f32[38,8,128]{2,1,0:T(8,128)S(1)}, f32[2,9,2,8,128]{4,3,2,1,0:T(8,128)S(1)}, f32[2,9,2,8,128]{4,3,2,1,0:T(8,128)S(1)}) custom-call(s32[1]{0:T(128)} %bitcast.flat_ref, f32[2,8,128]{2,1,0:T(8,128)S(1)} %bitcast.40, f32[64,8,128]{2,1,0:T(8,128)S(1)} %get-tuple-element.39.refs_0_.refs_1_, ...), custom_call_target="tpu_custom_call" | custom-call | flops 5046276 | bytes 5046276 | tf_op jit(solution)/shard_map/pallas_call | solution.py:526
  52.3 2.6 %collective-permute-start.14 = (f32[38,8,128]{2,1,0:T(8,128)S(1)}, f32[38,8,128]{2,1,0:T(8,128)S(1)}, u32[]{:S(2)}, u32[]{:S(2)}) collective-permute-start(f32[38,8,128]{2,1,0:T(8,128)S(1)} %get-tuple-element.63.mine_ref), channel_id=1, source_target_pairs={{0,16},{1,17},{2,18},{3,19},{4,20},{5,21},{6,22},{7,23},{8,24},{9,... | collective-permute-start | bytes 466952 | tf_op jit(solution)/shard_map/ppermute | solution.py:160
  55.0 0.0 collective-permute-done.12.refs_13_.refs_12_
  55.0 6.3 %collective-permute-done.10.refs_11_.refs_10_ = f32[2,27,8,128]{3,2,1,0:T(8,128)S(1)} collective-permute-done((f32[2,27,8,128]{3,2,1,0:T(8,128)S(1)}, f32[2,27,8,128]{3,2,1,0:T(8,128)S(1)}, u32[]{:S(2)}, u32[]{:S(2)}) %collective-permute-start.10) | collective-permute-done | bytes 221216 | tf_op jit(solution)/shard_map/ppermute | solution.py:160
  61.2 0.0 collective-permute-done.11.refs_12_.refs_11_
  61.2 0.7 shard_map.80.mine_ref
  62.0 0.4 collective-permute-start.13
  62.4 0.0 collective-permute-done.14.theirs_ref
  62.4 1.4 %shard_map.81 = (f32[18,8,128]{2,1,0:T(8,128)S(1)}, f32[4,2,6,8,128]{4,3,2,1,0:T(8,128)S(1)}, f32[2,9,2,8,128]{4,3,2,1,0:T(8,128)S(1)}) custom-call(s32[1]{0:T(128)} %bitcast.flat_ref, f32[2,8,128]{2,1,0:T(8,128)S(1)} %bitcast.42, f32[38,8,128]{2,1,0:T(8,128)S(1)} %get-tuple-element.63.mine_ref, f32[38,8,128]{2,1,0:T(8,128)S(1)} %collective-permute-done.14.theirs_ref, ...), custom_call_target="tpu_custom_call" | custom-call | flops 5619716 | bytes 5619716 | tf_op jit(solution)/shard_map/pallas_call | solution.py:526
  63.8 2.7 %collective-permute-start.16 = (f32[18,8,128]{2,1,0:T(8,128)S(1)}, f32[18,8,128]{2,1,0:T(8,128)S(1)}, u32[]{:S(2)}, u32[]{:S(2)}) collective-permute-start(f32[18,8,128]{2,1,0:T(8,128)S(1)} %get-tuple-element.68.mine_ref), channel_id=1, source_target_pairs={{0,16},{1,17},{2,18},{3,19},{4,20},{5,21},{6,22},{7,23},{8,24},{9,... | collective-permute-start | bytes 221192 | tf_op jit(solution)/shard_map/ppermute | solution.py:160
  66.5 1.7 %collective-permute-done.13.theirs_ref = f32[18,8,128]{2,1,0:T(8,128)S(1)} collective-permute-done((f32[18,8,128]{2,1,0:T(8,128)S(1)}, f32[18,8,128]{2,1,0:T(8,128)S(1)}, u32[]{:S(2)}, u32[]{:S(2)}) %collective-permute-start.13) | collective-permute-done | bytes 73760 | tf_op jit(solution)/shard_map/ppermute | solution.py:160
  68.2 1.4 %shard_map.82 = (f32[18,8,128]{2,1,0:T(8,128)S(1)}, f32[4,2,6,8,128]{4,3,2,1,0:T(8,128)S(1)}) custom-call(s32[1]{0:T(128)} %bitcast.flat_ref, f32[2,8,128]{2,1,0:T(8,128)S(1)} %bitcast.43, f32[18,8,128]{2,1,0:T(8,128)S(1)} %shard_map.80.mine_ref, f32[18,8,128]{2,1,0:T(8,128)S(1)} %collective-permute-done.13.theirs_ref, ...), custom_call_target="tpu_custom_call" | custom-call | flops 5971972 | bytes 5971972 | tf_op jit(solution)/shard_map/pallas_call | solution.py:526
  69.6 0.1 collective-permute-start.15
  69.6 0.7 collective-permute-done.16.theirs_ref
  70.3 0.7 shard_map.83.refs_0_
  71.1 4.0 %collective-permute-done.15.theirs_ref = f32[18,8,128]{2,1,0:T(8,128)S(1)} collective-permute-done((f32[18,8,128]{2,1,0:T(8,128)S(1)}, f32[18,8,128]{2,1,0:T(8,128)S(1)}, u32[]{:S(2)}, u32[]{:S(2)}) %collective-permute-start.15) | collective-permute-done | bytes 73760 | tf_op jit(solution)/shard_map/ppermute | solution.py:160
  75.1 0.8 shard_map.84
  75.9 12.7 %all_to_all.5.back_ref = f32[16,8,8,128]{3,2,1,0:T(8,128)S(1)} all-to-all(f32[16,8,8,128]{3,2,1,0:T(8,128)S(1)} %shard_map.84), channel_id=1, replica_groups={{0,1,2,3,4,5,6,7,8,9,10,11,12,13,14,15},{16,17,18,19,20,21,22,23,24,25,..., dimensions={0} | all-to-all | bytes 1048576 | tf_op jit(solution)/shard_map/all_to_all | solution.py:637
  88.6 1.0 %shard_map.85 = (f32[3,32,4,256]{3,2,1,0:T(4,128)}, f32[18,4,256]{2,1,0:T(4,128)}) custom-call(s32[1]{0:T(128)} %bitcast.flat_ref, f32[16,8,8,128]{3,2,1,0:T(8,128)S(1)} %all_to_all.5.back_ref), custom_call_target="tpu_custom_call" | custom-call | flops 991236 | bytes 991236 | tf_op jit(solution)/shard_map/pallas_call | solution.py:526
  (18 shorter events, 0.3 us)
Async XLA Ops:
  2.2 27.2 %collective-permute-start.4 = (f32[2,64,8,128]{3,2,1,0:T(8,128)S(1)}, f32[2,64,8,128]{3,2,1,0:T(8,128)S(1)}, u32[]{:S(2)}, u32[]{:S(2)}) collective-permute-start(f32[2,64,8,128]{3,2,1,0:T(8,128)S(1)} %get-tuple-element.46), channel_id=1, source_target_pairs={{0,12},{1,13},{2,14},{3,15},{4,8},{5,9},{6,10},{7,11},{8,4},{9,5},... | collective-permute-start | bytes 1572872 | tf_op jit(solution)/shard_map/ppermute | solution.py:160
  6.2 24.8 %collective-permute-start.1 = (f32[2,65,8,128]{3,2,1,0:T(8,128)S(1)}, f32[2,65,8,128]{3,2,1,0:T(8,128)S(1)}, u32[]{:S(2)}, u32[]{:S(2)}) collective-permute-start(f32[2,65,8,128]{3,2,1,0:T(8,128)S(1)} %get-tuple-element.41), channel_id=1, source_target_pairs={{0,1},{1,0},{2,3},{3,2},{4,5},{5,4},{6,7},{7,6},{8,9},{9,8},{10,11... | collective-permute-start | bytes 1597448 | tf_op jit(solution)/shard_map/ppermute | solution.py:160
  10.3 41.1 %collective-permute-start = (f32[64,8,128]{2,1,0:T(8,128)S(1)}, f32[64,8,128]{2,1,0:T(8,128)S(1)}, u32[]{:S(2)}, u32[]{:S(2)}) collective-permute-start(f32[64,8,128]{2,1,0:T(8,128)S(1)} %get-tuple-element.40), channel_id=1, source_target_pairs={{0,2},{1,3},{2,0},{3,1},{4,6},{5,7},{6,4},{7,5},{8,10},{9,11},{10,... | collective-permute-start | bytes 786440 | tf_op jit(solution)/shard_map/ppermute | solution.py:160
  10.4 19.0 %collective-permute-start.5 = (f32[2,64,8,128]{3,2,1,0:T(8,128)S(1)}, f32[2,64,8,128]{3,2,1,0:T(8,128)S(1)}, u32[]{:S(2)}, u32[]{:S(2)}) collective-permute-start(f32[2,64,8,128]{3,2,1,0:T(8,128)S(1)} %get-tuple-element.49), channel_id=1, source_target_pairs={{0,4},{1,5},{2,6},{3,7},{4,0},{5,1},{6,2},{7,3},{8,12},{9,13},{10,... | collective-permute-start | bytes 1572872 | tf_op jit(solution)/shard_map/ppermute | solution.py:160
  11.0 2.3 %collective-permute-start.3 = (f32[3,64,8,128]{3,2,1,0:T(8,128)S(1)}, f32[3,64,8,128]{3,2,1,0:T(8,128)S(1)}, u32[]{:S(2)}, u32[]{:S(2)}) collective-permute-start(f32[3,64,8,128]{3,2,1,0:T(8,128)S(1)} %get-tuple-element.44), channel_id=1, source_target_pairs={{0,2},{1,3},{2,0},{3,1},{4,6},{5,7},{6,4},{7,5},{8,10},{9,11},{10,... | collective-permute-start | bytes 2359304 | tf_op jit(solution)/shard_map/ppermute | solution.py:160
  13.3 17.4 %collective-permute-start.2 = (f32[2,64,8,128]{3,2,1,0:T(8,128)S(1)}, f32[2,64,8,128]{3,2,1,0:T(8,128)S(1)}, u32[]{:S(2)}, u32[]{:S(2)}) collective-permute-start(f32[2,64,8,128]{3,2,1,0:T(8,128)S(1)} %get-tuple-element.42), channel_id=1, source_target_pairs={{0,9},{1,8},{2,11},{3,10},{4,13},{5,12},{6,15},{7,14},{8,1},{9,0},... | collective-permute-start | bytes 1572872 | tf_op jit(solution)/shard_map/ppermute | solution.py:160
  31.1 20.3 %copy-start = (f32[2,4,256]{2,1,0:T(4,128)S(1)}, f32[2,4,256]{2,1,0:T(4,128)}, u32[]{:S(2)}) copy-start(f32[2,4,256]{2,1,0:T(4,128)} %param.10) | copy-start | bytes 24580
  31.2 20.2 %collective-permute-start.6 = (f32[4,64,8,128]{3,2,1,0:T(8,128)S(1)}, f32[4,64,8,128]{3,2,1,0:T(8,128)S(1)}, u32[]{:S(2)}, u32[]{:S(2)}) collective-permute-start(f32[4,64,8,128]{3,2,1,0:T(8,128)S(1)} %pad_maximum_fusion), channel_id=1, source_target_pairs={{0,2},{1,3},{2,0},{3,1},{4,6},{5,7},{6,4},{7,5},{8,10},{9,11},{10,... | collective-permute-start | bytes 3145736 | tf_op jit(solution)/shard_map/ppermute | solution.py:160
  31.3 11.9 %collective-permute-start.9 = (f32[2,37,8,128]{3,2,1,0:T(8,128)S(1)}, f32[2,37,8,128]{3,2,1,0:T(8,128)S(1)}, u32[]{:S(2)}, u32[]{:S(2)}) collective-permute-start(f32[2,37,8,128]{3,2,1,0:T(8,128)S(1)} %pad_maximum_fusion.1), channel_id=1, source_target_pairs={{0,13},{1,12},{2,15},{3,14},{4,9},{5,8},{6,11},{7,10},{8,5},{9,4},... | collective-permute-start | bytes 909320 | tf_op jit(solution)/shard_map/ppermute | solution.py:160
  33.5 15.3 %collective-permute-start.7 = (f32[2,37,8,128]{3,2,1,0:T(8,128)S(1)}, f32[2,37,8,128]{3,2,1,0:T(8,128)S(1)}, u32[]{:S(2)}, u32[]{:S(2)}) collective-permute-start(f32[2,37,8,128]{3,2,1,0:T(8,128)S(1)} %pad_maximum_fusion.2), channel_id=1, source_target_pairs={{0,8},{1,9},{2,10},{3,11},{4,12},{5,13},{6,14},{7,15},{8,0},{9,1},... | collective-permute-start | bytes 909320 | tf_op jit(solution)/shard_map/ppermute | solution.py:160
  34.3 15.7 %collective-permute-start.8 = (f32[2,37,8,128]{3,2,1,0:T(8,128)S(1)}, f32[2,37,8,128]{3,2,1,0:T(8,128)S(1)}, u32[]{:S(2)}, u32[]{:S(2)}) collective-permute-start(f32[2,37,8,128]{3,2,1,0:T(8,128)S(1)} %pad_maximum_fusion.3), channel_id=1, source_target_pairs={{0,5},{1,4},{2,7},{3,6},{4,1},{5,0},{6,3},{7,2},{8,13},{9,12},{10,... | collective-permute-start | bytes 909320 | tf_op jit(solution)/shard_map/ppermute | solution.py:160
  43.2 11.8 %collective-permute-start.12 = (f32[2,27,8,128]{3,2,1,0:T(8,128)S(1)}, f32[2,27,8,128]{3,2,1,0:T(8,128)S(1)}, u32[]{:S(2)}, u32[]{:S(2)}) collective-permute-start(f32[2,27,8,128]{3,2,1,0:T(8,128)S(1)} %pad_maximum_fusion.6), channel_id=1, source_target_pairs={{0,13},{1,12},{2,15},{3,14},{4,9},{5,8},{6,11},{7,10},{8,5},{9,4},... | collective-permute-start | bytes 663560 | tf_op jit(solution)/shard_map/ppermute | solution.py:160
  48.8 12.4 %collective-permute-start.10 = (f32[2,27,8,128]{3,2,1,0:T(8,128)S(1)}, f32[2,27,8,128]{3,2,1,0:T(8,128)S(1)}, u32[]{:S(2)}, u32[]{:S(2)}) collective-permute-start(f32[2,27,8,128]{3,2,1,0:T(8,128)S(1)} %pad_maximum_fusion.4), channel_id=1, source_target_pairs={{0,8},{1,9},{2,10},{3,11},{4,12},{5,13},{6,14},{7,15},{8,0},{9,1},... | collective-permute-start | bytes 663560 | tf_op jit(solution)/shard_map/ppermute | solution.py:160
  50.0 11.2 %collective-permute-start.11 = (f32[2,27,8,128]{3,2,1,0:T(8,128)S(1)}, f32[2,27,8,128]{3,2,1,0:T(8,128)S(1)}, u32[]{:S(2)}, u32[]{:S(2)}) collective-permute-start(f32[2,27,8,128]{3,2,1,0:T(8,128)S(1)} %pad_maximum_fusion.5), channel_id=1, source_target_pairs={{0,5},{1,4},{2,7},{3,6},{4,1},{5,0},{6,3},{7,2},{8,13},{9,12},{10,... | collective-permute-start | bytes 663560 | tf_op jit(solution)/shard_map/ppermute | solution.py:160
  52.3 10.0 %collective-permute-start.14 = (f32[38,8,128]{2,1,0:T(8,128)S(1)}, f32[38,8,128]{2,1,0:T(8,128)S(1)}, u32[]{:S(2)}, u32[]{:S(2)}) collective-permute-start(f32[38,8,128]{2,1,0:T(8,128)S(1)} %get-tuple-element.63.mine_ref), channel_id=1, source_target_pairs={{0,16},{1,17},{2,18},{3,19},{4,20},{5,21},{6,22},{7,23},{8,24},{9,... | collective-permute-start | bytes 466952 | tf_op jit(solution)/shard_map/ppermute | solution.py:160
  62.0 6.2 %collective-permute-start.13 = (f32[18,8,128]{2,1,0:T(8,128)S(1)}, f32[18,8,128]{2,1,0:T(8,128)S(1)}, u32[]{:S(2)}, u32[]{:S(2)}) collective-permute-start(f32[18,8,128]{2,1,0:T(8,128)S(1)} %shard_map.80.mine_ref), channel_id=1, source_target_pairs={{0,16},{1,17},{2,18},{3,19},{4,20},{5,21},{6,22},{7,23},{8,24},{9,... | collective-permute-start | bytes 221192 | tf_op jit(solution)/shard_map/ppermute | solution.py:160
  63.8 6.5 %collective-permute-start.16 = (f32[18,8,128]{2,1,0:T(8,128)S(1)}, f32[18,8,128]{2,1,0:T(8,128)S(1)}, u32[]{:S(2)}, u32[]{:S(2)}) collective-permute-start(f32[18,8,128]{2,1,0:T(8,128)S(1)} %get-tuple-element.68.mine_ref), channel_id=1, source_target_pairs={{0,16},{1,17},{2,18},{3,19},{4,20},{5,21},{6,22},{7,23},{8,24},{9,... | collective-permute-start | bytes 221192 | tf_op jit(solution)/shard_map/ppermute | solution.py:160
  69.6 5.6 %collective-permute-start.15 = (f32[18,8,128]{2,1,0:T(8,128)S(1)}, f32[18,8,128]{2,1,0:T(8,128)S(1)}, u32[]{:S(2)}, u32[]{:S(2)}) collective-permute-start(f32[18,8,128]{2,1,0:T(8,128)S(1)} %get-tuple-element.66.mine_ref), channel_id=1, source_target_pairs={{0,16},{1,17},{2,18},{3,19},{4,20},{5,21},{6,22},{7,23},{8,24},{9,... | collective-permute-start | bytes 221192 | tf_op jit(solution)/shard_map/ppermute | solution.py:160

commit v3 on v2

--- a/solution.py
+++ b/solution.py
@@ -351,15 +351,18 @@
     return near, far
 
 
+def add_chip(size, pieces, chip, spread, sums):
+    for core in range(CORES):
+        for field in range(size.fields):
+            for member in range(size.members):
+                plane = pieces.plane(chip, core, field * size.members + member)
+                term = plane * spread[core * size.members + member]
+                sums[field] = term if sums[field] is None else sums[field] + term
+
+
 def add_products(size, pieces, pair, spread, sums):
     for half in range(2):
-        for core in range(CORES):
-            for field in range(size.fields):
-                for member in range(size.members):
-                    plane = pieces.plane(2 * pair + half, core, field * size.members + member)
-                    term = plane * spread[half][core * size.members + member]
-                    known = sums[half][field]
-                    sums[half][field] = term if known is None else known + term
+        add_chip(size, pieces, 2 * pair + half, spread[half], sums[half])
 
 
 def adjoint_of(size, pieces, pair, misfit):
@@ -409,27 +412,54 @@
     return found
 
 
-def first_kernel(chunk, size, flat_ref, near_ref, *refs):
-    if chunk:
-        innov_ref, sum_ref = refs[0], refs[-1]
-        pieces = Pieces(size, chunk, refs[1:-1])
-    else:
-        sum_ref, gain_ref, innov_ref = refs[-3:]
-        pieces = Pieces(size, chunk, refs[:-3])
+def first_kernel(size, flat_ref, near_ref, *refs):
+    sum_ref, gain_ref, innov_ref = refs[-3:]
+    pieces = Pieces(size, 0, refs[:-3])
     flat = flat_ref[0]
     stencil = stencils(flat, [near_ref[0], near_ref[1]], pieces.far())
-    if not chunk:
-        side = lax.div(flat, GROUP)
-        gather_slots(size, pieces, lax.div(flat, 2), lax.rem(flat, GROUP), gain_ref, innov_ref)
-        for row, part, first, second in gain_places(size):
-            sum_ref[pl.ds(row, 2)] = gain_ref[part, jnp.where(side == 0, first, second)]
+    side = lax.div(flat, GROUP)
+    gather_slots(size, pieces, lax.div(flat, 2), lax.rem(flat, GROUP), gain_ref, innov_ref)
+    for row, part, first, second in gain_places(size):
+        sum_ref[pl.ds(row, 2)] = gain_ref[part, jnp.where(side == 0, first, second)]
     sums = [[None] * size.fields for _ in range(2)]
     for pair in range(CHIPS // 2):
         spread = diffuse_pair(*first_alpha(pieces, pair), stencil)
         add_products(size, pieces, pair, spread, sums)
     for field in range(size.fields):
         for half in range(2):
-            sum_ref[field * 2 + half] = sums[half][field] - innov_ref[chunk, field, half]
+            sum_ref[field * 2 + half] = sums[half][field] - innov_ref[0, field, half]
+
+
+def ahead_kernel(chunk, size, flat_ref, near_ref, innov_ref, *refs):
+    part_ref, spread_ref = refs[-2:]
+    pieces = Pieces(size, chunk, refs[:-2])
+    stencil = stencils(flat_ref[0], [near_ref[0], near_ref[1]], pieces.far())
+    sums = [[None] * size.fields for _ in range(2)]
+    for pair in range(CHIPS // 2):
+        spread = diffuse_pair(*first_alpha(pieces, pair), stencil)
+        for half in range(2):
+            chip = 2 * pair + half
+            if chip in LATE:
+                spread_ref[LATE.index(chip)] = spread[half]
+            else:
+                add_chip(size, pieces, chip, spread[half], sums[half])
+    for field in range(size.fields):
+        for half in range(2):
+            part_ref[field * 2 + half] = sums[half][field] - innov_ref[chunk, field, half]
+
+
+def rest_kernel(size, flat_ref, part_ref, spread_ref, *refs):
+    late, sum_ref = refs[:-1], refs[-1]
+    sums = [[part_ref[field * 2 + half] for field in range(size.fields)] for half in range(2)]
+    for place, chip in enumerate(LATE):
+        for core in range(CORES):
+            for field in range(size.fields):
+                for member in range(size.members):
+                    plane = late[place][core, field * size.members + member]
+                    sums[chip & 1][field] += plane * spread_ref[place, core * size.members + member]
+    for field in range(size.fields):
+        for half in range(2):
+            sum_ref[field * 2 + half] = sums[half][field]
 
 
 def misfit_of(size, chunk, gain_ref, mine_ref, theirs_ref):
@@ -611,13 +641,14 @@
     alpha_shape = (CHIPS // 2, 2, CORES * size.members, *block)
     chunks = range(size.chunks)
     first, second, back, held, innov, gain = [], [], None, None, None, None
-    for chunk in chunks:
-        kernel = functools.partial(first_kernel, chunk, size)
-        if chunk:
-            (mine,) = call(kernel, [(size.sums, *block)], common + (innov,) + pieces[chunk])
-        else:
-            shapes = [(size.sums + size.sent_gains, *block), all_fields, all_fields]
-            mine, held, innov = call(kernel, shapes, common + pieces[chunk])
+    shapes = [(size.sums + size.sent_gains, *block), all_fields, all_fields]
+    mine, held, innov = call(functools.partial(first_kernel, size), shapes, common + pieces[0])
+    first.append((mine, shift_by(GROUP, mine)))
+    for chunk in chunks[1:]:
+        shapes = [(size.sums, *block), (len(LATE), CORES * size.members, *block)]
+        known = call(functools.partial(ahead_kernel, chunk, size), shapes, common + (innov,) + pieces[0])
+        late = pieces[chunk][-len(LATE) :]
+        (mine,) = call(functools.partial(rest_kernel, size), [(size.sums, *block)], (flat, *known, *late))
         first.append((mine, shift_by(GROUP, mine)))
     for chunk in chunks:
         kernel = functools.partial(middle_kernel, chunk, size)

time: 89.9 us -> 89.6 us (level)
    pallas_call x9 -> x10, Pallas kernels: 11 us -> 11 us  [call(): pl.pallas_call(kernel, out_shape=[jax.ShapeDtypeStruct(shape, jnp.float32...]
where the time goes in v3:
time: 89.6 us; the launch traced here: 89.4 us
  waiting for transfers between devices  42.4 us (47%)
  starting transfers between devices  21.5 us (24%)
  blocking collectives  13.2 us (15%)
  Pallas kernels  11 us (12%)
    ppermute x17, waiting for transfers between devices, shift_by(): return lax.ppermute(cells, axes, [(i, i ^ mask) for i in range(count)])  42.4 us
    ppermute x17, starting transfers between devices, shift_by(): return lax.ppermute(cells, axes, [(i, i ^ mask) for i in range(count)])  21.5 us
    all_to_all x1, blocking collectives, level_shards(): lax.all_to_all(back, ('mem', 'lat'), 0, 0, axis_index_groups=groups, tile...  13.2 us
    pallas_call x10, Pallas kernels, call(): pl.pallas_call(kernel, out_shape=[jax.ShapeDtypeStruct(shape, jnp.float32...  11 us
  transfers between devices with their start and end apart: 17, of which 10 were waited for; matrix products, arithmetic and copies ran while one was open for 0% of the time, Pallas kernels for 9%

profile of v3, /device:TPU:0, one launch (start us, length us, event | category | flops | bytes accessed | tf_op | source)
XLA Modules:
  0.0 89.4 jit_solution(16670244771196634768)
XLA Ops:
  0.6 1.5 %shard_map.77 = (f32[2,65,8,128]{3,2,1,0:T(8,128)S(1)}, f32[2,64,8,128]{3,2,1,0:T(8,128)S(1)}) custom-call(s32[1]{0:T(128)} %bitcast.flat_ref, bf16[27,32,8,128]{3,2,1,0:T(8,128)(2,1)} %bitcast.46, f32[3,32,8,128]{3,2,1,0:T(8,128)} %bitcast.48, f32[18,8,128]{2,1,0:T(8,128)} %bitcast.50, f32[18,8,128]{2,1,0:T(8,128)} %bitcast.52, s32[3,1,64]{2,1,0:T(1,128)} %mask_hbm.3, ...), custom_call_target="tpu_custom_call" | custom-call | flops 3375876 | bytes 3375876 | tf_op jit(solution)/shard_map/pallas_call | solution.py:556
  2.2 4.0 %collective-permute-start.4 = (f32[2,64,8,128]{3,2,1,0:T(8,128)S(1)}, f32[2,64,8,128]{3,2,1,0:T(8,128)S(1)}, u32[]{:S(2)}, u32[]{:S(2)}) collective-permute-start(f32[2,64,8,128]{3,2,1,0:T(8,128)S(1)} %get-tuple-element.48), channel_id=1, source_target_pairs={{0,12},{1,13},{2,14},{3,15},{4,8},{5,9},{6,10},{7,11},{8,4},{9,5},... | collective-permute-start | bytes 1572872 | tf_op jit(solution)/shard_map/ppermute | solution.py:160
  6.2 1.5 %collective-permute-start.1 = (f32[2,65,8,128]{3,2,1,0:T(8,128)S(1)}, f32[2,65,8,128]{3,2,1,0:T(8,128)S(1)}, u32[]{:S(2)}, u32[]{:S(2)}) collective-permute-start(f32[2,65,8,128]{3,2,1,0:T(8,128)S(1)} %get-tuple-element.43), channel_id=1, source_target_pairs={{0,1},{1,0},{2,3},{3,2},{4,5},{5,4},{6,7},{7,6},{8,9},{9,8},{10,11... | collective-permute-start | bytes 1597448 | tf_op jit(solution)/shard_map/ppermute | solution.py:160
  7.7 2.6 %shard_map.78 = (f32[2,64,8,128]{3,2,1,0:T(8,128)S(1)}, f32[2,64,8,128]{3,2,1,0:T(8,128)S(1)}, f32[64,8,128]{2,1,0:T(8,128)S(1)}, f32[64,8,128]{2,1,0:T(8,128)S(...) custom-call(s32[1]{0:T(128)} %bitcast.flat_ref, ...), custom_call_target="tpu_custom_call" | custom-call | flops 5464836 | bytes 5464836 | tf_op jit(solution)/shard_map/pallas_call | solution.py:556
  10.3 0.1 collective-permute-start
  10.4 0.6 collective-permute-start.5
  11.0 0.2 collective-permute-start.3
  11.2 2.0 %collective-permute-done.3 = f32[3,64,8,128]{3,2,1,0:T(8,128)S(1)} collective-permute-done((f32[3,64,8,128]{3,2,1,0:T(8,128)S(1)}, f32[3,64,8,128]{3,2,1,0:T(8,128)S(1)}, u32[]{:S(2)}, u32[]{:S(2)}) %collective-permute-start.3) | collective-permute-done | bytes 786464 | tf_op jit(solution)/shard_map/ppermute | solution.py:160
  13.3 0.2 collective-permute-start.2
  13.5 15.9 %collective-permute-done.5.refs_4_.refs_5_ = f32[2,64,8,128]{3,2,1,0:T(8,128)S(1)} collective-permute-done((f32[2,64,8,128]{3,2,1,0:T(8,128)S(1)}, f32[2,64,8,128]{3,2,1,0:T(8,128)S(1)}, u32[]{:S(2)}, u32[]{:S(2)}) %collective-permute-start.5) | collective-permute-done | bytes 524320 | tf_op jit(solution)/shard_map/ppermute | solution.py:160
  29.4 0.0 collective-permute-done.4.refs_3_.refs_4_
  29.4 1.2 %collective-permute-done.2.refs_5_.refs_6_ = f32[2,64,8,128]{3,2,1,0:T(8,128)S(1)} collective-permute-done((f32[2,64,8,128]{3,2,1,0:T(8,128)S(1)}, f32[2,64,8,128]{3,2,1,0:T(8,128)S(1)}, u32[]{:S(2)}, u32[]{:S(2)}) %collective-permute-start.2) | collective-permute-done | bytes 524320 | tf_op jit(solution)/shard_map/ppermute | solution.py:160
  30.6 0.4 collective-permute-done.1.refs_2_.refs_3_
  31.1 0.0 copy-start
  31.1 0.1 pad_maximum_fusion
  31.2 0.1 collective-permute-start.6
  31.3 2.2 %collective-permute-start.9 = (f32[2,37,8,128]{3,2,1,0:T(8,128)S(1)}, f32[2,37,8,128]{3,2,1,0:T(8,128)S(1)}, u32[]{:S(2)}, u32[]{:S(2)}) collective-permute-start(f32[2,37,8,128]{3,2,1,0:T(8,128)S(1)} %pad_maximum_fusion.1), channel_id=1, source_target_pairs={{0,13},{1,12},{2,15},{3,14},{4,9},{5,8},{6,11},{7,10},{8,5},{9,4},... | collective-permute-start | bytes 909320 | tf_op jit(solution)/shard_map/ppermute | solution.py:160
  33.5 0.9 collective-permute-start.7
  34.3 1.4 %collective-permute-start.8 = (f32[2,37,8,128]{3,2,1,0:T(8,128)S(1)}, f32[2,37,8,128]{3,2,1,0:T(8,128)S(1)}, u32[]{:S(2)}, u32[]{:S(2)}) collective-permute-start(f32[2,37,8,128]{3,2,1,0:T(8,128)S(1)} %pad_maximum_fusion.3), channel_id=1, source_target_pairs={{0,5},{1,4},{2,7},{3,6},{4,1},{5,0},{6,3},{7,2},{8,13},{9,12},{10,... | collective-permute-start | bytes 909320 | tf_op jit(solution)/shard_map/ppermute | solution.py:160
  35.9 7.3 %collective-permute-done.9.refs_9_.refs_10_ = f32[2,37,8,128]{3,2,1,0:T(8,128)S(1)} collective-permute-done((f32[2,37,8,128]{3,2,1,0:T(8,128)S(1)}, f32[2,37,8,128]{3,2,1,0:T(8,128)S(1)}, u32[]{:S(2)}, u32[]{:S(2)}) %collective-permute-start.9) | collective-permute-done | bytes 303136 | tf_op jit(solution)/shard_map/ppermute | solution.py:160
  43.2 2.1 %collective-permute-start.12 = (f32[2,27,8,128]{3,2,1,0:T(8,128)S(1)}, f32[2,27,8,128]{3,2,1,0:T(8,128)S(1)}, u32[]{:S(2)}, u32[]{:S(2)}) collective-permute-start(f32[2,27,8,128]{3,2,1,0:T(8,128)S(1)} %pad_maximum_fusion.6), channel_id=1, source_target_pairs={{0,13},{1,12},{2,15},{3,14},{4,9},{5,8},{6,11},{7,10},{8,5},{9,4},... | collective-permute-start | bytes 663560 | tf_op jit(solution)/shard_map/ppermute | solution.py:160
  45.3 3.5 %collective-permute-done.7.refs_7_.refs_8_ = f32[2,37,8,128]{3,2,1,0:T(8,128)S(1)} collective-permute-done((f32[2,37,8,128]{3,2,1,0:T(8,128)S(1)}, f32[2,37,8,128]{3,2,1,0:T(8,128)S(1)}, u32[]{:S(2)}, u32[]{:S(2)}) %collective-permute-start.7) | collective-permute-done | bytes 303136 | tf_op jit(solution)/shard_map/ppermute | solution.py:160
  48.8 1.2 %collective-permute-start.10 = (f32[2,27,8,128]{3,2,1,0:T(8,128)S(1)}, f32[2,27,8,128]{3,2,1,0:T(8,128)S(1)}, u32[]{:S(2)}, u32[]{:S(2)}) collective-permute-start(f32[2,27,8,128]{3,2,1,0:T(8,128)S(1)} %pad_maximum_fusion.4), channel_id=1, source_target_pairs={{0,8},{1,9},{2,10},{3,11},{4,12},{5,13},{6,14},{7,15},{8,0},{9,1},... | collective-permute-start | bytes 663560 | tf_op jit(solution)/shard_map/ppermute | solution.py:160
  50.0 0.0 collective-permute-done.8.refs_8_.refs_9_
  50.0 1.4 %collective-permute-start.11 = (f32[2,27,8,128]{3,2,1,0:T(8,128)S(1)}, f32[2,27,8,128]{3,2,1,0:T(8,128)S(1)}, u32[]{:S(2)}, u32[]{:S(2)}) collective-permute-start(f32[2,27,8,128]{3,2,1,0:T(8,128)S(1)} %pad_maximum_fusion.5), channel_id=1, source_target_pairs={{0,5},{1,4},{2,7},{3,6},{4,1},{5,0},{6,3},{7,2},{8,13},{9,12},{10,... | collective-permute-start | bytes 663560 | tf_op jit(solution)/shard_map/ppermute | solution.py:160
  51.4 0.0 collective-permute-done.refs_1_.refs_2_
  51.4 0.0 collective-permute-done.6.refs_6_.refs_7_
  51.4 0.0 copy-done
  51.4 0.9 %shard_map.79 = (f32[38,8,128]{2,1,0:T(8,128)S(1)}, f32[2,9,2,8,128]{4,3,2,1,0:T(8,128)S(1)}, f32[2,9,2,8,128]{4,3,2,1,0:T(8,128)S(1)}) custom-call(s32[1]{0:T(128)} %bitcast.flat_ref, f32[2,8,128]{2,1,0:T(8,128)S(1)} %bitcast.40, f32[64,8,128]{2,1,0:T(8,128)S(1)} %get-tuple-element.41.refs_0_.refs_1_, ...), custom_call_target="tpu_custom_call" | custom-call | flops 5046276 | bytes 5046276 | tf_op jit(solution)/shard_map/pallas_call | solution.py:556
  52.3 2.6 %collective-permute-start.14 = (f32[38,8,128]{2,1,0:T(8,128)S(1)}, f32[38,8,128]{2,1,0:T(8,128)S(1)}, u32[]{:S(2)}, u32[]{:S(2)}) collective-permute-start(f32[38,8,128]{2,1,0:T(8,128)S(1)} %get-tuple-element.67.mine_ref), channel_id=1, source_target_pairs={{0,16},{1,17},{2,18},{3,19},{4,20},{5,21},{6,22},{7,23},{8,24},{9,... | collective-permute-start | bytes 466952 | tf_op jit(solution)/shard_map/ppermute | solution.py:160
  55.0 0.7 shard_map.80
  55.7 0.0 collective-permute-done.12.refs_2_.refs_12_.refs_13_
  55.7 5.6 %collective-permute-done.10.refs_0_.refs_10_.refs_11_ = f32[2,27,8,128]{3,2,1,0:T(8,128)S(1)} collective-permute-done((f32[2,27,8,128]{3,2,1,0:T(8,128)S(1)}, f32[2,27,8,128]{3,2,1,0:T(8,128)S(1)}, u32[]{:S(2)}, u32[]{:S(2)}) %collective-permute-start.10) | collective-permute-done | bytes 221216 | tf_op jit(solution)/shard_map/ppermute | solution.py:160
  61.2 0.0 collective-permute-done.11.refs_1_.refs_11_.refs_12_
  61.2 0.1 shard_map.81.mine_ref
  61.3 0.4 collective-permute-start.13
  61.7 0.0 collective-permute-done.14.theirs_ref
  61.7 1.4 %shard_map.82 = (f32[18,8,128]{2,1,0:T(8,128)S(1)}, f32[4,2,6,8,128]{4,3,2,1,0:T(8,128)S(1)}, f32[2,9,2,8,128]{4,3,2,1,0:T(8,128)S(1)}) custom-call(s32[1]{0:T(128)} %bitcast.flat_ref, f32[2,8,128]{2,1,0:T(8,128)S(1)} %bitcast.42, f32[38,8,128]{2,1,0:T(8,128)S(1)} %get-tuple-element.67.mine_ref, f32[38,8,128]{2,1,0:T(8,128)S(1)} %collective-permute-done.14.theirs_ref, ...), custom_call_target="tpu_custom_call" | custom-call | flops 5619716 | bytes 5619716 | tf_op jit(solution)/shard_map/pallas_call | solution.py:556
  63.1 2.7 %collective-permute-start.16 = (f32[18,8,128]{2,1,0:T(8,128)S(1)}, f32[18,8,128]{2,1,0:T(8,128)S(1)}, u32[]{:S(2)}, u32[]{:S(2)}) collective-permute-start(f32[18,8,128]{2,1,0:T(8,128)S(1)} %get-tuple-element.72.mine_ref), channel_id=1, source_target_pairs={{0,16},{1,17},{2,18},{3,19},{4,20},{5,21},{6,22},{7,23},{8,24},{9,... | collective-permute-start | bytes 221192 | tf_op jit(solution)/shard_map/ppermute | solution.py:160
  65.8 1.7 %collective-permute-done.13.theirs_ref = f32[18,8,128]{2,1,0:T(8,128)S(1)} collective-permute-done((f32[18,8,128]{2,1,0:T(8,128)S(1)}, f32[18,8,128]{2,1,0:T(8,128)S(1)}, u32[]{:S(2)}, u32[]{:S(2)}) %collective-permute-start.13) | collective-permute-done | bytes 73760 | tf_op jit(solution)/shard_map/ppermute | solution.py:160
  67.5 1.3 %shard_map.83 = (f32[18,8,128]{2,1,0:T(8,128)S(1)}, f32[4,2,6,8,128]{4,3,2,1,0:T(8,128)S(1)}) custom-call(s32[1]{0:T(128)} %bitcast.flat_ref, f32[2,8,128]{2,1,0:T(8,128)S(1)} %bitcast.43, f32[18,8,128]{2,1,0:T(8,128)S(1)} %shard_map.81.mine_ref, f32[18,8,128]{2,1,0:T(8,128)S(1)} %collective-permute-done.13.theirs_ref, ...), custom_call_target="tpu_custom_call" | custom-call | flops 5971972 | bytes 5971972 | tf_op jit(solution)/shard_map/pallas_call | solution.py:556
  68.9 0.1 collective-permute-start.15
  69.0 0.7 collective-permute-done.16.theirs_ref
  69.7 0.7 shard_map.84.refs_0_
  70.4 4.0 %collective-permute-done.15.theirs_ref = f32[18,8,128]{2,1,0:T(8,128)S(1)} collective-permute-done((f32[18,8,128]{2,1,0:T(8,128)S(1)}, f32[18,8,128]{2,1,0:T(8,128)S(1)}, u32[]{:S(2)}, u32[]{:S(2)}) %collective-permute-start.15) | collective-permute-done | bytes 73760 | tf_op jit(solution)/shard_map/ppermute | solution.py:160
  74.4 0.8 shard_map.85
  75.2 13.2 %all_to_all.5.back_ref = f32[16,8,8,128]{3,2,1,0:T(8,128)S(1)} all-to-all(f32[16,8,8,128]{3,2,1,0:T(8,128)S(1)} %shard_map.85), channel_id=1, replica_groups={{0,1,2,3,4,5,6,7,8,9,10,11,12,13,14,15},{16,17,18,19,20,21,22,23,24,25,..., dimensions={0} | all-to-all | bytes 1048576 | tf_op jit(solution)/shard_map/all_to_all | solution.py:668
  88.4 1.0 %shard_map.86 = (f32[3,32,4,256]{3,2,1,0:T(4,128)}, f32[18,4,256]{2,1,0:T(4,128)}) custom-call(s32[1]{0:T(128)} %bitcast.flat_ref, f32[16,8,8,128]{3,2,1,0:T(8,128)S(1)} %all_to_all.5.back_ref), custom_call_target="tpu_custom_call" | custom-call | flops 991236 | bytes 991236 | tf_op jit(solution)/shard_map/pallas_call | solution.py:556
  (18 shorter events, 0.3 us)
Async XLA Ops:
  2.2 27.2 %collective-permute-start.4 = (f32[2,64,8,128]{3,2,1,0:T(8,128)S(1)}, f32[2,64,8,128]{3,2,1,0:T(8,128)S(1)}, u32[]{:S(2)}, u32[]{:S(2)}) collective-permute-start(f32[2,64,8,128]{3,2,1,0:T(8,128)S(1)} %get-tuple-element.48), channel_id=1, source_target_pairs={{0,12},{1,13},{2,14},{3,15},{4,8},{5,9},{6,10},{7,11},{8,4},{9,5},... | collective-permute-start | bytes 1572872 | tf_op jit(solution)/shard_map/ppermute | solution.py:160
  6.2 24.8 %collective-permute-start.1 = (f32[2,65,8,128]{3,2,1,0:T(8,128)S(1)}, f32[2,65,8,128]{3,2,1,0:T(8,128)S(1)}, u32[]{:S(2)}, u32[]{:S(2)}) collective-permute-start(f32[2,65,8,128]{3,2,1,0:T(8,128)S(1)} %get-tuple-element.43), channel_id=1, source_target_pairs={{0,1},{1,0},{2,3},{3,2},{4,5},{5,4},{6,7},{7,6},{8,9},{9,8},{10,11... | collective-permute-start | bytes 1597448 | tf_op jit(solution)/shard_map/ppermute | solution.py:160
  10.3 41.1 %collective-permute-start = (f32[64,8,128]{2,1,0:T(8,128)S(1)}, f32[64,8,128]{2,1,0:T(8,128)S(1)}, u32[]{:S(2)}, u32[]{:S(2)}) collective-permute-start(f32[64,8,128]{2,1,0:T(8,128)S(1)} %get-tuple-element.42), channel_id=1, source_target_pairs={{0,2},{1,3},{2,0},{3,1},{4,6},{5,7},{6,4},{7,5},{8,10},{9,11},{10,... | collective-permute-start | bytes 786440 | tf_op jit(solution)/shard_map/ppermute | solution.py:160
  10.4 19.0 %collective-permute-start.5 = (f32[2,64,8,128]{3,2,1,0:T(8,128)S(1)}, f32[2,64,8,128]{3,2,1,0:T(8,128)S(1)}, u32[]{:S(2)}, u32[]{:S(2)}) collective-permute-start(f32[2,64,8,128]{3,2,1,0:T(8,128)S(1)} %get-tuple-element.51), channel_id=1, source_target_pairs={{0,4},{1,5},{2,6},{3,7},{4,0},{5,1},{6,2},{7,3},{8,12},{9,13},{10,... | collective-permute-start | bytes 1572872 | tf_op jit(solution)/shard_map/ppermute | solution.py:160
  11.0 2.3 %collective-permute-start.3 = (f32[3,64,8,128]{3,2,1,0:T(8,128)S(1)}, f32[3,64,8,128]{3,2,1,0:T(8,128)S(1)}, u32[]{:S(2)}, u32[]{:S(2)}) collective-permute-start(f32[3,64,8,128]{3,2,1,0:T(8,128)S(1)} %get-tuple-element.46), channel_id=1, source_target_pairs={{0,2},{1,3},{2,0},{3,1},{4,6},{5,7},{6,4},{7,5},{8,10},{9,11},{10,... | collective-permute-start | bytes 2359304 | tf_op jit(solution)/shard_map/ppermute | solution.py:160
  13.3 17.4 %collective-permute-start.2 = (f32[2,64,8,128]{3,2,1,0:T(8,128)S(1)}, f32[2,64,8,128]{3,2,1,0:T(8,128)S(1)}, u32[]{:S(2)}, u32[]{:S(2)}) collective-permute-start(f32[2,64,8,128]{3,2,1,0:T(8,128)S(1)} %get-tuple-element.44), channel_id=1, source_target_pairs={{0,9},{1,8},{2,11},{3,10},{4,13},{5,12},{6,15},{7,14},{8,1},{9,0},... | collective-permute-start | bytes 1572872 | tf_op jit(solution)/shard_map/ppermute | solution.py:160
  31.1 20.3 %copy-start = (f32[2,4,256]{2,1,0:T(4,128)S(1)}, f32[2,4,256]{2,1,0:T(4,128)}, u32[]{:S(2)}) copy-start(f32[2,4,256]{2,1,0:T(4,128)} %param.10) | copy-start | bytes 24580
  31.2 20.2 %collective-permute-start.6 = (f32[4,64,8,128]{3,2,1,0:T(8,128)S(1)}, f32[4,64,8,128]{3,2,1,0:T(8,128)S(1)}, u32[]{:S(2)}, u32[]{:S(2)}) collective-permute-start(f32[4,64,8,128]{3,2,1,0:T(8,128)S(1)} %pad_maximum_fusion), channel_id=1, source_target_pairs={{0,2},{1,3},{2,0},{3,1},{4,6},{5,7},{6,4},{7,5},{8,10},{9,11},{10,... | collective-permute-start | bytes 3145736 | tf_op jit(solution)/shard_map/ppermute | solution.py:160
  31.3 11.9 %collective-permute-start.9 = (f32[2,37,8,128]{3,2,1,0:T(8,128)S(1)}, f32[2,37,8,128]{3,2,1,0:T(8,128)S(1)}, u32[]{:S(2)}, u32[]{:S(2)}) collective-permute-start(f32[2,37,8,128]{3,2,1,0:T(8,128)S(1)} %pad_maximum_fusion.1), channel_id=1, source_target_pairs={{0,13},{1,12},{2,15},{3,14},{4,9},{5,8},{6,11},{7,10},{8,5},{9,4},... | collective-permute-start | bytes 909320 | tf_op jit(solution)/shard_map/ppermute | solution.py:160
  33.5 15.3 %collective-permute-start.7 = (f32[2,37,8,128]{3,2,1,0:T(8,128)S(1)}, f32[2,37,8,128]{3,2,1,0:T(8,128)S(1)}, u32[]{:S(2)}, u32[]{:S(2)}) collective-permute-start(f32[2,37,8,128]{3,2,1,0:T(8,128)S(1)} %pad_maximum_fusion.2), channel_id=1, source_target_pairs={{0,8},{1,9},{2,10},{3,11},{4,12},{5,13},{6,14},{7,15},{8,0},{9,1},... | collective-permute-start | bytes 909320 | tf_op jit(solution)/shard_map/ppermute | solution.py:160
  34.3 15.7 %collective-permute-start.8 = (f32[2,37,8,128]{3,2,1,0:T(8,128)S(1)}, f32[2,37,8,128]{3,2,1,0:T(8,128)S(1)}, u32[]{:S(2)}, u32[]{:S(2)}) collective-permute-start(f32[2,37,8,128]{3,2,1,0:T(8,128)S(1)} %pad_maximum_fusion.3), channel_id=1, source_target_pairs={{0,5},{1,4},{2,7},{3,6},{4,1},{5,0},{6,3},{7,2},{8,13},{9,12},{10,... | collective-permute-start | bytes 909320 | tf_op jit(solution)/shard_map/ppermute | solution.py:160
  43.2 12.5 %collective-permute-start.12 = (f32[2,27,8,128]{3,2,1,0:T(8,128)S(1)}, f32[2,27,8,128]{3,2,1,0:T(8,128)S(1)}, u32[]{:S(2)}, u32[]{:S(2)}) collective-permute-start(f32[2,27,8,128]{3,2,1,0:T(8,128)S(1)} %pad_maximum_fusion.6), channel_id=1, source_target_pairs={{0,13},{1,12},{2,15},{3,14},{4,9},{5,8},{6,11},{7,10},{8,5},{9,4},... | collective-permute-start | bytes 663560 | tf_op jit(solution)/shard_map/ppermute | solution.py:160
  48.8 12.4 %collective-permute-start.10 = (f32[2,27,8,128]{3,2,1,0:T(8,128)S(1)}, f32[2,27,8,128]{3,2,1,0:T(8,128)S(1)}, u32[]{:S(2)}, u32[]{:S(2)}) collective-permute-start(f32[2,27,8,128]{3,2,1,0:T(8,128)S(1)} %pad_maximum_fusion.4), channel_id=1, source_target_pairs={{0,8},{1,9},{2,10},{3,11},{4,12},{5,13},{6,14},{7,15},{8,0},{9,1},... | collective-permute-start | bytes 663560 | tf_op jit(solution)/shard_map/ppermute | solution.py:160
  50.0 11.2 %collective-permute-start.11 = (f32[2,27,8,128]{3,2,1,0:T(8,128)S(1)}, f32[2,27,8,128]{3,2,1,0:T(8,128)S(1)}, u32[]{:S(2)}, u32[]{:S(2)}) collective-permute-start(f32[2,27,8,128]{3,2,1,0:T(8,128)S(1)} %pad_maximum_fusion.5), channel_id=1, source_target_pairs={{0,5},{1,4},{2,7},{3,6},{4,1},{5,0},{6,3},{7,2},{8,13},{9,12},{10,... | collective-permute-start | bytes 663560 | tf_op jit(solution)/shard_map/ppermute | solution.py:160
  52.3 9.4 %collective-permute-start.14 = (f32[38,8,128]{2,1,0:T(8,128)S(1)}, f32[38,8,128]{2,1,0:T(8,128)S(1)}, u32[]{:S(2)}, u32[]{:S(2)}) collective-permute-start(f32[38,8,128]{2,1,0:T(8,128)S(1)} %get-tuple-element.67.mine_ref), channel_id=1, source_target_pairs={{0,16},{1,17},{2,18},{3,19},{4,20},{5,21},{6,22},{7,23},{8,24},{9,... | collective-permute-start | bytes 466952 | tf_op jit(solution)/shard_map/ppermute | solution.py:160
  61.3 6.2 %collective-permute-start.13 = (f32[18,8,128]{2,1,0:T(8,128)S(1)}, f32[18,8,128]{2,1,0:T(8,128)S(1)}, u32[]{:S(2)}, u32[]{:S(2)}) collective-permute-start(f32[18,8,128]{2,1,0:T(8,128)S(1)} %shard_map.81.mine_ref), channel_id=1, source_target_pairs={{0,16},{1,17},{2,18},{3,19},{4,20},{5,21},{6,22},{7,23},{8,24},{9,... | collective-permute-start | bytes 221192 | tf_op jit(solution)/shard_map/ppermute | solution.py:160
  63.1 6.5 %collective-permute-start.16 = (f32[18,8,128]{2,1,0:T(8,128)S(1)}, f32[18,8,128]{2,1,0:T(8,128)S(1)}, u32[]{:S(2)}, u32[]{:S(2)}) collective-permute-start(f32[18,8,128]{2,1,0:T(8,128)S(1)} %get-tuple-element.72.mine_ref), channel_id=1, source_target_pairs={{0,16},{1,17},{2,18},{3,19},{4,20},{5,21},{6,22},{7,23},{8,24},{9,... | collective-permute-start | bytes 221192 | tf_op jit(solution)/shard_map/ppermute | solution.py:160
  68.9 5.6 %collective-permute-start.15 = (f32[18,8,128]{2,1,0:T(8,128)S(1)}, f32[18,8,128]{2,1,0:T(8,128)S(1)}, u32[]{:S(2)}, u32[]{:S(2)}) collective-permute-start(f32[18,8,128]{2,1,0:T(8,128)S(1)} %get-tuple-element.70.mine_ref), channel_id=1, source_target_pairs={{0,16},{1,17},{2,18},{3,19},{4,20},{5,21},{6,22},{7,23},{8,24},{9,... | collective-permute-start | bytes 221192 | tf_op jit(solution)/shard_map/ppermute | solution.py:160

commit v4 on v3

--- a/solution.py
+++ b/solution.py
@@ -212,27 +212,31 @@
     return outs[place] if core == 0 else outs[-1].at[LATE.index(chip)]
 
 
-def pack_kernel(size, chips, flat_ref, perturb_hbm, alpha_hbm, innov_hbm, weight_hbm, mask_hbm, near_hbm, *refs):
-    outs, scratch = refs[:-10], refs[-10:]
-    perturb_ref, alpha_ref, innov_ref, weight_ref, mask_ref, near_ref, tiles_ref, plane_sems, alpha_sems, sems = scratch
+def pack_kernel(size, chips, fetch, flat_ref, *refs):
     flat = flat_ref[0]
     own = lax.rem(flat, GROUP)
     mem_index = lax.div(flat, 2)
     places = [(chip, core, chunk) for chip in chips for core in range(CORES) for chunk in range(size.chunks)]
     levels = [lax.bitwise_xor(own, flat_offset(chip, core)) + chunk * GROUP for chip, core, chunk in places]
-    plane_copies = [
-        pltpu.make_async_copy(perturb_hbm.at[:, level], perturb_ref.at[place], plane_sems.at[place])
-        for place, level in enumerate(levels)
-    ]
-    alpha_copies = [
-        pltpu.make_async_copy(alpha_hbm.at[:, level], alpha_ref.at[place], alpha_sems.at[place])
-        for place, level in enumerate(levels)
-    ]
-    pairs = ((mask_hbm, mask_ref), (near_hbm, near_ref), (innov_hbm, innov_ref), (weight_hbm, weight_ref))
-    copies = [pltpu.make_async_copy(source, target, sems.at[place]) for place, (source, target) in enumerate(pairs)]
-    for copy in plane_copies + copies + alpha_copies:
-        copy.start()
-    copies[0].wait()
+    sources = refs[:6]
+    if fetch:
+        outs, scratch = refs[6:-10], refs[-10:]
+        perturb_ref, alpha_ref, *held, tiles_ref, plane_sems, alpha_sems, sems = scratch
+        plane_copies = [
+            pltpu.make_async_copy(sources[0].at[:, level], perturb_ref.at[place], plane_sems.at[place])
+            for place, level in enumerate(levels)
+        ]
+        alpha_copies = [
+            pltpu.make_async_copy(sources[1].at[:, level], alpha_ref.at[place], alpha_sems.at[place])
+            for place, level in enumerate(levels)
+        ]
+        copies = [pltpu.make_async_copy(sources[2 + n], held[n], sems.at[n]) for n in range(4)]
+        for copy in plane_copies + copies + alpha_copies:
+            copy.start()
+        copies[2].wait()
+    else:
+        outs, tiles_ref, held = refs[6:-1], refs[-1], sources[2:]
+    innov_ref, weight_ref, mask_ref, near_ref = held
     tiles = mask_ref.shape[-1]
     shape = (tiles, tiles * TILE)
     spread_out = lax.broadcasted_iota(jnp.int32, shape, 0) == lax.div(lax.broadcasted_iota(jnp.int32, shape, 1), TILE)
@@ -242,22 +246,27 @@
             mask_ref[slot].astype(jnp.float32), spread_out.astype(jnp.float32), preferred_element_type=jnp.float32
         )
         tiles_ref[slot] = jnp.where(line < TILE, cells[:, :LANES], cells[:, LANES:])
-    copies[1].wait()
+    if fetch:
+        copies[3].wait()
     if 1 in chips:
         coef_out = outs[chips.index(1)]
         coef_out[0, size.all_rows] = near_ref[0]
         coef_out[1, size.all_rows] = near_ref[1]
     for place, (chip, core, chunk) in enumerate(places):
-        plane_copies[place].wait()
+        if fetch:
+            plane_copies[place].wait()
+        planes = perturb_ref[place] if fetch else sources[0][:, levels[place]]
         base = size.planes_at(chunk)
-        pack_target(outs, chips, chip, core)[base : base + size.planes] = perturb_ref[place].astype(jnp.float32)
-    copies[2].wait()
-    copies[3].wait()
+        pack_target(outs, chips, chip, core)[base : base + size.planes] = planes.astype(jnp.float32)
+    if fetch:
+        copies[0].wait()
+        copies[1].wait()
     for place, (chip, core, chunk) in enumerate(places):
         out = pack_target(outs, chips, chip, core)
         base = size.extras_at(chunk)
-        alpha_copies[place].wait()
-        out[base : base + size.members] = alpha_ref[place]
+        if fetch:
+            alpha_copies[place].wait()
+        out[base : base + size.members] = alpha_ref[place] if fetch else sources[1][:, levels[place]]
         row, inside, field = row_in_block(size, levels[place], mem_index)
         row = jnp.minimum(row, size.owned - 1)
         slot = jnp.minimum(lax.div(field, size.vars), size.slots - 1)
@@ -579,35 +588,32 @@
         near,
     )
 
-    def pack(chips, flat):
+    def pack(chips, flat, fetch):
         count = len(chips) * CORES * size.chunks
-        return call(
-            functools.partial(pack_kernel, size, chips),
-            pack_shapes(size, chips),
-            (flat,) + operands,
-            [
+        scratch = [pltpu.VMEM((size.slots, *block), jnp.float32)]
+        if fetch:
+            scratch = [
                 pltpu.VMEM((count, size.planes, *block), jnp.bfloat16),
                 pltpu.VMEM((count, size.members, *block), jnp.float32),
-                pltpu.VMEM((size.owned, *block), jnp.float32),
-                pltpu.VMEM((size.owned, *block), jnp.float32),
-                pltpu.VMEM(obs_mask.shape, jnp.int32),
-                pltpu.VMEM(near.shape, jnp.float32),
-                pltpu.VMEM((size.slots, *block), jnp.float32),
+                *(pltpu.VMEM(cells.shape, cells.dtype) for cells in operands[2:]),
+                *scratch,
                 pltpu.SemaphoreType.DMA((count,)),
                 pltpu.SemaphoreType.DMA((count,)),
                 pltpu.SemaphoreType.DMA((4,)),
-            ],
-            [pltpu.SMEM] + [pltpu.HBM] * 6,
-        )
-
-    early = list(pack(EARLY[:2], flat))
+            ]
+        spaces = [pltpu.SMEM] + [pltpu.HBM if fetch else pltpu.VMEM] * 6
+        kernel = functools.partial(pack_kernel, size, chips, fetch)
+        return call(kernel, pack_shapes(size, chips), (flat,) + operands, scratch, spaces)
+
+    early = list(pack(EARLY[:2], flat, True))
     flat, early[0], early[1] = lax.optimization_barrier((flat, early[0], early[1]))
-    packed = pack(EARLY[2:] + (0,) + LATE, flat)
+    packed = pack(EARLY[2:] + (0,) + LATE, flat, False)
     early += packed[:2]
     kept, late, late_out = packed[2:4], packed[4:7], packed[7]
     crossed = shift_by(CORES, late_out)
-    own_crossed = shift_by(CORES, kept[1])
     got = [shift_by(flat_offset(chip, 0), cells) for chip, cells in zip(EARLY, early)]
+    got[1], own_out = lax.optimization_barrier((got[1], kept[1]))
+    own_crossed = shift_by(CORES, own_out)
     got_late = []
     for chunk in range(size.chunks):
         base = size.planes_at(chunk)

time: 89.6 us -> 89.6 us (level)
  waiting for transfers between devices: 42.4 us -> 44.6 us
  Pallas kernels: 11 us -> 9.19 us
    ppermute x17, waiting for transfers between devices: 42.4 us -> 44.6 us  [shift_by(): return lax.ppermute(cells, axes, [(i, i ^ mask) for i in range(count)])]
    pallas_call x10, Pallas kernels: 11 us -> 9.19 us  [call(): pl.pallas_call(kernel, out_shape=[jax.ShapeDtypeStruct(shape, jnp.float32...]
  transfers between devices with their start and end apart: 17 -> 17, of which waited for: 10 -> 10; matrix products, arithmetic and copies ran while one was open for 0% -> 0% of each run, Pallas kernels for 9% -> 6%
where the time goes in v4:
time: 89.6 us; the launch traced here: 89.4 us
  waiting for transfers between devices  44.6 us (50%)
  starting transfers between devices  21.6 us (24%)
  blocking collectives  12.7 us (14%)
  Pallas kernels  9.19 us (10%)
  between operations  0.92 us (1%)
    ppermute x17, waiting for transfers between devices, shift_by(): return lax.ppermute(cells, axes, [(i, i ^ mask) for i in range(count)])  44.6 us
    ppermute x17, starting transfers between devices, shift_by(): return lax.ppermute(cells, axes, [(i, i ^ mask) for i in range(count)])  21.6 us
    all_to_all x1, blocking collectives, level_shards(): lax.all_to_all(back, ('mem', 'lat'), 0, 0, axis_index_groups=groups, tile...  12.7 us
    pallas_call x10, Pallas kernels, call(): pl.pallas_call(kernel, out_shape=[jax.ShapeDtypeStruct(shape, jnp.float32...  9.19 us
  transfers between devices with their start and end apart: 17, of which 10 were waited for; matrix products, arithmetic and copies ran while one was open for 0% of the time, Pallas kernels for 6%

profile of v4, /device:TPU:0, one launch (start us, length us, event | category | flops | bytes accessed | tf_op | source)
XLA Modules:
  0.0 89.4 jit_solution(3283450149419381271)
XLA Ops:
  0.6 0.0 copy-start.5
  0.7 1.7 %shard_map.77 = (f32[2,65,8,128]{3,2,1,0:T(8,128)S(1)}, f32[2,64,8,128]{3,2,1,0:T(8,128)S(1)}) custom-call(s32[1]{0:T(128)} %bitcast.flat_ref, bf16[27,32,8,128]{3,2,1,0:T(8,128)(2,1)} %bitcast.38, f32[3,32,8,128]{3,2,1,0:T(8,128)} %bitcast.40, f32[18,8,128]{2,1,0:T(8,128)} %bitcast.50, f32[18,8,128]{2,1,0:T(8,128)} %bitcast.52, s32[3,1,64]{2,1,0:T(1,128)} %refs_4_.3, ...), custom_call_target="tpu_custom_call" | custom-call | flops 3375876 | bytes 3375876 | tf_op jit(solution)/shard_map/pallas_call | solution.py:565
  2.4 4.0 %collective-permute-start = (f32[2,64,8,128]{3,2,1,0:T(8,128)S(1)}, f32[2,64,8,128]{3,2,1,0:T(8,128)S(1)}, u32[]{:S(2)}, u32[]{:S(2)}) collective-permute-start(f32[2,64,8,128]{3,2,1,0:T(8,128)S(1)} %get-tuple-element.44), channel_id=1, source_target_pairs={{0,12},{1,13},{2,14},{3,15},{4,8},{5,9},{6,10},{7,11},{8,4},{9,5},... | collective-permute-start | bytes 1572872 | tf_op jit(solution)/shard_map/ppermute | solution.py:160
  6.4 1.5 %collective-permute-start.2 = (f32[2,65,8,128]{3,2,1,0:T(8,128)S(1)}, f32[2,65,8,128]{3,2,1,0:T(8,128)S(1)}, u32[]{:S(2)}, u32[]{:S(2)}) collective-permute-start(f32[2,65,8,128]{3,2,1,0:T(8,128)S(1)} %get-tuple-element.47), channel_id=1, source_target_pairs={{0,1},{1,0},{2,3},{3,2},{4,5},{5,4},{6,7},{7,6},{8,9},{9,8},{10,11... | collective-permute-start | bytes 1597448 | tf_op jit(solution)/shard_map/ppermute | solution.py:160
  7.9 0.0 copy-done.2
  8.0 0.6 shard_map.78
  8.6 0.5 collective-permute-start.3
  9.0 0.2 collective-permute-start.5
  9.3 0.0 collective-permute-start.4
  9.3 9.9 %collective-permute-done.refs_3_.refs_4_ = f32[2,64,8,128]{3,2,1,0:T(8,128)S(1)} collective-permute-done((f32[2,64,8,128]{3,2,1,0:T(8,128)S(1)}, f32[2,64,8,128]{3,2,1,0:T(8,128)S(1)}, u32[]{:S(2)}, u32[]{:S(2)}) %collective-permute-start) | collective-permute-done | bytes 524320 | tf_op jit(solution)/shard_map/ppermute | solution.py:160
  19.2 0.0 collective-permute-done.4
  19.3 10.3 %collective-permute-done.5.refs_4_.refs_5_ = f32[2,64,8,128]{3,2,1,0:T(8,128)S(1)} collective-permute-done((f32[2,64,8,128]{3,2,1,0:T(8,128)S(1)}, f32[2,64,8,128]{3,2,1,0:T(8,128)S(1)}, u32[]{:S(2)}, u32[]{:S(2)}) %collective-permute-start.5) | collective-permute-done | bytes 524320 | tf_op jit(solution)/shard_map/ppermute | solution.py:160
  29.6 1.2 %collective-permute-done.3.refs_5_.refs_6_ = f32[2,64,8,128]{3,2,1,0:T(8,128)S(1)} collective-permute-done((f32[2,64,8,128]{3,2,1,0:T(8,128)S(1)}, f32[2,64,8,128]{3,2,1,0:T(8,128)S(1)}, u32[]{:S(2)}, u32[]{:S(2)}) %collective-permute-start.3) | collective-permute-done | bytes 524320 | tf_op jit(solution)/shard_map/ppermute | solution.py:160
  30.8 0.4 collective-permute-done.2.refs_2_.refs_3_
  31.3 0.1 pad_maximum_fusion
  31.4 0.1 collective-permute-start.6
  31.5 0.6 collective-permute-start.1
  32.1 2.0 %collective-permute-start.9 = (f32[2,37,8,128]{3,2,1,0:T(8,128)S(1)}, f32[2,37,8,128]{3,2,1,0:T(8,128)S(1)}, u32[]{:S(2)}, u32[]{:S(2)}) collective-permute-start(f32[2,37,8,128]{3,2,1,0:T(8,128)S(1)} %pad_maximum_fusion.1), channel_id=1, source_target_pairs={{0,13},{1,12},{2,15},{3,14},{4,9},{5,8},{6,11},{7,10},{8,5},{9,4},... | collective-permute-start | bytes 909320 | tf_op jit(solution)/shard_map/ppermute | solution.py:160
  34.1 0.9 %collective-permute-start.7 = (f32[2,37,8,128]{3,2,1,0:T(8,128)S(1)}, f32[2,37,8,128]{3,2,1,0:T(8,128)S(1)}, u32[]{:S(2)}, u32[]{:S(2)}) collective-permute-start(f32[2,37,8,128]{3,2,1,0:T(8,128)S(1)} %pad_maximum_fusion.2), channel_id=1, source_target_pairs={{0,8},{1,9},{2,10},{3,11},{4,12},{5,13},{6,14},{7,15},{8,0},{9,1},... | collective-permute-start | bytes 909320 | tf_op jit(solution)/shard_map/ppermute | solution.py:160
  35.0 1.4 %collective-permute-start.8 = (f32[2,37,8,128]{3,2,1,0:T(8,128)S(1)}, f32[2,37,8,128]{3,2,1,0:T(8,128)S(1)}, u32[]{:S(2)}, u32[]{:S(2)}) collective-permute-start(f32[2,37,8,128]{3,2,1,0:T(8,128)S(1)} %pad_maximum_fusion.3), channel_id=1, source_target_pairs={{0,5},{1,4},{2,7},{3,6},{4,1},{5,0},{6,3},{7,2},{8,13},{9,12},{10,... | collective-permute-start | bytes 909320 | tf_op jit(solution)/shard_map/ppermute | solution.py:160
  36.6 7.4 %collective-permute-done.9.refs_9_.refs_10_ = f32[2,37,8,128]{3,2,1,0:T(8,128)S(1)} collective-permute-done((f32[2,37,8,128]{3,2,1,0:T(8,128)S(1)}, f32[2,37,8,128]{3,2,1,0:T(8,128)S(1)}, u32[]{:S(2)}, u32[]{:S(2)}) %collective-permute-start.9) | collective-permute-done | bytes 303136 | tf_op jit(solution)/shard_map/ppermute | solution.py:160
  44.0 2.0 %collective-permute-start.12 = (f32[2,27,8,128]{3,2,1,0:T(8,128)S(1)}, f32[2,27,8,128]{3,2,1,0:T(8,128)S(1)}, u32[]{:S(2)}, u32[]{:S(2)}) collective-permute-start(f32[2,27,8,128]{3,2,1,0:T(8,128)S(1)} %pad_maximum_fusion.6), channel_id=1, source_target_pairs={{0,13},{1,12},{2,15},{3,14},{4,9},{5,8},{6,11},{7,10},{8,5},{9,4},... | collective-permute-start | bytes 663560 | tf_op jit(solution)/shard_map/ppermute | solution.py:160
  46.0 3.6 %collective-permute-done.7.refs_7_.refs_8_ = f32[2,37,8,128]{3,2,1,0:T(8,128)S(1)} collective-permute-done((f32[2,37,8,128]{3,2,1,0:T(8,128)S(1)}, f32[2,37,8,128]{3,2,1,0:T(8,128)S(1)}, u32[]{:S(2)}, u32[]{:S(2)}) %collective-permute-start.7) | collective-permute-done | bytes 303136 | tf_op jit(solution)/shard_map/ppermute | solution.py:160
  49.6 1.1 %collective-permute-start.10 = (f32[2,27,8,128]{3,2,1,0:T(8,128)S(1)}, f32[2,27,8,128]{3,2,1,0:T(8,128)S(1)}, u32[]{:S(2)}, u32[]{:S(2)}) collective-permute-start(f32[2,27,8,128]{3,2,1,0:T(8,128)S(1)} %pad_maximum_fusion.4), channel_id=1, source_target_pairs={{0,8},{1,9},{2,10},{3,11},{4,12},{5,13},{6,14},{7,15},{8,0},{9,1},... | collective-permute-start | bytes 663560 | tf_op jit(solution)/shard_map/ppermute | solution.py:160
  50.7 0.0 collective-permute-done.8.refs_8_.refs_9_
  50.7 1.4 %collective-permute-start.11 = (f32[2,27,8,128]{3,2,1,0:T(8,128)S(1)}, f32[2,27,8,128]{3,2,1,0:T(8,128)S(1)}, u32[]{:S(2)}, u32[]{:S(2)}) collective-permute-start(f32[2,27,8,128]{3,2,1,0:T(8,128)S(1)} %pad_maximum_fusion.5), channel_id=1, source_target_pairs={{0,5},{1,4},{2,7},{3,6},{4,1},{5,0},{6,3},{7,2},{8,13},{9,12},{10,... | collective-permute-start | bytes 663560 | tf_op jit(solution)/shard_map/ppermute | solution.py:160
  52.1 0.0 collective-permute-done.1.refs_1_.refs_2_
  52.1 0.0 collective-permute-done.6.refs_6_.refs_7_
  52.1 0.9 %shard_map.79 = (f32[38,8,128]{2,1,0:T(8,128)S(1)}, f32[2,9,2,8,128]{4,3,2,1,0:T(8,128)S(1)}, f32[2,9,2,8,128]{4,3,2,1,0:T(8,128)S(1)}) custom-call(s32[1]{0:T(128)} %bitcast.flat_ref, f32[2,8,128]{2,1,0:T(8,128)S(1)} %bitcast.44, f32[64,8,128]{2,1,0:T(8,128)S(1)} %get-tuple-element.43.refs_0_.refs_1_, ...), custom_call_target="tpu_custom_call" | custom-call | flops 5046276 | bytes 5046276 | tf_op jit(solution)/shard_map/pallas_call | solution.py:565
  53.1 2.6 %collective-permute-start.14 = (f32[38,8,128]{2,1,0:T(8,128)S(1)}, f32[38,8,128]{2,1,0:T(8,128)S(1)}, u32[]{:S(2)}, u32[]{:S(2)}) collective-permute-start(f32[38,8,128]{2,1,0:T(8,128)S(1)} %get-tuple-element.71.mine_ref), channel_id=1, source_target_pairs={{0,16},{1,17},{2,18},{3,19},{4,20},{5,21},{6,22},{7,23},{8,24},{9,... | collective-permute-start | bytes 466952 | tf_op jit(solution)/shard_map/ppermute | solution.py:160
  55.7 0.7 shard_map.80
  56.4 0.0 collective-permute-done.12.refs_2_.refs_12_.refs_13_
  56.4 5.1 %collective-permute-done.10.refs_0_.refs_10_.refs_11_ = f32[2,27,8,128]{3,2,1,0:T(8,128)S(1)} collective-permute-done((f32[2,27,8,128]{3,2,1,0:T(8,128)S(1)}, f32[2,27,8,128]{3,2,1,0:T(8,128)S(1)}, u32[]{:S(2)}, u32[]{:S(2)}) %collective-permute-start.10) | collective-permute-done | bytes 221216 | tf_op jit(solution)/shard_map/ppermute | solution.py:160
  61.5 0.0 collective-permute-done.11.refs_1_.refs_11_.refs_12_
  61.5 0.1 shard_map.81.mine_ref
  61.6 0.3 collective-permute-start.13
  61.9 0.0 collective-permute-done.14.theirs_ref
  61.9 1.4 %shard_map.82 = (f32[18,8,128]{2,1,0:T(8,128)S(1)}, f32[4,2,6,8,128]{4,3,2,1,0:T(8,128)S(1)}, f32[2,9,2,8,128]{4,3,2,1,0:T(8,128)S(1)}) custom-call(s32[1]{0:T(128)} %bitcast.flat_ref, f32[2,8,128]{2,1,0:T(8,128)S(1)} %bitcast.46, f32[38,8,128]{2,1,0:T(8,128)S(1)} %get-tuple-element.71.mine_ref, f32[38,8,128]{2,1,0:T(8,128)S(1)} %collective-permute-done.14.theirs_ref, ...), custom_call_target="tpu_custom_call" | custom-call | flops 5619716 | bytes 5619716 | tf_op jit(solution)/shard_map/pallas_call | solution.py:565
  63.4 2.7 %collective-permute-start.16 = (f32[18,8,128]{2,1,0:T(8,128)S(1)}, f32[18,8,128]{2,1,0:T(8,128)S(1)}, u32[]{:S(2)}, u32[]{:S(2)}) collective-permute-start(f32[18,8,128]{2,1,0:T(8,128)S(1)} %get-tuple-element.76.mine_ref), channel_id=1, source_target_pairs={{0,16},{1,17},{2,18},{3,19},{4,20},{5,21},{6,22},{7,23},{8,24},{9,... | collective-permute-start | bytes 221192 | tf_op jit(solution)/shard_map/ppermute | solution.py:160
  66.1 1.5 %collective-permute-done.13.theirs_ref = f32[18,8,128]{2,1,0:T(8,128)S(1)} collective-permute-done((f32[18,8,128]{2,1,0:T(8,128)S(1)}, f32[18,8,128]{2,1,0:T(8,128)S(1)}, u32[]{:S(2)}, u32[]{:S(2)}) %collective-permute-start.13) | collective-permute-done | bytes 73760 | tf_op jit(solution)/shard_map/ppermute | solution.py:160
  67.6 1.3 %shard_map.83 = (f32[18,8,128]{2,1,0:T(8,128)S(1)}, f32[4,2,6,8,128]{4,3,2,1,0:T(8,128)S(1)}) custom-call(s32[1]{0:T(128)} %bitcast.flat_ref, f32[2,8,128]{2,1,0:T(8,128)S(1)} %bitcast.47, f32[18,8,128]{2,1,0:T(8,128)S(1)} %shard_map.81.mine_ref, f32[18,8,128]{2,1,0:T(8,128)S(1)} %collective-permute-done.13.theirs_ref, ...), custom_call_target="tpu_custom_call" | custom-call | flops 5971972 | bytes 5971972 | tf_op jit(solution)/shard_map/pallas_call | solution.py:565
  68.9 0.1 collective-permute-start.15
  69.0 0.3 collective-permute-done.16.theirs_ref
  69.3 0.7 shard_map.84.refs_0_
  70.1 5.0 %collective-permute-done.15.theirs_ref = f32[18,8,128]{2,1,0:T(8,128)S(1)} collective-permute-done((f32[18,8,128]{2,1,0:T(8,128)S(1)}, f32[18,8,128]{2,1,0:T(8,128)S(1)}, u32[]{:S(2)}, u32[]{:S(2)}) %collective-permute-start.15) | collective-permute-done | bytes 73760 | tf_op jit(solution)/shard_map/ppermute | solution.py:160
  75.0 0.8 shard_map.85
  75.8 12.7 %all_to_all.5.back_ref = f32[16,8,8,128]{3,2,1,0:T(8,128)S(1)} all-to-all(f32[16,8,8,128]{3,2,1,0:T(8,128)S(1)} %shard_map.85), channel_id=1, replica_groups={{0,1,2,3,4,5,6,7,8,9,10,11,12,13,14,15},{16,17,18,19,20,21,22,23,24,25,..., dimensions={0} | all-to-all | bytes 1048576 | tf_op jit(solution)/shard_map/all_to_all | solution.py:674
  88.5 1.0 %shard_map.86 = (f32[3,32,4,256]{3,2,1,0:T(4,128)}, f32[18,4,256]{2,1,0:T(4,128)}) custom-call(s32[1]{0:T(128)} %bitcast.flat_ref, f32[16,8,8,128]{3,2,1,0:T(8,128)S(1)} %all_to_all.5.back_ref), custom_call_target="tpu_custom_call" | custom-call | flops 991236 | bytes 991236 | tf_op jit(solution)/shard_map/pallas_call | solution.py:565
  (28 shorter events, 0.3 us)
Async XLA Ops:
  0.6 7.3 %copy-start.5 = (s32[3,1,64]{2,1,0:T(1,128)S(1)}, s32[3,1,64]{2,1,0:T(1,128)}, u32[]{:S(2)}) copy-start(s32[3,1,64]{2,1,0:T(1,128)} %refs_4_.3) | copy-start | bytes 2308
  0.6 7.3 %copy-start.2 = (f32[2,4,256]{2,1,0:T(4,128)S(1)}, f32[2,4,256]{2,1,0:T(4,128)}, u32[]{:S(2)}) copy-start(f32[2,4,256]{2,1,0:T(4,128)} %param.10) | copy-start | bytes 24580
  0.7 7.3 %copy-start.4 = (f32[18,4,256]{2,1,0:T(4,128)S(1)}, f32[18,4,256]{2,1,0:T(4,128)}, u32[]{:S(2)}) copy-start(f32[18,4,256]{2,1,0:T(4,128)} %param.9) | copy-start | bytes 221188
  0.7 7.3 %copy-start.3 = (f32[18,4,256]{2,1,0:T(4,128)S(1)}, f32[18,4,256]{2,1,0:T(4,128)}, u32[]{:S(2)}) copy-start(f32[18,4,256]{2,1,0:T(4,128)} %param.8) | copy-start | bytes 221188
  0.7 7.3 %copy-start.1 = (f32[3,32,4,256]{3,2,1,0:T(4,128)S(1)}, f32[3,32,4,256]{3,2,1,0:T(4,128)}, u32[]{:S(2)}) copy-start(f32[3,32,4,256]{3,2,1,0:T(4,128)} %param.7) | copy-start | bytes 1179652
  0.7 7.3 %copy-start = (bf16[3,3,3,32,4,256]{5,4,3,2,1,0:T(4,128)(2,1)S(1)}, bf16[3,3,3,32,4,256]{5,4,3,2,1,0:T(4,128)(2,1)}, u32[]{:S(2)}) copy-start(bf16[3,3,3,32,4,256]{5,4,3,2,1,0:T(4,128)(2,1)} %param.6) | copy-start | bytes 5308420
  2.4 16.8 %collective-permute-start = (f32[2,64,8,128]{3,2,1,0:T(8,128)S(1)}, f32[2,64,8,128]{3,2,1,0:T(8,128)S(1)}, u32[]{:S(2)}, u32[]{:S(2)}) collective-permute-start(f32[2,64,8,128]{3,2,1,0:T(8,128)S(1)} %get-tuple-element.44), channel_id=1, source_target_pairs={{0,12},{1,13},{2,14},{3,15},{4,8},{5,9},{6,10},{7,11},{8,4},{9,5},... | collective-permute-start | bytes 1572872 | tf_op jit(solution)/shard_map/ppermute | solution.py:160
  6.4 24.8 %collective-permute-start.2 = (f32[2,65,8,128]{3,2,1,0:T(8,128)S(1)}, f32[2,65,8,128]{3,2,1,0:T(8,128)S(1)}, u32[]{:S(2)}, u32[]{:S(2)}) collective-permute-start(f32[2,65,8,128]{3,2,1,0:T(8,128)S(1)} %get-tuple-element.47), channel_id=1, source_target_pairs={{0,1},{1,0},{2,3},{3,2},{4,5},{5,4},{6,7},{7,6},{8,9},{9,8},{10,11... | collective-permute-start | bytes 1597448 | tf_op jit(solution)/shard_map/ppermute | solution.py:160
  8.6 22.3 %collective-permute-start.3 = (f32[2,64,8,128]{3,2,1,0:T(8,128)S(1)}, f32[2,64,8,128]{3,2,1,0:T(8,128)S(1)}, u32[]{:S(2)}, u32[]{:S(2)}) collective-permute-start(f32[2,64,8,128]{3,2,1,0:T(8,128)S(1)} %get-tuple-element.48), channel_id=1, source_target_pairs={{0,9},{1,8},{2,11},{3,10},{4,13},{5,12},{6,15},{7,14},{8,1},{9,0},... | collective-permute-start | bytes 1572872 | tf_op jit(solution)/shard_map/ppermute | solution.py:160
  9.0 20.5 %collective-permute-start.5 = (f32[2,64,8,128]{3,2,1,0:T(8,128)S(1)}, f32[2,64,8,128]{3,2,1,0:T(8,128)S(1)}, u32[]{:S(2)}, u32[]{:S(2)}) collective-permute-start(f32[2,64,8,128]{3,2,1,0:T(8,128)S(1)} %get-tuple-element.55), channel_id=1, source_target_pairs={{0,4},{1,5},{2,6},{3,7},{4,0},{5,1},{6,2},{7,3},{8,12},{9,13},{10,... | collective-permute-start | bytes 1572872 | tf_op jit(solution)/shard_map/ppermute | solution.py:160
  9.3 9.9 %collective-permute-start.4 = (f32[3,64,8,128]{3,2,1,0:T(8,128)S(1)}, f32[3,64,8,128]{3,2,1,0:T(8,128)S(1)}, u32[]{:S(2)}, u32[]{:S(2)}) collective-permute-start(f32[3,64,8,128]{3,2,1,0:T(8,128)S(1)} %get-tuple-element.50), channel_id=1, source_target_pairs={{0,2},{1,3},{2,0},{3,1},{4,6},{5,7},{6,4},{7,5},{8,10},{9,11},{10,... | collective-permute-start | bytes 2359304 | tf_op jit(solution)/shard_map/ppermute | solution.py:160
  31.4 20.7 %collective-permute-start.6 = (f32[4,64,8,128]{3,2,1,0:T(8,128)S(1)}, f32[4,64,8,128]{3,2,1,0:T(8,128)S(1)}, u32[]{:S(2)}, u32[]{:S(2)}) collective-permute-start(f32[4,64,8,128]{3,2,1,0:T(8,128)S(1)} %pad_maximum_fusion), channel_id=1, source_target_pairs={{0,2},{1,3},{2,0},{3,1},{4,6},{5,7},{6,4},{7,5},{8,10},{9,11},{10,... | collective-permute-start | bytes 3145736 | tf_op jit(solution)/shard_map/ppermute | solution.py:160
  31.5 20.6 %collective-permute-start.1 = (f32[64,8,128]{2,1,0:T(8,128)S(1)}, f32[64,8,128]{2,1,0:T(8,128)S(1)}, u32[]{:S(2)}, u32[]{:S(2)}) collective-permute-start(f32[64,8,128]{2,1,0:T(8,128)S(1)} %get-tuple-element.46), channel_id=1, source_target_pairs={{0,2},{1,3},{2,0},{3,1},{4,6},{5,7},{6,4},{7,5},{8,10},{9,11},{10,... | collective-permute-start | bytes 786440 | tf_op jit(solution)/shard_map/ppermute | solution.py:160
  32.1 11.9 %collective-permute-start.9 = (f32[2,37,8,128]{3,2,1,0:T(8,128)S(1)}, f32[2,37,8,128]{3,2,1,0:T(8,128)S(1)}, u32[]{:S(2)}, u32[]{:S(2)}) collective-permute-start(f32[2,37,8,128]{3,2,1,0:T(8,128)S(1)} %pad_maximum_fusion.1), channel_id=1, source_target_pairs={{0,13},{1,12},{2,15},{3,14},{4,9},{5,8},{6,11},{7,10},{8,5},{9,4},... | collective-permute-start | bytes 909320 | tf_op jit(solution)/shard_map/ppermute | solution.py:160
  34.1 15.5 %collective-permute-start.7 = (f32[2,37,8,128]{3,2,1,0:T(8,128)S(1)}, f32[2,37,8,128]{3,2,1,0:T(8,128)S(1)}, u32[]{:S(2)}, u32[]{:S(2)}) collective-permute-start(f32[2,37,8,128]{3,2,1,0:T(8,128)S(1)} %pad_maximum_fusion.2), channel_id=1, source_target_pairs={{0,8},{1,9},{2,10},{3,11},{4,12},{5,13},{6,14},{7,15},{8,0},{9,1},... | collective-permute-start | bytes 909320 | tf_op jit(solution)/shard_map/ppermute | solution.py:160
  35.0 15.7 %collective-permute-start.8 = (f32[2,37,8,128]{3,2,1,0:T(8,128)S(1)}, f32[2,37,8,128]{3,2,1,0:T(8,128)S(1)}, u32[]{:S(2)}, u32[]{:S(2)}) collective-permute-start(f32[2,37,8,128]{3,2,1,0:T(8,128)S(1)} %pad_maximum_fusion.3), channel_id=1, source_target_pairs={{0,5},{1,4},{2,7},{3,6},{4,1},{5,0},{6,3},{7,2},{8,13},{9,12},{10,... | collective-permute-start | bytes 909320 | tf_op jit(solution)/shard_map/ppermute | solution.py:160
  44.0 12.5 %collective-permute-start.12 = (f32[2,27,8,128]{3,2,1,0:T(8,128)S(1)}, f32[2,27,8,128]{3,2,1,0:T(8,128)S(1)}, u32[]{:S(2)}, u32[]{:S(2)}) collective-permute-start(f32[2,27,8,128]{3,2,1,0:T(8,128)S(1)} %pad_maximum_fusion.6), channel_id=1, source_target_pairs={{0,13},{1,12},{2,15},{3,14},{4,9},{5,8},{6,11},{7,10},{8,5},{9,4},... | collective-permute-start | bytes 663560 | tf_op jit(solution)/shard_map/ppermute | solution.py:160
  49.6 11.9 %collective-permute-start.10 = (f32[2,27,8,128]{3,2,1,0:T(8,128)S(1)}, f32[2,27,8,128]{3,2,1,0:T(8,128)S(1)}, u32[]{:S(2)}, u32[]{:S(2)}) collective-permute-start(f32[2,27,8,128]{3,2,1,0:T(8,128)S(1)} %pad_maximum_fusion.4), channel_id=1, source_target_pairs={{0,8},{1,9},{2,10},{3,11},{4,12},{5,13},{6,14},{7,15},{8,0},{9,1},... | collective-permute-start | bytes 663560 | tf_op jit(solution)/shard_map/ppermute | solution.py:160
  50.7 10.8 %collective-permute-start.11 = (f32[2,27,8,128]{3,2,1,0:T(8,128)S(1)}, f32[2,27,8,128]{3,2,1,0:T(8,128)S(1)}, u32[]{:S(2)}, u32[]{:S(2)}) collective-permute-start(f32[2,27,8,128]{3,2,1,0:T(8,128)S(1)} %pad_maximum_fusion.5), channel_id=1, source_target_pairs={{0,5},{1,4},{2,7},{3,6},{4,1},{5,0},{6,3},{7,2},{8,13},{9,12},{10,... | collective-permute-start | bytes 663560 | tf_op jit(solution)/shard_map/ppermute | solution.py:160
  53.1 8.9 %collective-permute-start.14 = (f32[38,8,128]{2,1,0:T(8,128)S(1)}, f32[38,8,128]{2,1,0:T(8,128)S(1)}, u32[]{:S(2)}, u32[]{:S(2)}) collective-permute-start(f32[38,8,128]{2,1,0:T(8,128)S(1)} %get-tuple-element.71.mine_ref), channel_id=1, source_target_pairs={{0,16},{1,17},{2,18},{3,19},{4,20},{5,21},{6,22},{7,23},{8,24},{9,... | collective-permute-start | bytes 466952 | tf_op jit(solution)/shard_map/ppermute | solution.py:160
  61.6 6.0 %collective-permute-start.13 = (f32[18,8,128]{2,1,0:T(8,128)S(1)}, f32[18,8,128]{2,1,0:T(8,128)S(1)}, u32[]{:S(2)}, u32[]{:S(2)}) collective-permute-start(f32[18,8,128]{2,1,0:T(8,128)S(1)} %shard_map.81.mine_ref), channel_id=1, source_target_pairs={{0,16},{1,17},{2,18},{3,19},{4,20},{5,21},{6,22},{7,23},{8,24},{9,... | collective-permute-start | bytes 221192 | tf_op jit(solution)/shard_map/ppermute | solution.py:160
  63.4 6.0 %collective-permute-start.16 = (f32[18,8,128]{2,1,0:T(8,128)S(1)}, f32[18,8,128]{2,1,0:T(8,128)S(1)}, u32[]{:S(2)}, u32[]{:S(2)}) collective-permute-start(f32[18,8,128]{2,1,0:T(8,128)S(1)} %get-tuple-element.76.mine_ref), channel_id=1, source_target_pairs={{0,16},{1,17},{2,18},{3,19},{4,20},{5,21},{6,22},{7,23},{8,24},{9,... | collective-permute-start | bytes 221192 | tf_op jit(solution)/shard_map/ppermute | solution.py:160
  68.9 6.1 %collective-permute-start.15 = (f32[18,8,128]{2,1,0:T(8,128)S(1)}, f32[18,8,128]{2,1,0:T(8,128)S(1)}, u32[]{:S(2)}, u32[]{:S(2)}) collective-permute-start(f32[18,8,128]{2,1,0:T(8,128)S(1)} %get-tuple-element.74.mine_ref), channel_id=1, source_target_pairs={{0,16},{1,17},{2,18},{3,19},{4,20},{5,21},{6,22},{7,23},{8,24},{9,... | collective-permute-start | bytes 221192 | tf_op jit(solution)/shard_map/ppermute | solution.py:160

commit v5 on v3

--- a/solution.py
+++ b/solution.py
@@ -535,29 +535,38 @@
     out[at + (slice(None), slice(LANES, 2 * LANES))] = block[..., rows:, :]
 
 
-def place_kernel(size, flat_ref, back_ref, alpha_ref, misfit_ref):
+def place_kernel(size, flat_ref, back_ref, alpha_hbm, misfit_hbm, alpha_ref, misfit_ref, sems):
     mem_index = lax.div(flat_ref[0], 2)
     for source in range(GROUP):
         for chunk in range(size.chunks):
-            base = chunk * (size.members + 1)
-            level = source + chunk * GROUP
-            for member in range(size.members):
-                unfold_into(alpha_ref, (member, level), back_ref[source, base + member])
-            row, inside, _ = row_in_block(size, level, mem_index)
+            slot = chunk * (size.members + 1) + size.members
+            row, inside, _ = row_in_block(size, source + chunk * GROUP, mem_index)
 
             @pl.when(inside)
-            def _(source=source, base=base, row=row):
-                unfold_into(misfit_ref, (row,), back_ref[source, base + size.members])
-
-
-def call(kernel, outs, operands, scratch=(), spaces=None, limit=24):
+            def _(source=source, slot=slot, row=row):
+                unfold_into(misfit_ref, (row,), back_ref[source, slot])
+
+    copies = [pltpu.make_async_copy(misfit_ref, misfit_hbm, sems.at[size.members])]
+    copies[0].start()
+    for member in range(size.members):
+        for source in range(GROUP):
+            for chunk in range(size.chunks):
+                block = back_ref[source, chunk * (size.members + 1) + member]
+                unfold_into(alpha_ref, (member, source + chunk * GROUP), block)
+        copies.append(pltpu.make_async_copy(alpha_ref.at[member], alpha_hbm.at[member], sems.at[member]))
+        copies[-1].start()
+    for copy in copies:
+        copy.wait()
+
+
+def call(kernel, outs, operands, scratch=(), spaces=None, out_space=pltpu.VMEM, limit=24):
     spaces = spaces or [pltpu.VMEM] * len(operands)
     moved = 4 * sum(math.prod(shape) for shape in outs) + sum(x.size * x.dtype.itemsize for x in operands)
     return pl.pallas_call(
         kernel,
         out_shape=[jax.ShapeDtypeStruct(shape, jnp.float32) for shape in outs],
         in_specs=[pl.BlockSpec(memory_space=space) for space in [pltpu.SMEM] + spaces[1:]],
-        out_specs=[pl.BlockSpec(memory_space=pltpu.VMEM)] * len(outs),
+        out_specs=[pl.BlockSpec(memory_space=out_space)] * len(outs),
         scratch_shapes=scratch,
         cost_estimate=pl.CostEstimate(flops=moved, bytes_accessed=moved, transcendentals=0),
         compiler_params=pltpu.CompilerParams(vmem_limit_bytes=limit * 1024 * 1024),
@@ -666,11 +675,14 @@
         )
     groups = [[half * GROUP + place for place in range(GROUP)] for half in range(2)]
     back = lax.all_to_all(back, ("mem", "lat"), 0, 0, axis_index_groups=groups, tiled=True)
+    places = [(size.members, levels, rows, lon_cells), (size.owned, rows, lon_cells)]
     return tuple(
         call(
             functools.partial(place_kernel, size),
-            [(size.members, levels, rows, lon_cells), (size.owned, rows, lon_cells)],
+            places,
             (flat, back),
+            [*(pltpu.VMEM(place, jnp.float32) for place in places), pltpu.SemaphoreType.DMA((size.members + 1,))],
+            out_space=pltpu.HBM,
         )
     )
 

time: 89.6 us -> 89.7 us (level)
  no operation moved by 1% of the time
where the time goes in v5:
time: 89.7 us; the launch traced here: 89.4 us
  waiting for transfers between devices  42.4 us (47%)
  starting transfers between devices  21.5 us (24%)
  blocking collectives  13.2 us (15%)
  Pallas kernels  11.1 us (12%)
    ppermute x17, waiting for transfers between devices, shift_by(): return lax.ppermute(cells, axes, [(i, i ^ mask) for i in range(count)])  42.4 us
    ppermute x17, starting transfers between devices, shift_by(): return lax.ppermute(cells, axes, [(i, i ^ mask) for i in range(count)])  21.5 us
    all_to_all x1, blocking collectives, level_shards(): lax.all_to_all(back, ('mem', 'lat'), 0, 0, axis_index_groups=groups, tile...  13.2 us
    pallas_call x10, Pallas kernels, call(): pl.pallas_call(kernel, out_shape=[jax.ShapeDtypeStruct(shape, jnp.float32...  11.1 us
  transfers between devices with their start and end apart: 17, of which 10 were waited for; matrix products, arithmetic and copies ran while one was open for 0% of the time, Pallas kernels for 9%

profile of v5, /device:TPU:0, one launch (start us, length us, event | category | flops | bytes accessed | tf_op | source)
XLA Modules:
  0.0 89.4 jit_solution(1751029047309208929)
XLA Ops:
  0.6 1.5 %shard_map.77 = (f32[2,65,8,128]{3,2,1,0:T(8,128)S(1)}, f32[2,64,8,128]{3,2,1,0:T(8,128)S(1)}) custom-call(s32[1]{0:T(128)} %bitcast.flat_ref, bf16[27,32,8,128]{3,2,1,0:T(8,128)(2,1)} %bitcast.46, f32[3,32,8,128]{3,2,1,0:T(8,128)} %bitcast.48, f32[18,8,128]{2,1,0:T(8,128)} %bitcast.50, f32[18,8,128]{2,1,0:T(8,128)} %bitcast.52, s32[3,1,64]{2,1,0:T(1,128)} %mask_hbm.3, ...), custom_call_target="tpu_custom_call" | custom-call | flops 3375876 | bytes 3375876 | tf_op jit(solution)/shard_map/pallas_call | solution.py:565
  2.2 4.0 %collective-permute-start.4 = (f32[2,64,8,128]{3,2,1,0:T(8,128)S(1)}, f32[2,64,8,128]{3,2,1,0:T(8,128)S(1)}, u32[]{:S(2)}, u32[]{:S(2)}) collective-permute-start(f32[2,64,8,128]{3,2,1,0:T(8,128)S(1)} %get-tuple-element.48), channel_id=1, source_target_pairs={{0,12},{1,13},{2,14},{3,15},{4,8},{5,9},{6,10},{7,11},{8,4},{9,5},... | collective-permute-start | bytes 1572872 | tf_op jit(solution)/shard_map/ppermute | solution.py:160
  6.2 1.5 %collective-permute-start.1 = (f32[2,65,8,128]{3,2,1,0:T(8,128)S(1)}, f32[2,65,8,128]{3,2,1,0:T(8,128)S(1)}, u32[]{:S(2)}, u32[]{:S(2)}) collective-permute-start(f32[2,65,8,128]{3,2,1,0:T(8,128)S(1)} %get-tuple-element.43), channel_id=1, source_target_pairs={{0,1},{1,0},{2,3},{3,2},{4,5},{5,4},{6,7},{7,6},{8,9},{9,8},{10,11... | collective-permute-start | bytes 1597448 | tf_op jit(solution)/shard_map/ppermute | solution.py:160
  7.7 2.6 %shard_map.78 = (f32[2,64,8,128]{3,2,1,0:T(8,128)S(1)}, f32[2,64,8,128]{3,2,1,0:T(8,128)S(1)}, f32[64,8,128]{2,1,0:T(8,128)S(1)}, f32[64,8,128]{2,1,0:T(8,128)S(...) custom-call(s32[1]{0:T(128)} %bitcast.flat_ref, ...), custom_call_target="tpu_custom_call" | custom-call | flops 5464836 | bytes 5464836 | tf_op jit(solution)/shard_map/pallas_call | solution.py:565
  10.3 0.1 collective-permute-start
  10.4 0.6 collective-permute-start.5
  11.0 0.2 collective-permute-start.3
  11.2 2.0 %collective-permute-done.3 = f32[3,64,8,128]{3,2,1,0:T(8,128)S(1)} collective-permute-done((f32[3,64,8,128]{3,2,1,0:T(8,128)S(1)}, f32[3,64,8,128]{3,2,1,0:T(8,128)S(1)}, u32[]{:S(2)}, u32[]{:S(2)}) %collective-permute-start.3) | collective-permute-done | bytes 786464 | tf_op jit(solution)/shard_map/ppermute | solution.py:160
  13.3 0.2 collective-permute-start.2
  13.5 15.9 %collective-permute-done.5.refs_4_.refs_5_ = f32[2,64,8,128]{3,2,1,0:T(8,128)S(1)} collective-permute-done((f32[2,64,8,128]{3,2,1,0:T(8,128)S(1)}, f32[2,64,8,128]{3,2,1,0:T(8,128)S(1)}, u32[]{:S(2)}, u32[]{:S(2)}) %collective-permute-start.5) | collective-permute-done | bytes 524320 | tf_op jit(solution)/shard_map/ppermute | solution.py:160
  29.4 0.0 collective-permute-done.4.refs_3_.refs_4_
  29.4 1.2 %collective-permute-done.2.refs_5_.refs_6_ = f32[2,64,8,128]{3,2,1,0:T(8,128)S(1)} collective-permute-done((f32[2,64,8,128]{3,2,1,0:T(8,128)S(1)}, f32[2,64,8,128]{3,2,1,0:T(8,128)S(1)}, u32[]{:S(2)}, u32[]{:S(2)}) %collective-permute-start.2) | collective-permute-done | bytes 524320 | tf_op jit(solution)/shard_map/ppermute | solution.py:160
  30.6 0.4 collective-permute-done.1.refs_2_.refs_3_
  31.1 0.0 copy-start
  31.1 0.1 pad_maximum_fusion
  31.2 0.1 collective-permute-start.6
  31.3 2.2 %collective-permute-start.9 = (f32[2,37,8,128]{3,2,1,0:T(8,128)S(1)}, f32[2,37,8,128]{3,2,1,0:T(8,128)S(1)}, u32[]{:S(2)}, u32[]{:S(2)}) collective-permute-start(f32[2,37,8,128]{3,2,1,0:T(8,128)S(1)} %pad_maximum_fusion.1), channel_id=1, source_target_pairs={{0,13},{1,12},{2,15},{3,14},{4,9},{5,8},{6,11},{7,10},{8,5},{9,4},... | collective-permute-start | bytes 909320 | tf_op jit(solution)/shard_map/ppermute | solution.py:160
  33.5 0.9 collective-permute-start.7
  34.3 1.4 %collective-permute-start.8 = (f32[2,37,8,128]{3,2,1,0:T(8,128)S(1)}, f32[2,37,8,128]{3,2,1,0:T(8,128)S(1)}, u32[]{:S(2)}, u32[]{:S(2)}) collective-permute-start(f32[2,37,8,128]{3,2,1,0:T(8,128)S(1)} %pad_maximum_fusion.3), channel_id=1, source_target_pairs={{0,5},{1,4},{2,7},{3,6},{4,1},{5,0},{6,3},{7,2},{8,13},{9,12},{10,... | collective-permute-start | bytes 909320 | tf_op jit(solution)/shard_map/ppermute | solution.py:160
  35.9 7.3 %collective-permute-done.9.refs_9_.refs_10_ = f32[2,37,8,128]{3,2,1,0:T(8,128)S(1)} collective-permute-done((f32[2,37,8,128]{3,2,1,0:T(8,128)S(1)}, f32[2,37,8,128]{3,2,1,0:T(8,128)S(1)}, u32[]{:S(2)}, u32[]{:S(2)}) %collective-permute-start.9) | collective-permute-done | bytes 303136 | tf_op jit(solution)/shard_map/ppermute | solution.py:160
  43.2 2.1 %collective-permute-start.12 = (f32[2,27,8,128]{3,2,1,0:T(8,128)S(1)}, f32[2,27,8,128]{3,2,1,0:T(8,128)S(1)}, u32[]{:S(2)}, u32[]{:S(2)}) collective-permute-start(f32[2,27,8,128]{3,2,1,0:T(8,128)S(1)} %pad_maximum_fusion.6), channel_id=1, source_target_pairs={{0,13},{1,12},{2,15},{3,14},{4,9},{5,8},{6,11},{7,10},{8,5},{9,4},... | collective-permute-start | bytes 663560 | tf_op jit(solution)/shard_map/ppermute | solution.py:160
  45.3 3.5 %collective-permute-done.7.refs_7_.refs_8_ = f32[2,37,8,128]{3,2,1,0:T(8,128)S(1)} collective-permute-done((f32[2,37,8,128]{3,2,1,0:T(8,128)S(1)}, f32[2,37,8,128]{3,2,1,0:T(8,128)S(1)}, u32[]{:S(2)}, u32[]{:S(2)}) %collective-permute-start.7) | collective-permute-done | bytes 303136 | tf_op jit(solution)/shard_map/ppermute | solution.py:160
  48.8 1.2 %collective-permute-start.10 = (f32[2,27,8,128]{3,2,1,0:T(8,128)S(1)}, f32[2,27,8,128]{3,2,1,0:T(8,128)S(1)}, u32[]{:S(2)}, u32[]{:S(2)}) collective-permute-start(f32[2,27,8,128]{3,2,1,0:T(8,128)S(1)} %pad_maximum_fusion.4), channel_id=1, source_target_pairs={{0,8},{1,9},{2,10},{3,11},{4,12},{5,13},{6,14},{7,15},{8,0},{9,1},... | collective-permute-start | bytes 663560 | tf_op jit(solution)/shard_map/ppermute | solution.py:160
  50.0 0.0 collective-permute-done.8.refs_8_.refs_9_
  50.0 1.4 %collective-permute-start.11 = (f32[2,27,8,128]{3,2,1,0:T(8,128)S(1)}, f32[2,27,8,128]{3,2,1,0:T(8,128)S(1)}, u32[]{:S(2)}, u32[]{:S(2)}) collective-permute-start(f32[2,27,8,128]{3,2,1,0:T(8,128)S(1)} %pad_maximum_fusion.5), channel_id=1, source_target_pairs={{0,5},{1,4},{2,7},{3,6},{4,1},{5,0},{6,3},{7,2},{8,13},{9,12},{10,... | collective-permute-start | bytes 663560 | tf_op jit(solution)/shard_map/ppermute | solution.py:160
  51.4 0.0 collective-permute-done.refs_1_.refs_2_
  51.4 0.0 collective-permute-done.6.refs_6_.refs_7_
  51.4 0.0 copy-done
  51.4 0.9 %shard_map.79 = (f32[38,8,128]{2,1,0:T(8,128)S(1)}, f32[2,9,2,8,128]{4,3,2,1,0:T(8,128)S(1)}, f32[2,9,2,8,128]{4,3,2,1,0:T(8,128)S(1)}) custom-call(s32[1]{0:T(128)} %bitcast.flat_ref, f32[2,8,128]{2,1,0:T(8,128)S(1)} %bitcast.40, f32[64,8,128]{2,1,0:T(8,128)S(1)} %get-tuple-element.41.refs_0_.refs_1_, ...), custom_call_target="tpu_custom_call" | custom-call | flops 5046276 | bytes 5046276 | tf_op jit(solution)/shard_map/pallas_call | solution.py:565
  52.3 2.6 %collective-permute-start.14 = (f32[38,8,128]{2,1,0:T(8,128)S(1)}, f32[38,8,128]{2,1,0:T(8,128)S(1)}, u32[]{:S(2)}, u32[]{:S(2)}) collective-permute-start(f32[38,8,128]{2,1,0:T(8,128)S(1)} %get-tuple-element.67.mine_ref), channel_id=1, source_target_pairs={{0,16},{1,17},{2,18},{3,19},{4,20},{5,21},{6,22},{7,23},{8,24},{9,... | collective-permute-start | bytes 466952 | tf_op jit(solution)/shard_map/ppermute | solution.py:160
  55.0 0.7 shard_map.80
  55.7 0.0 collective-permute-done.12.refs_2_.refs_12_.refs_13_
  55.7 5.6 %collective-permute-done.10.refs_0_.refs_10_.refs_11_ = f32[2,27,8,128]{3,2,1,0:T(8,128)S(1)} collective-permute-done((f32[2,27,8,128]{3,2,1,0:T(8,128)S(1)}, f32[2,27,8,128]{3,2,1,0:T(8,128)S(1)}, u32[]{:S(2)}, u32[]{:S(2)}) %collective-permute-start.10) | collective-permute-done | bytes 221216 | tf_op jit(solution)/shard_map/ppermute | solution.py:160
  61.2 0.0 collective-permute-done.11.refs_1_.refs_11_.refs_12_
  61.2 0.1 shard_map.81.mine_ref
  61.3 0.4 collective-permute-start.13
  61.7 0.0 collective-permute-done.14.theirs_ref
  61.7 1.4 %shard_map.82 = (f32[18,8,128]{2,1,0:T(8,128)S(1)}, f32[4,2,6,8,128]{4,3,2,1,0:T(8,128)S(1)}, f32[2,9,2,8,128]{4,3,2,1,0:T(8,128)S(1)}) custom-call(s32[1]{0:T(128)} %bitcast.flat_ref, f32[2,8,128]{2,1,0:T(8,128)S(1)} %bitcast.42, f32[38,8,128]{2,1,0:T(8,128)S(1)} %get-tuple-element.67.mine_ref, f32[38,8,128]{2,1,0:T(8,128)S(1)} %collective-permute-done.14.theirs_ref, ...), custom_call_target="tpu_custom_call" | custom-call | flops 5619716 | bytes 5619716 | tf_op jit(solution)/shard_map/pallas_call | solution.py:565
  63.1 2.7 %collective-permute-start.16 = (f32[18,8,128]{2,1,0:T(8,128)S(1)}, f32[18,8,128]{2,1,0:T(8,128)S(1)}, u32[]{:S(2)}, u32[]{:S(2)}) collective-permute-start(f32[18,8,128]{2,1,0:T(8,128)S(1)} %get-tuple-element.72.mine_ref), channel_id=1, source_target_pairs={{0,16},{1,17},{2,18},{3,19},{4,20},{5,21},{6,22},{7,23},{8,24},{9,... | collective-permute-start | bytes 221192 | tf_op jit(solution)/shard_map/ppermute | solution.py:160
  65.8 1.7 %collective-permute-done.13.theirs_ref = f32[18,8,128]{2,1,0:T(8,128)S(1)} collective-permute-done((f32[18,8,128]{2,1,0:T(8,128)S(1)}, f32[18,8,128]{2,1,0:T(8,128)S(1)}, u32[]{:S(2)}, u32[]{:S(2)}) %collective-permute-start.13) | collective-permute-done | bytes 73760 | tf_op jit(solution)/shard_map/ppermute | solution.py:160
  67.5 1.3 %shard_map.83 = (f32[18,8,128]{2,1,0:T(8,128)S(1)}, f32[4,2,6,8,128]{4,3,2,1,0:T(8,128)S(1)}) custom-call(s32[1]{0:T(128)} %bitcast.flat_ref, f32[2,8,128]{2,1,0:T(8,128)S(1)} %bitcast.43, f32[18,8,128]{2,1,0:T(8,128)S(1)} %shard_map.81.mine_ref, f32[18,8,128]{2,1,0:T(8,128)S(1)} %collective-permute-done.13.theirs_ref, ...), custom_call_target="tpu_custom_call" | custom-call | flops 5971972 | bytes 5971972 | tf_op jit(solution)/shard_map/pallas_call | solution.py:565
  68.9 0.1 collective-permute-start.15
  69.0 0.7 collective-permute-done.16.theirs_ref
  69.7 0.7 shard_map.84.refs_0_
  70.4 4.0 %collective-permute-done.15.theirs_ref = f32[18,8,128]{2,1,0:T(8,128)S(1)} collective-permute-done((f32[18,8,128]{2,1,0:T(8,128)S(1)}, f32[18,8,128]{2,1,0:T(8,128)S(1)}, u32[]{:S(2)}, u32[]{:S(2)}) %collective-permute-start.15) | collective-permute-done | bytes 73760 | tf_op jit(solution)/shard_map/ppermute | solution.py:160
  74.4 0.8 shard_map.85
  75.2 13.2 %all_to_all.5.back_ref = f32[16,8,8,128]{3,2,1,0:T(8,128)S(1)} all-to-all(f32[16,8,8,128]{3,2,1,0:T(8,128)S(1)} %shard_map.85), channel_id=1, replica_groups={{0,1,2,3,4,5,6,7,8,9,10,11,12,13,14,15},{16,17,18,19,20,21,22,23,24,25,..., dimensions={0} | all-to-all | bytes 1048576 | tf_op jit(solution)/shard_map/all_to_all | solution.py:677
  88.4 1.0 %shard_map.86 = (f32[3,32,4,256]{3,2,1,0:T(4,128)}, f32[18,4,256]{2,1,0:T(4,128)}) custom-call(s32[1]{0:T(128)} %bitcast.flat_ref, f32[16,8,8,128]{3,2,1,0:T(8,128)S(1)} %all_to_all.5.back_ref), custom_call_target="tpu_custom_call" | custom-call | flops 991236 | bytes 991236 | tf_op jit(solution)/shard_map/pallas_call | solution.py:565
  (18 shorter events, 0.3 us)
Async XLA Ops:
  2.2 27.2 %collective-permute-start.4 = (f32[2,64,8,128]{3,2,1,0:T(8,128)S(1)}, f32[2,64,8,128]{3,2,1,0:T(8,128)S(1)}, u32[]{:S(2)}, u32[]{:S(2)}) collective-permute-start(f32[2,64,8,128]{3,2,1,0:T(8,128)S(1)} %get-tuple-element.48), channel_id=1, source_target_pairs={{0,12},{1,13},{2,14},{3,15},{4,8},{5,9},{6,10},{7,11},{8,4},{9,5},... | collective-permute-start | bytes 1572872 | tf_op jit(solution)/shard_map/ppermute | solution.py:160
  6.2 24.8 %collective-permute-start.1 = (f32[2,65,8,128]{3,2,1,0:T(8,128)S(1)}, f32[2,65,8,128]{3,2,1,0:T(8,128)S(1)}, u32[]{:S(2)}, u32[]{:S(2)}) collective-permute-start(f32[2,65,8,128]{3,2,1,0:T(8,128)S(1)} %get-tuple-element.43), channel_id=1, source_target_pairs={{0,1},{1,0},{2,3},{3,2},{4,5},{5,4},{6,7},{7,6},{8,9},{9,8},{10,11... | collective-permute-start | bytes 1597448 | tf_op jit(solution)/shard_map/ppermute | solution.py:160
  10.3 41.1 %collective-permute-start = (f32[64,8,128]{2,1,0:T(8,128)S(1)}, f32[64,8,128]{2,1,0:T(8,128)S(1)}, u32[]{:S(2)}, u32[]{:S(2)}) collective-permute-start(f32[64,8,128]{2,1,0:T(8,128)S(1)} %get-tuple-element.42), channel_id=1, source_target_pairs={{0,2},{1,3},{2,0},{3,1},{4,6},{5,7},{6,4},{7,5},{8,10},{9,11},{10,... | collective-permute-start | bytes 786440 | tf_op jit(solution)/shard_map/ppermute | solution.py:160
  10.4 19.0 %collective-permute-start.5 = (f32[2,64,8,128]{3,2,1,0:T(8,128)S(1)}, f32[2,64,8,128]{3,2,1,0:T(8,128)S(1)}, u32[]{:S(2)}, u32[]{:S(2)}) collective-permute-start(f32[2,64,8,128]{3,2,1,0:T(8,128)S(1)} %get-tuple-element.51), channel_id=1, source_target_pairs={{0,4},{1,5},{2,6},{3,7},{4,0},{5,1},{6,2},{7,3},{8,12},{9,13},{10,... | collective-permute-start | bytes 1572872 | tf_op jit(solution)/shard_map/ppermute | solution.py:160
  11.0 2.3 %collective-permute-start.3 = (f32[3,64,8,128]{3,2,1,0:T(8,128)S(1)}, f32[3,64,8,128]{3,2,1,0:T(8,128)S(1)}, u32[]{:S(2)}, u32[]{:S(2)}) collective-permute-start(f32[3,64,8,128]{3,2,1,0:T(8,128)S(1)} %get-tuple-element.46), channel_id=1, source_target_pairs={{0,2},{1,3},{2,0},{3,1},{4,6},{5,7},{6,4},{7,5},{8,10},{9,11},{10,... | collective-permute-start | bytes 2359304 | tf_op jit(solution)/shard_map/ppermute | solution.py:160
  13.3 17.4 %collective-permute-start.2 = (f32[2,64,8,128]{3,2,1,0:T(8,128)S(1)}, f32[2,64,8,128]{3,2,1,0:T(8,128)S(1)}, u32[]{:S(2)}, u32[]{:S(2)}) collective-permute-start(f32[2,64,8,128]{3,2,1,0:T(8,128)S(1)} %get-tuple-element.44), channel_id=1, source_target_pairs={{0,9},{1,8},{2,11},{3,10},{4,13},{5,12},{6,15},{7,14},{8,1},{9,0},... | collective-permute-start | bytes 1572872 | tf_op jit(solution)/shard_map/ppermute | solution.py:160
  31.1 20.3 %copy-start = (f32[2,4,256]{2,1,0:T(4,128)S(1)}, f32[2,4,256]{2,1,0:T(4,128)}, u32[]{:S(2)}) copy-start(f32[2,4,256]{2,1,0:T(4,128)} %param.10) | copy-start | bytes 24580
  31.2 20.2 %collective-permute-start.6 = (f32[4,64,8,128]{3,2,1,0:T(8,128)S(1)}, f32[4,64,8,128]{3,2,1,0:T(8,128)S(1)}, u32[]{:S(2)}, u32[]{:S(2)}) collective-permute-start(f32[4,64,8,128]{3,2,1,0:T(8,128)S(1)} %pad_maximum_fusion), channel_id=1, source_target_pairs={{0,2},{1,3},{2,0},{3,1},{4,6},{5,7},{6,4},{7,5},{8,10},{9,11},{10,... | collective-permute-start | bytes 3145736 | tf_op jit(solution)/shard_map/ppermute | solution.py:160
  31.3 11.9 %collective-permute-start.9 = (f32[2,37,8,128]{3,2,1,0:T(8,128)S(1)}, f32[2,37,8,128]{3,2,1,0:T(8,128)S(1)}, u32[]{:S(2)}, u32[]{:S(2)}) collective-permute-start(f32[2,37,8,128]{3,2,1,0:T(8,128)S(1)} %pad_maximum_fusion.1), channel_id=1, source_target_pairs={{0,13},{1,12},{2,15},{3,14},{4,9},{5,8},{6,11},{7,10},{8,5},{9,4},... | collective-permute-start | bytes 909320 | tf_op jit(solution)/shard_map/ppermute | solution.py:160
  33.5 15.3 %collective-permute-start.7 = (f32[2,37,8,128]{3,2,1,0:T(8,128)S(1)}, f32[2,37,8,128]{3,2,1,0:T(8,128)S(1)}, u32[]{:S(2)}, u32[]{:S(2)}) collective-permute-start(f32[2,37,8,128]{3,2,1,0:T(8,128)S(1)} %pad_maximum_fusion.2), channel_id=1, source_target_pairs={{0,8},{1,9},{2,10},{3,11},{4,12},{5,13},{6,14},{7,15},{8,0},{9,1},... | collective-permute-start | bytes 909320 | tf_op jit(solution)/shard_map/ppermute | solution.py:160
  34.3 15.7 %collective-permute-start.8 = (f32[2,37,8,128]{3,2,1,0:T(8,128)S(1)}, f32[2,37,8,128]{3,2,1,0:T(8,128)S(1)}, u32[]{:S(2)}, u32[]{:S(2)}) collective-permute-start(f32[2,37,8,128]{3,2,1,0:T(8,128)S(1)} %pad_maximum_fusion.3), channel_id=1, source_target_pairs={{0,5},{1,4},{2,7},{3,6},{4,1},{5,0},{6,3},{7,2},{8,13},{9,12},{10,... | collective-permute-start | bytes 909320 | tf_op jit(solution)/shard_map/ppermute | solution.py:160
  43.2 12.5 %collective-permute-start.12 = (f32[2,27,8,128]{3,2,1,0:T(8,128)S(1)}, f32[2,27,8,128]{3,2,1,0:T(8,128)S(1)}, u32[]{:S(2)}, u32[]{:S(2)}) collective-permute-start(f32[2,27,8,128]{3,2,1,0:T(8,128)S(1)} %pad_maximum_fusion.6), channel_id=1, source_target_pairs={{0,13},{1,12},{2,15},{3,14},{4,9},{5,8},{6,11},{7,10},{8,5},{9,4},... | collective-permute-start | bytes 663560 | tf_op jit(solution)/shard_map/ppermute | solution.py:160
  48.8 12.4 %collective-permute-start.10 = (f32[2,27,8,128]{3,2,1,0:T(8,128)S(1)}, f32[2,27,8,128]{3,2,1,0:T(8,128)S(1)}, u32[]{:S(2)}, u32[]{:S(2)}) collective-permute-start(f32[2,27,8,128]{3,2,1,0:T(8,128)S(1)} %pad_maximum_fusion.4), channel_id=1, source_target_pairs={{0,8},{1,9},{2,10},{3,11},{4,12},{5,13},{6,14},{7,15},{8,0},{9,1},... | collective-permute-start | bytes 663560 | tf_op jit(solution)/shard_map/ppermute | solution.py:160
  50.0 11.2 %collective-permute-start.11 = (f32[2,27,8,128]{3,2,1,0:T(8,128)S(1)}, f32[2,27,8,128]{3,2,1,0:T(8,128)S(1)}, u32[]{:S(2)}, u32[]{:S(2)}) collective-permute-start(f32[2,27,8,128]{3,2,1,0:T(8,128)S(1)} %pad_maximum_fusion.5), channel_id=1, source_target_pairs={{0,5},{1,4},{2,7},{3,6},{4,1},{5,0},{6,3},{7,2},{8,13},{9,12},{10,... | collective-permute-start | bytes 663560 | tf_op jit(solution)/shard_map/ppermute | solution.py:160
  52.3 9.4 %collective-permute-start.14 = (f32[38,8,128]{2,1,0:T(8,128)S(1)}, f32[38,8,128]{2,1,0:T(8,128)S(1)}, u32[]{:S(2)}, u32[]{:S(2)}) collective-permute-start(f32[38,8,128]{2,1,0:T(8,128)S(1)} %get-tuple-element.67.mine_ref), channel_id=1, source_target_pairs={{0,16},{1,17},{2,18},{3,19},{4,20},{5,21},{6,22},{7,23},{8,24},{9,... | collective-permute-start | bytes 466952 | tf_op jit(solution)/shard_map/ppermute | solution.py:160
  61.3 6.2 %collective-permute-start.13 = (f32[18,8,128]{2,1,0:T(8,128)S(1)}, f32[18,8,128]{2,1,0:T(8,128)S(1)}, u32[]{:S(2)}, u32[]{:S(2)}) collective-permute-start(f32[18,8,128]{2,1,0:T(8,128)S(1)} %shard_map.81.mine_ref), channel_id=1, source_target_pairs={{0,16},{1,17},{2,18},{3,19},{4,20},{5,21},{6,22},{7,23},{8,24},{9,... | collective-permute-start | bytes 221192 | tf_op jit(solution)/shard_map/ppermute | solution.py:160
  63.1 6.5 %collective-permute-start.16 = (f32[18,8,128]{2,1,0:T(8,128)S(1)}, f32[18,8,128]{2,1,0:T(8,128)S(1)}, u32[]{:S(2)}, u32[]{:S(2)}) collective-permute-start(f32[18,8,128]{2,1,0:T(8,128)S(1)} %get-tuple-element.72.mine_ref), channel_id=1, source_target_pairs={{0,16},{1,17},{2,18},{3,19},{4,20},{5,21},{6,22},{7,23},{8,24},{9,... | collective-permute-start | bytes 221192 | tf_op jit(solution)/shard_map/ppermute | solution.py:160
  68.9 5.6 %collective-permute-start.15 = (f32[18,8,128]{2,1,0:T(8,128)S(1)}, f32[18,8,128]{2,1,0:T(8,128)S(1)}, u32[]{:S(2)}, u32[]{:S(2)}) collective-permute-start(f32[18,8,128]{2,1,0:T(8,128)S(1)} %get-tuple-element.70.mine_ref), channel_id=1, source_target_pairs={{0,16},{1,17},{2,18},{3,19},{4,20},{5,21},{6,22},{7,23},{8,24},{9,... | collective-permute-start | bytes 221192 | tf_op jit(solution)/shard_map/ppermute | solution.py:160
